TPU v7x, 128 devices: a whole 4x4x4 slice. The times are simulated.
128 devices in a mesh: group: 4 (over y_hi, core), wide: 32 (over z, y_lo, x).
Axes of the slice: x: 4, y: 4 (y_hi: 2, y_lo: 2; y = y_hi * 2 + y_lo), z: 4, core: 2. Of those that a mesh axis runs over, the one named last changes fastest.
Arguments:
- acts: bfloat16 [4, 8192, 1280], P('group', 'wide'), may hold values from -6 to 6
- block_in: bfloat16 [4, 1280, 2560], P('group'), may hold values from -0.15625 to 0.15625
- block_out: bfloat16 [4, 2560, 1280], P('group'), may hold values from -0.125 to 0.125
- adapt_in: bfloat16 [3, 1280, 640], replicated, may hold values from -0.15625 to 0.15625
- adapt_out: bfloat16 [3, 640, 1280], replicated, may hold values from -0.25 to 0.25
- owner: int32 [4, 8], replicated, may hold values from 0 to 7, each once within a row
Outputs:
- grad_adapt_in: float32 [4, 1280, 640], P('group', 'wide')
- grad_adapt_out: float32 [4, 640, 1280], P('group', 'wide')
- grad_block_in: float32 [4, 1280, 2560], P('group', 'wide')
- grad_block_out: float32 [4, 2560, 1280], P('group', 'wide')
Inputs may be any that keep to these rules, and one draw needn't show every extreme that they name: `owner`: each row is a permutation of the image numbers.
All inputs are finite; a program needn't handle non-finite values.
Results may differ from a plain program's by a relative error of at most 0.011.
Values may be sent and summed in bfloat16 or wider, within the bound.
No kernel may reach another device: no remote copies, remote signals or barrier semaphores. Data moves between devices by JAX's collectives and lax.ppermute only.
A program may use at most 128 MiB of HBM per device.

v0:
```python
import jax
import jax.numpy as jnp
from jax import lax
from jax.sharding import PartitionSpec as P

PATCHES = 1024


EPS = 1e-06


def broadcast(value, axis, source):
    kept = jnp.where(lax.axis_index(axis) == source, value, 0).astype(value.dtype)
    return lax.psum(kept, axis)


def block_forward(inputs, w_first, w_second):
    values = inputs.astype(jnp.float32)
    center = values - jnp.mean(values, axis=-1, keepdims=True)
    spread = jnp.mean(center * center, axis=-1, keepdims=True)
    normed = (center * lax.rsqrt(spread + EPS)).astype(jnp.bfloat16)
    before = jnp.dot(normed, w_first, preferred_element_type=jnp.float32)
    hidden = jax.nn.gelu(before, approximate=True).astype(jnp.bfloat16)
    output = (values + jnp.dot(hidden, w_second, preferred_element_type=jnp.float32)).astype(
        jnp.bfloat16
    )
    return (normed, before, hidden, output)


def token_loss(predicted, target):
    width = predicted.shape[-1]
    inner = jnp.mean(predicted * target, axis=-1)
    first = jnp.mean(predicted * predicted, axis=-1) + EPS
    second = jnp.mean(target * target, axis=-1) + EPS
    cosine = inner * lax.rsqrt(first * second)
    differ = predicted - target
    return jnp.sum(width * (1.0 - cosine) + jnp.sum(differ * differ, axis=-1))


def contract_rows(left, right):
    return lax.dot_general(
        left, right, (((0,), (0,)), ((), ())), preferred_element_type=jnp.float32
    )


def contract_cols(left, right):
    return lax.dot_general(
        left, right, (((1,), (1,)), ((), ())), preferred_element_type=jnp.float32
    )


def gelu_grad(point, upstream):
    pull = jax.vjp(lambda z: jax.nn.gelu(z, approximate=True), point)[1]
    return pull(upstream)[0]


def small_lookup(table, indices):
    ranks = jnp.arange(table.shape[0], dtype=jnp.int32)
    return jnp.sum(jnp.where(indices[:, None] == ranks[None, :], table[None, :], 0), axis=1)


def body(acts, block_in, block_out, adapt_in, adapt_out, owner):
    group_index = lax.axis_index("group")
    wide_count = lax.axis_size("wide")
    token_count = acts.shape[1]
    width = acts.shape[2]
    piece = token_count // wide_count
    per_image = PATCHES // token_count
    loss_scale = 1.0 / (token_count * wide_count) ** 0.5
    teacher_mask = (group_index < 3).astype(jnp.float32)
    student_mask = (group_index == 3).astype(jnp.float32)
    normed, before, hidden, output = block_forward(acts[0], block_in[0], block_out[0])
    student_all = broadcast(output, "group", 3)
    image_count = owner.shape[1]
    image_ranks = jnp.arange(image_count, dtype=jnp.int32)
    positions = jnp.arange(wide_count, dtype=jnp.int32)
    student_order = owner[3]
    own_order = lax.dynamic_index_in_dim(owner, group_index, 0, keepdims=False)
    student_slot = jnp.sum(
        jnp.where(student_order[None, :] == image_ranks[:, None], image_ranks[None, :], 0), axis=1
    )
    slot_image = small_lookup(own_order, positions // per_image)
    block_index = per_image * small_lookup(student_slot, slot_image) + positions % per_image
    block_source = jnp.sum(
        jnp.where(block_index[None, :] == positions[:, None], positions[None, :], 0), axis=1
    )
    send_blocks = jnp.take(student_all.reshape(wide_count, piece, width), block_index, axis=0)
    student = lax.all_to_all(
        send_blocks.reshape(token_count, width), "wide", split_axis=0, concat_axis=0, tiled=True
    )
    chosen = jnp.minimum(group_index, 2)
    a_first = lax.dynamic_index_in_dim(adapt_in, chosen, 0, keepdims=False)
    a_second = lax.dynamic_index_in_dim(adapt_out, chosen, 0, keepdims=False)
    target = output.astype(jnp.float32)
    zeta = jnp.dot(student, a_first, preferred_element_type=jnp.float32)
    gamma = jax.nn.gelu(zeta, approximate=True).astype(jnp.bfloat16)
    predicted = jnp.dot(gamma, a_second, preferred_element_type=jnp.float32)
    pull = jax.vjp(lambda p: token_loss(p, target), predicted)[1]
    grad_pred = pull(jnp.asarray(loss_scale, jnp.float32))[0] * teacher_mask
    grad_pred_b = grad_pred.astype(jnp.bfloat16)
    grad_gamma = contract_cols(grad_pred_b, a_second)
    grad_zeta = gelu_grad(zeta, grad_gamma).astype(jnp.bfloat16)
    grad_student = contract_cols(grad_zeta, a_first)
    returned = lax.all_to_all(grad_student, "wide", split_axis=0, concat_axis=0, tiled=True)
    arranged = jnp.take(returned.reshape(wide_count, piece, width), block_source, axis=0).reshape(
        token_count, width
    )
    grad_total = lax.psum(arranged, "group")
    grad_out = (grad_total * student_mask).astype(jnp.bfloat16)
    grad_hidden = contract_cols(grad_out, block_out[0])
    grad_before = gelu_grad(before, grad_hidden).astype(jnp.bfloat16)
    term_adapt_in = contract_rows(student, grad_zeta)
    term_adapt_out = contract_rows(gamma, grad_pred_b)
    term_block_in = contract_rows(normed, grad_before)
    term_block_out = contract_rows(hidden, grad_out)
    shards = (
        lax.psum_scatter(term_adapt_in, "wide", scatter_dimension=0, tiled=True),
        lax.psum_scatter(term_adapt_out, "wide", scatter_dimension=0, tiled=True),
        lax.psum_scatter(term_block_in, "wide", scatter_dimension=0, tiled=True),
        lax.psum_scatter(term_block_out, "wide", scatter_dimension=0, tiled=True),
    )
    return (shards[0][None], shards[1][None], shards[2][None], shards[3][None])


def solution(mesh):
    placed = (
        P("group", "wide", None),
        P("group", None, None),
        P("group", None, None),
        P(),
        P(),
        P(),
    )
    return jax.shard_map(
        body,
        mesh=mesh,
        in_specs=placed,
        out_specs=(
            P("group", "wide", None),
            P("group", "wide", None),
            P("group", "wide", None),
            P("group", "wide", None),
        ),
        check_vma=False,
    )
```

profile of v0, /device:TPU:0, one launch (start us, length us, event | category | flops | bytes accessed | tf_op | source)
XLA Modules:
  0.0 739.4 jit_solution(12684598158224637140)
XLA Ops:
  8.5 1.4 fusion.42
  9.9 5.1 fusion.5
  15.0 5.2 fusion.19
  22.3 45.0 %all-reduce.6.cloned.1.call-done = bf16[32,8,1280]{2,1,0:T(8,128)(2,1)} async-done(((bf16[32,8,1280]{2,1,0:T(8,128)(2,1)}), bf16[32,8,1280]{2,1,0:T(8,128)(2,1)}) %all-reduce.6.cloned.1.call-update) | async-done | bytes 655376 | tf_op jit(solution)/shard_map/psum | solution.py:14
  67.4 2.5 gather_fusion
  69.9 2.1 broadcast_select_fusion
  72.0 7.4 all-to-all-start
  79.4 13.3 %all-to-all-done = bf16[32,8,1280]{2,1,0:T(8,128)(2,1)} async-done(((bf16[32,8,1280]{2,1,0:T(8,128)(2,1)}), bf16[32,8,1280]{2,1,0:T(8,128)(2,1)}, u32[]{:S(2)}, u32[]{:S(2)}) %all-to-all-start) | async-done | bytes 655392 | tf_op jit(solution)/shard_map/all_to_all | solution.py:88
  92.6 2.4 fusion.33
  95.0 2.6 fusion.51
  97.7 3.0 fusion.65
  101.5 3.2 fusion.27
  104.7 4.7 all-to-all-start.1
  109.8 18.1 %all-to-all-done.1 = f32[32,8,1280]{2,1,0:T(8,128)} async-done(((f32[32,8,1280]{2,1,0:T(8,128)}), f32[32,8,1280]{2,1,0:T(8,128)}, u32[]{:S(2)}, u32[]{:S(2)}) %all-to-all-start.1) | async-done | bytes 1310752 | tf_op jit(solution)/shard_map/all_to_all | solution.py:104
  127.8 3.0 gather_fusion.1
  130.9 2.5 bitcast_select_fusion
  133.5 3.6 fusion.69
  137.3 41.9 %all-reduce.8.cloned.1.call-done = f32[256,1280]{1,0:T(8,128)} async-done(((f32[256,1280]{1,0:T(8,128)}), f32[256,1280]{1,0:T(8,128)}) %all-reduce.8.cloned.1.call-update) | async-done | bytes 1310736 | tf_op jit(solution)/shard_map/psum | solution.py:108
  179.2 12.2 %fusion.23 = f32[1280,2560]{1,0:T(8,128)} fusion(f32[256,2560]{1,0:T(8,128)S(1)} %fusion.5, bf16[1,2560,1280]{2,1,0:T(8,128)(2,1)} %param.8, bf16[1,256,1280]{2,1,0:T(8,128)(2,1)S(1)} %copy-done, f32[256]{0:T(256)S(1)} %add_rsqrt_fusion, f32[256]{0:T(256)S(1)} %broadcast_multiply_fusion, f32[256,1280]{1,0:T(8,128)} %all-reduce.8.cloned.1.call-done, ...), kind=kOutput, calls=%fused_computation.20 | convolution fusion | flops 3370516480 | bytes 24250372 | tf_op jit(solution)/shard_map/dot_general | solution.py:41
  191.5 8.6 %fusion.79 = f32[2560,1280]{1,0:T(8,128)} fusion(f32[256,1280]{1,0:T(8,128)} %all-reduce.8.cloned.1.call-done, f32[]{:T(128)S(6)} %convert_element_type.59, f32[256,2560]{1,0:T(8,128)S(1)} %fusion.5), kind=kOutput, calls=%fused_computation.86 | convolution fusion | flops 1684275200 | bytes 17039364 | tf_op jit(solution)/shard_map/dot_general | solution.py:41
  200.1 2.6 fusion.99
  202.8 104.7 %fusion = f32[24,1280]{1,0:T(8,128)S(1)} fusion(f32[640,1280]{1,0:T(8,128)S(1)} %fusion.99), kind=kCustom, calls=%all-reduce-scatter | all-reduce-scatter fusion | flops 983041 | bytes 3400192
  307.5 1.3 collective-permute-start.5
  308.8 1.3 collective-permute-start.4
  310.1 1.3 collective-permute-start.3
  311.5 1.3 collective-permute-start.2
  312.8 2.6 collective-permute-start.1
  315.4 1.9 collective-permute-start
  318.5 1.7 collective-permute-done
  322.0 28.4 %reduce-scatter.13.cloned.1.call-done = f32[40,640]{1,0:T(8,128)} async-done(((f32[1280,640]{1,0:T(8,128)}), f32[40,640]{1,0:T(8,128)}) %reduce-scatter.13.cloned.1.call-update) | async-done | bytes 102416
  350.4 191.2 %reduce-scatter.9.cloned.1.call-done = f32[40,2560]{1,0:T(8,128)} async-done(((f32[1280,2560]{1,0:T(8,128)}), f32[40,2560]{1,0:T(8,128)}) %reduce-scatter.9.cloned.1.call-update) | async-done | bytes 409616 | tf_op jit(solution)/shard_map/reduce_scatter | solution.py:119
  541.6 191.3 %reduce-scatter.11.cloned.1.call-done = f32[80,1280]{1,0:T(8,128)} async-done(((f32[2560,1280]{1,0:T(8,128)}), f32[80,1280]{1,0:T(8,128)}) %reduce-scatter.11.cloned.1.call-update) | async-done | bytes 409616 | tf_op jit(solution)/shard_map/reduce_scatter | solution.py:120
  (55 shorter events, 7.3 us)
Async XLA Ops:
  7.2 60.2 %all-reduce.6.cloned.1.call-start = ((), (), s32[]{:S(2)}) async-start(), calls=%async_computation.5 | async-start | bytes 1310720 | tf_op jit(solution)/shard_map/psum | solution.py:14
  9.9 5.1 copy-start
  15.0 7.0 copy-start.7
  20.2 0.9 copy-start.2
  72.0 20.6 %all-to-all-start = ((bf16[32,8,1280]{2,1,0:T(8,128)(2,1)}), bf16[32,8,1280]{2,1,0:T(8,128)(2,1)}, u32[]{:S(2)}, u32[]{:S(2)}) async-start(bf16[32,8,1280]{2,1,0:T(8,128)(2,1)} %broadcast_select_fusion), calls=%async_computation | async-start | bytes 1310720 | tf_op jit(solution)/shard_map/all_to_all | solution.py:88
  92.6 2.4 copy-start.3
  95.0 2.7 copy-start.1
  97.7 3.1 copy-start.4
  100.7 0.7 copy-start.5
  104.7 23.1 %all-to-all-start.1 = ((f32[32,8,1280]{2,1,0:T(8,128)}), f32[32,8,1280]{2,1,0:T(8,128)}, u32[]{:S(2)}, u32[]{:S(2)}) async-start(f32[32,8,1280]{2,1,0:T(8,128)} %fusion.27), calls=%async_computation.1 | async-start | bytes 2621440 | tf_op jit(solution)/shard_map/all_to_all | solution.py:104
  109.4 69.8 %all-reduce.8.cloned.1.call-start = ((), (), s32[]{:S(2)}) async-start(), calls=%async_computation.6 | async-start | bytes 2621440 | tf_op jit(solution)/shard_map/psum | solution.py:108
  133.4 217.0 %reduce-scatter.13.cloned.1.call-start = ((), (), s32[]{:S(2)}) async-start(), calls=%async_computation.9 | async-start | bytes 3379200
  137.1 404.5 %reduce-scatter.9.cloned.1.call-start = ((), (), s32[]{:S(2)}) async-start(), calls=%async_computation.7 | async-start | bytes 13516800 | tf_op jit(solution)/shard_map/reduce_scatter | solution.py:119
  191.4 541.4 %reduce-scatter.11.cloned.1.call-start = ((), (), s32[]{:S(2)}) async-start(), calls=%async_computation.8 | async-start | bytes 13516800 | tf_op jit(solution)/shard_map/reduce_scatter | solution.py:120
  202.8 114.5 %copy-start.6 = (u32[128]{0:T(128)S(1)}, u32[128]{0:T(128)}, u32[]{:S(2)}) copy-start(u32[128]{0:T(128)} %constant.135) | copy-start | bytes 1540
  307.5 7.8 %collective-permute-start.5 = (f32[4,1280]{1,0:T(4,128)S(1)}, f32[4,1280]{1,0:T(4,128)S(1)}, u32[]{:S(2)}, u32[]{:S(2)}) collective-permute-start(f32[4,1280]{1,0:T(4,128)S(1)} %slice.8), channel_id=1, source_target_pairs={{0,6},{1,7},{2,8},{3,9},{4,10},{5,11},{6,12},{7,13},{8,14},{9,15},... | collective-permute-start | bytes 61448
  308.8 9.6 %collective-permute-start.4 = (f32[24,1280]{1,0:T(8,128)S(1)}, f32[24,1280]{1,0:T(8,128)S(1)}, u32[]{:S(2)}, u32[]{:S(2)}) collective-permute-start(f32[24,1280]{1,0:T(8,128)S(1)} %fusion), channel_id=1, source_target_pairs={{0,5},{1,6},{2,7},{3,8},{4,9},{5,10},{6,11},{7,12},{8,13},{9,14},{... | collective-permute-start | bytes 368648
  310.1 8.3 %collective-permute-start.3 = (f32[24,1280]{1,0:T(8,128)S(1)}, f32[24,1280]{1,0:T(8,128)S(1)}, u32[]{:S(2)}, u32[]{:S(2)}) collective-permute-start(f32[24,1280]{1,0:T(8,128)S(1)} %fusion), channel_id=1, source_target_pairs={{0,4},{1,5},{2,6},{3,7},{4,8},{5,9},{6,10},{7,11},{8,12},{9,13},{1... | collective-permute-start | bytes 368648
  311.5 7.0 collective-permute-start.2
  312.8 5.8 collective-permute-start.1
  315.4 4.8 collective-permute-start
Sparse Core Ops, SparseCore 0:
  22.1 45.2 all-reduce.5
  133.5 45.5 all-reduce.7
  182.1 168.1 reduce-scatter.12
  353.3 188.2 reduce-scatter.8
  544.4 188.3 reduce-scatter.10
where the time goes:
time: 740 us; the launch traced here: 739 us
  waiting for transfers between devices  531 us (72%)
  blocking collectives  105 us (14%)
  matrix products  48.6 us (7%)
  starting transfers between devices  22.1 us (3%)
  between operations  14.8 us (2%)
  local copies, waits for them, and re-layouts  9.7 us (1%)
  other arithmetic  8.63 us (1%)
    reduce_scatter x1, waiting for transfers between devices, body(): lax.psum_scatter(term_block_out, 'wide', scatter_dimension=0, tiled=True)  191 us
    reduce_scatter x1, waiting for transfers between devices, body(): lax.psum_scatter(term_block_in, 'wide', scatter_dimension=0, tiled=True)  191 us
    unnamed x1, blocking collectives  105 us
    psum x1, waiting for transfers between devices, broadcast(): return lax.psum(kept, axis)  45 us
    psum x1, waiting for transfers between devices, body(): grad_total = lax.psum(arranged, 'group')  41.9 us
    unnamed x12, waiting for transfers between devices  30.2 us
    dot_general x4, matrix products, contract_rows(): lax.dot_general(left, right, (((0,), (0,)), ((), ())), preferred_element_...  27.1 us
    all_to_all x1, waiting for transfers between devices, body(): lax.all_to_all(grad_student, 'wide', split_axis=0, concat_axis=0, tiled=T...  18.1 us
  transfers between devices with their start and end apart: 13, of which 8 were waited for; matrix products, arithmetic and copies ran while one was open for 18% of the time, Pallas kernels for 0%

commit v1 on v0

v1 whole, which is shorter than its diff:
```python
import functools

import jax
import jax.numpy as jnp
from jax import lax
from jax.experimental import pallas as pl
from jax.experimental.pallas import tpu as pltpu
from jax.sharding import Mesh
from jax.sharding import PartitionSpec as P

PATCHES = 1024


EPS = 1e-06
WIDE = ("z", "yl", "x")
GROUP = ("yh", "core")
ALL = GROUP + WIDE
SIZES = (2, 2, 4, 2, 4)
MIB = 1024 * 1024
BF16 = jnp.bfloat16


def cost(flops, moved):
    return pl.CostEstimate(flops=flops, bytes_accessed=moved, transcendentals=0)


F32 = jnp.float32
CORE, FLIP, GROUP_AT, CHOSEN, YL, KEEP, FIRST, SECOND = range(8)


def route(move):
    pairs = []
    for flat in range(128):
        x, yl, z, core, yh = flat % 4, flat // 4 % 2, flat // 8 % 4, flat // 32 % 2, flat // 64
        to = move(yh, core, z, yl, x)
        if to is not None:
            yh, core, z, yl, x = to
            pairs.append((flat, (((yh * 2 + core) * 4 + z % 4) * 2 + yl) * 4 + x % 4))
    return pairs


def send(value, move):
    return lax.ppermute(value, ALL, route(move))


def vmem(count):
    return [pl.BlockSpec(memory_space=pltpu.VMEM)] * count


def smem():
    return pl.BlockSpec(memory_space=pltpu.SMEM)


def in_hbm(*weights):
    return [pltpu.with_memory_space_constraint(w, pltpu.HBM) for w in weights]


def shaped(shape, dtype):
    return jax.ShapeDtypeStruct(shape, dtype)


def call(kernel, scalars, inputs, outputs, scratch=(), grant=16, flops=0):
    moved = sum(a.size * a.dtype.itemsize for a in (*inputs, *outputs))
    return pl.pallas_call(
        kernel,
        out_shape=list(outputs),
        in_specs=[smem()] + vmem(len(inputs)),
        out_specs=vmem(len(outputs)),
        scratch_shapes=list(scratch),
        compiler_params=pltpu.CompilerParams(vmem_limit_bytes=grant * MIB),
        cost_estimate=cost(flops, moved),
    )(scalars, *inputs)


def contract_rows(left, right):
    return lax.dot_general(
        left, right, (((0,), (0,)), ((), ())), preferred_element_type=F32
    )


def contract_cols(left, right):
    return lax.dot_general(
        left, right, (((1,), (1,)), ((), ())), preferred_element_type=F32
    )


def gelu_parts(point):
    root = 0.7978845608028654
    square = point * point
    bent = jnp.tanh(root * (point + 0.044715 * point * square))
    share = 0.5 * (1.0 + bent)
    slope = share + 0.5 * point * (1.0 - bent * bent) * (root * (1.0 + 0.134145 * square))
    return point * share, slope


CHUNK = 512


def forward_kernel(
    at, acts_hbm, first_hbm, second_hbm, hidden_hbm, hand_hbm, slope_hbm, out_ref, sent_ref,
    acts_ref, first_ref, second_ref, total, hidden_ref, normed_ref, slope_ref,
    first_sem, second_sem, hidden_sem, slope_sem, other_sem,
):
    tokens, hidden_width = slope_ref.shape
    width = out_ref.shape[1]
    count = hidden_width // CHUNK

    def first_copy(j):
        cut = pl.ds(j * CHUNK, CHUNK)
        return pltpu.make_async_copy(
            first_hbm.at[0, :, cut], first_ref.at[j], first_sem.at[j]
        )

    def second_copy(j):
        cut = pl.ds(j * CHUNK, CHUNK)
        return pltpu.make_async_copy(
            second_hbm.at[0, cut, :], second_ref.at[j], second_sem.at[j]
        )

    def hidden_copy(j):
        cut = pl.ds(j * CHUNK, CHUNK)
        return pltpu.make_async_copy(
            hidden_ref.at[:, cut], hidden_hbm.at[:, cut], hidden_sem.at[j]
        )

    def slope_copy(part):
        cut = pl.ds(part * (hidden_width // 2), hidden_width // 2)
        target = slope_hbm if part else hand_hbm.at[pl.ds(width + tokens, tokens)]
        return pltpu.make_async_copy(slope_ref.at[:, cut], target, slope_sem.at[part])

    def weight_copy(j):
        rows = min(CHUNK, width - j * CHUNK)
        return pltpu.make_async_copy(
            second_ref.at[j, pl.ds(0, rows)],
            hand_hbm.at[pl.ds(j * CHUNK, rows)],
            other_sem.at[2 + j],
        )

    acts_copy = pltpu.make_async_copy(acts_hbm.at[0], acts_ref, other_sem.at[0])
    normed_copy = pltpu.make_async_copy(
        normed_ref, hand_hbm.at[pl.ds(width, tokens)], other_sem.at[1]
    )
    acts_copy.start()
    first_copy(0).start()
    second_copy(0).start()
    first_copy(1).start()
    acts_copy.wait()
    values = acts_ref[...].astype(F32)
    center = values - jnp.mean(values, axis=-1, keepdims=True)
    spread = jnp.mean(center * center, axis=-1, keepdims=True)
    normed = (center * lax.rsqrt(spread + EPS)).astype(BF16)
    normed_ref[...] = normed
    normed_copy.start()
    total[...] = values
    first_copy(0).wait()
    before = jnp.dot(normed, first_ref[0], preferred_element_type=F32)
    for j in range(count):
        if j + 1 < count:
            second_copy(j + 1).start()
        if j + 2 < count:
            first_copy(j + 2).start()
        second_copy(j).wait()
        if j * CHUNK < width:
            weight_copy(j).start()
        if j + 1 < count:
            first_copy(j + 1).wait()
            later = jnp.dot(normed, first_ref[j + 1], preferred_element_type=F32)
        else:
            later = None
        hidden, slope = gelu_parts(before)
        hidden = hidden.astype(BF16)
        slope_ref[:, j * CHUNK : (j + 1) * CHUNK] = slope.astype(BF16)
        hidden_ref[:, j * CHUNK : (j + 1) * CHUNK] = hidden
        hidden_copy(j).start()
        if j == count // 2:
            slope_copy(0).start()
        total[...] += jnp.dot(hidden, second_ref[j], preferred_element_type=F32)
        before = later
    slope_copy(1).start()
    out_ref[...] = total[...].astype(BF16)
    for block in range(8):
        source = jnp.where(at[FLIP] == 1, block ^ 1, block) * 32
        sent_ref[block * 32 : block * 32 + 32] = total[
            pl.ds(pl.multiple_of(source, 32), 32)
        ].astype(BF16)
    for j in range(count):
        hidden_copy(j).wait()
        if j * CHUNK < width:
            weight_copy(j).wait()
    for part in range(2):
        slope_copy(part).wait()
    normed_copy.wait()


def block_forward(scalars, acts, block_in, block_out):
    _, tokens, width = acts.shape
    hidden = block_in.shape[2]
    count = hidden // CHUNK
    return pl.pallas_call(
        forward_kernel,
        out_shape=[
            pltpu.HBM((tokens, hidden), BF16),
            pltpu.HBM((hidden // 2 + 2 * tokens, width), BF16),
            pltpu.HBM((tokens, hidden // 2), BF16),
            shaped((tokens, width), BF16),
            shaped((tokens, width), BF16),
        ],
        in_specs=[smem()] + [pl.BlockSpec(memory_space=pltpu.HBM)] * 3,
        out_specs=[pl.BlockSpec(memory_space=pltpu.HBM)] * 3 + vmem(2),
        scratch_shapes=[
            pltpu.VMEM((tokens, width), BF16),
            pltpu.VMEM((count, width, CHUNK), BF16),
            pltpu.VMEM((count, CHUNK, width), BF16),
            pltpu.VMEM((tokens, width), F32),
            pltpu.VMEM((tokens, hidden), BF16),
            pltpu.VMEM((tokens, width), BF16),
            pltpu.VMEM((tokens, hidden), BF16),
            pltpu.SemaphoreType.DMA((count,)),
            pltpu.SemaphoreType.DMA((count,)),
            pltpu.SemaphoreType.DMA((count,)),
            pltpu.SemaphoreType.DMA((count,)),
            pltpu.SemaphoreType.DMA((2 + count,)),
        ],
        compiler_params=pltpu.CompilerParams(vmem_limit_bytes=32 * MIB),
        cost_estimate=cost(4 * tokens * width * hidden, 16777216),
    )(scalars, *in_hbm(acts, block_in, block_out))


def weight_copies(at, first_hbm, second_hbm, first_ref, second_ref, sems):
    first = pltpu.make_async_copy(first_hbm.at[at[CHOSEN]], first_ref, sems.at[0])
    second = pltpu.make_async_copy(second_hbm.at[at[CHOSEN]], second_ref, sems.at[1])
    return first, second


def pick_kernel(at, own_ref, crossed_ref, shared_ref):
    @pl.when(at[FLIP] == 0)
    def _():
        shared_ref[...] = own_ref[...]

    @pl.when(at[FLIP] == 1)
    def _():
        shared_ref[...] = crossed_ref[...]


def adapt_forward_kernel(
    at, shared_ref, handed_ref, first_hbm, second_hbm,
    student_ref, gamma_ref, mixed_ref, first_ref, second_ref, sems,
):
    first, second = weight_copies(at, first_hbm, second_hbm, first_ref, second_ref, sems)
    first.start()
    second.start()
    for core, source in enumerate((handed_ref, shared_ref)):

        @pl.when(at[CORE] == core)
        def _(source=source):
            student_ref[...] = source[...]

    first.wait()
    zeta = jnp.dot(student_ref[...], first_ref[...], preferred_element_type=F32)
    gamma, slope = gelu_parts(zeta)
    gamma = gamma.astype(BF16)
    gamma_ref[...] = gamma
    mixed_ref[:, 1280:] = slope
    second.wait()
    mixed_ref[:, :1280] = jnp.dot(gamma, second_ref[...], preferred_element_type=F32)


def adapt_call(kernel, scalars, inputs, adapt_in, adapt_out, outputs):
    return pl.pallas_call(
        kernel,
        out_shape=list(outputs),
        in_specs=[smem()] + vmem(len(inputs)) + [pl.BlockSpec(memory_space=pl.ANY)] * 2,
        out_specs=vmem(len(outputs)),
        scratch_shapes=[
            pltpu.VMEM(adapt_in.shape[1:], BF16),
            pltpu.VMEM(adapt_out.shape[1:], BF16),
            pltpu.SemaphoreType.DMA((2,)),
        ],
        compiler_params=pltpu.CompilerParams(vmem_limit_bytes=24 * MIB),
        cost_estimate=cost(1024, 1024),
    )(scalars, *inputs, *in_hbm(adapt_in, adapt_out))


def adapt_backward_kernel(
    scale, at, sorter_ref, arrived_ref, mixed_ref, first_hbm, second_hbm,
    grad_pred_ref, grad_zeta_ref, kept_ref, given_ref, first_ref, second_ref, sems,
):
    first_copy, second_copy = weight_copies(
        at, first_hbm, second_hbm, first_ref, second_ref, sems
    )
    second_copy.start()
    first_copy.start()
    target = jnp.dot(sorter_ref[...], arrived_ref[...], preferred_element_type=F32)
    pred = mixed_ref[:, :1280]
    inner = jnp.mean(pred * target, axis=-1, keepdims=True)
    first = jnp.mean(pred * pred, axis=-1, keepdims=True) + EPS
    second = jnp.mean(target * target, axis=-1, keepdims=True) + EPS
    turn = lax.rsqrt(first * second)
    grad_pred = scale * (2.0 * (pred - target) - turn * (target - (inner / first) * pred))
    grad_pred = grad_pred.astype(BF16)
    grad_pred_ref[...] = grad_pred
    second_copy.wait()
    grad_gamma = contract_cols(grad_pred, second_ref[...])
    grad_zeta = (grad_gamma * mixed_ref[:, 1280:]).astype(BF16)
    grad_zeta_ref[...] = grad_zeta
    first_copy.wait()
    grad = contract_cols(grad_zeta, first_ref[...])
    grad = jnp.where(at[GROUP_AT] < 3, grad, 0.0)

    @pl.when(at[CORE] == 0)
    def _():
        kept_ref[...] = grad[:128]
        given_ref[...] = grad[128:].astype(BF16)

    @pl.when(at[CORE] == 1)
    def _():
        kept_ref[...] = grad[128:]
        given_ref[...] = grad[:128].astype(BF16)


def pair_kernel(at, kept_ref, came_ref, pair_ref, sent_ref):
    pair = kept_ref[...] + came_ref[...].astype(F32)
    pair_ref[...] = pair
    sent_ref[...] = pair.astype(BF16)


def half_kernel(at, pair_ref, across_ref, out_ref):
    out_ref[...] = (pair_ref[...] + across_ref[...].astype(F32)).astype(BF16)


def join_halves(at, mine_ref, other_ref, joined):
    @pl.when(at[CORE] == 0)
    def _():
        joined[:128] = mine_ref[...]
        joined[128:] = other_ref[...]

    @pl.when(at[CORE] == 1)
    def _():
        joined[:128] = other_ref[...]
        joined[128:] = mine_ref[...]


def hand_out(at, terms, turn, keep_ref, give_ref, columns=slice(None)):
    for place in range(8):
        for ref, lines in ((keep_ref, (0, turn ^ 2)), (give_ref, (turn, 2))):
            for slot, mask in enumerate(lines):
                line = at[FIRST] ^ mask
                wide = jnp.where(
                    at[CORE] == 0, place * 4 + line, line * 8 + place % 2 * 4 + place // 2
                )
                ref[slot, place] = terms[wide, :, columns].astype(BF16)


def stage_kernel(
    at, crossed_hbm, crossed_core_hbm, hand_hbm, hand_core_hbm, slope_hbm, second_hbm,
    left, slope, weight, sems,
):
    tokens, width = slope.shape
    weight_part = pl.ds(0, width)
    normed_part, slope_part = pl.ds(width, tokens), pl.ds(width + tokens, tokens)

    def student_copies(normed, slopes, weights):
        copies = (
            pltpu.make_async_copy(normed, left.at[:, pl.ds(0, width)], sems.at[0]),
            pltpu.make_async_copy(slopes, slope, sems.at[1]),
            pltpu.make_async_copy(weights, weight, sems.at[2]),
        )
        for copy in copies:
            copy.start()
        for copy in copies:
            copy.wait()

    for core, source in enumerate((crossed_core_hbm, crossed_hbm)):

        @pl.when((at[FLIP] == 1) & (at[CORE] == core))
        def _(source=source):
            copy = pltpu.make_async_copy(source, left, sems.at[0])
            copy.start()
            copy.wait()

    @pl.when((at[FLIP] == 0) & (at[CORE] == 0))
    def _():
        student_copies(
            hand_core_hbm.at[normed_part],
            hand_core_hbm.at[slope_part],
            hand_core_hbm.at[weight_part],
        )

    @pl.when((at[FLIP] == 0) & (at[CORE] == 1))
    def _():
        student_copies(
            hand_hbm.at[normed_part], slope_hbm, second_hbm.at[0, pl.ds(width, width), :]
        )


def stage(scalars, sources):
    tokens, width = sources[4].shape
    return pl.pallas_call(
        stage_kernel,
        out_shape=[
            shaped((tokens, 2 * width), BF16),
            shaped((tokens, width), BF16),
            shaped((width, width), BF16),
        ],
        in_specs=[smem()] + [pl.BlockSpec(memory_space=pltpu.HBM)] * 6,
        out_specs=vmem(3),
        scratch_shapes=[pltpu.SemaphoreType.DMA((3,))],
        compiler_params=pltpu.CompilerParams(vmem_limit_bytes=16 * MIB),
        cost_estimate=cost(0, 8388608),
    )(scalars, *in_hbm(*sources))


def student_kernel(
    at, left, slope, weight, mine_ref, other_ref, keep_a, give_a, keep_b, give_b, joined, before, terms
):
    join_halves(at, mine_ref, other_ref, joined)

    @pl.when(at[FLIP] == 1)
    def _():
        right = jnp.where(at[CORE] == 0, joined[:, :640], joined[:, 640:])
        for start in range(0, 2560, 640):
            block = contract_rows(left[:, start : start + 640], right)
            for index in range(8):
                row = index * 80
                terms[start // 80 + index, :, :640] = block[row : row + 40].astype(BF16)
                terms[start // 80 + index, :, 640:] = block[row + 40 : row + 80].astype(BF16)

    @pl.when(at[FLIP] == 0)
    def _():
        for start in range(0, 1280, 640):
            cut = slice(start, start + 640)
            grad_hidden = contract_cols(joined[...], weight[cut])
            before[:, cut] = (grad_hidden * slope[:, cut].astype(F32)).astype(BF16)
        for start in range(0, 1280, 640):
            block = contract_rows(left[:, start : start + 640], before[...]).astype(BF16)
            for index in range(16):
                terms[start // 40 + index] = block[index * 40 : index * 40 + 40]

    hand_out(at, terms, 1, keep_a, give_a, slice(0, 640))
    hand_out(at, terms, 3, keep_b, give_b, slice(640, 1280))


def student_partial(scalars, staged, mine, other):
    half, width = mine.shape
    tokens = 2 * half
    return call(
        student_kernel,
        scalars,
        (*staged, mine, other),
        [shaped((2, 8, 40, 640), BF16)] * 4,
        [
            pltpu.VMEM((tokens, width), BF16),
            pltpu.VMEM((tokens, width), BF16),
            pltpu.VMEM((32, 40, 1280), BF16),
        ],
        24,
        4 * tokens * width * width,
    )


def adapt_partial_kernel(
    at, student_ref, grad_zeta_ref, gamma_ref, grad_pred_ref, keep_a, give_a, keep_b, give_b, terms
):
    first = contract_rows(student_ref[...], grad_zeta_ref[...])
    second = contract_rows(gamma_ref[...], grad_pred_ref[...])
    for wide in range(32):
        terms[wide, :, :640] = first[wide * 40 : wide * 40 + 40]
        terms[wide, :20, 640:] = second[wide * 20 : wide * 20 + 20, :640]
        terms[wide, 20:, 640:] = second[wide * 20 : wide * 20 + 20, 640:]
    hand_out(at, terms, 1, keep_a, give_a, slice(0, 640))
    hand_out(at, terms, 3, keep_b, give_b, slice(640, 1280))


def next_kernel(at, keep_ref, came_ref, give_ref):
    give_ref[...] = (keep_ref[1].astype(F32) + came_ref[1].astype(F32)).astype(BF16)


def next_two_kernel(at, keep_a, came_a, keep_b, came_b, give_a, give_b):
    give_a[...] = (keep_a[1].astype(F32) + came_a[1].astype(F32)).astype(BF16)
    give_b[...] = (keep_b[1].astype(F32) + came_b[1].astype(F32)).astype(BF16)


def axis_two_kernel(
    turn, at, keep_a, came_a, last_a, keep_b, came_b, last_b, next_keep_ref, next_give_ref, total
):
    total[:, :, :640] = (
        keep_a[0].astype(F32) + came_a[0].astype(F32) + last_a[...].astype(F32)
    )
    total[:, :, 640:] = (
        keep_b[0].astype(F32) + came_b[0].astype(F32) + last_b[...].astype(F32)
    )
    for ref, lines in ((next_keep_ref, (0, turn ^ 2)), (next_give_ref, (turn, 2))):
        for slot, mask in enumerate(lines):
            line = at[SECOND] ^ mask
            for yl in range(2):
                ref[slot, yl] = total[line * 2 + yl].astype(ref.dtype)


def total_kernel(own_at, at, keep, came, last, mine_ref, given_ref, total):
    total[...] = keep[0] + came[0].astype(F32) + last[...].astype(F32)
    mine_ref[...] = total[at[own_at]]
    given_ref[...] = total[1 - at[own_at]].astype(BF16)


def piece_kernel(at, mine_ref, beside_ref, piece_ref, sent_ref):
    piece = mine_ref[...] + beside_ref[...].astype(F32)
    piece_ref[...] = piece
    sent_ref[...] = piece.astype(BF16)


def adapt_last_kernel(at, mine_ref, beside_ref, first_ref, second_ref):
    total = mine_ref[...] + beside_ref[...].astype(F32)
    total = jnp.where(at[GROUP_AT] < 3, total, 0.0)
    first_ref[0] = total[:, :640]
    second_ref[0, :, :640] = total[:20, 640:]
    second_ref[0, :, 640:] = total[20:, 640:]


def last_kernel(at, high_ref, low_ref, out_low_ref, out_high_ref, in_ref, out_ref):
    student = at[GROUP_AT] == 3
    in_ref[0, :, :1280] = jnp.where(student, low_ref[...], 0.0)
    in_ref[0, :, 1280:] = jnp.where(student, high_ref[...], 0.0)
    for start, ref in ((0, out_low_ref), (640, out_high_ref)):
        total = jnp.where(student, ref[...].astype(F32), 0.0)
        out_ref[0, :40, start : start + 640] = total[:, :640]
        out_ref[0, 40:, start : start + 640] = total[:, 640:]


def first_axis(mask):
    def to(yh, core, z, yl, x):
        return (yh, core, z, yl, x ^ mask) if core == 0 else (yh, core, z ^ mask, yl, x)

    return to


def second_axis(mask):
    def to(yh, core, z, yl, x):
        return (yh, core, z ^ mask, yl, x) if core == 0 else (yh, core, z, yl, x ^ mask)

    return to


def beside(yh, core, z, yl, x):
    return (yh, core, z, 1 - yl, x)


def first_next(scalars, keep_a, came_a, keep_b, came_b):
    next_a, next_b = call(
        next_two_kernel,
        scalars,
        (keep_a, came_a, keep_b, came_b),
        [shaped(keep_a.shape[1:], BF16)] * 2,
    )
    last_a = send(next_a, first_axis(3))
    last_b = send(next_b, first_axis(1))
    return keep_a, came_a, last_a, keep_b, came_b, last_b


def both_axes(scalars, student, adaptor):
    keep_a, give_a, keep_b, give_b = student
    came_a = send(give_a, first_axis(1))
    came_b = send(give_b, first_axis(3))
    adapt_keep_a, adapt_came_a, adapt_keep_b, adapt_came_b = adaptor
    adapt_parts = first_next(scalars, adapt_keep_a, adapt_came_a, adapt_keep_b, adapt_came_b)
    keep_b, *adapt_lasts = lax.optimization_barrier((keep_b, adapt_parts[2], adapt_parts[5]))
    parts = first_next(scalars, keep_a, came_a, keep_b, came_b)
    piece = (2, 2, 40, 1280)
    shapes = [shaped(piece, F32), shaped(piece, BF16)]
    scratch = [pltpu.VMEM((8, 40, 1280), F32)]
    keep, give = call(
        functools.partial(axis_two_kernel, 1),
        scalars,
        parts,
        shapes,
        scratch,
    )
    came = send(give, second_axis(1))
    keep, adapt_last = lax.optimization_barrier((keep, adapt_lasts[0]))
    adapt_parts = (*adapt_parts[:2], adapt_last, *adapt_parts[3:5], adapt_lasts[1])
    adapt_keep, adapt_give = call(
        functools.partial(axis_two_kernel, 3), scalars, adapt_parts, shapes, scratch
    )
    adapt_came = send(adapt_give, second_axis(3))
    (onward,) = call(next_kernel, scalars, (keep, came), [shaped(piece[1:], BF16)])
    last = send(onward, second_axis(3))
    onward, adapt_came = lax.optimization_barrier((onward, adapt_came))
    (adapt_next,) = call(
        next_kernel, scalars, (adapt_keep, adapt_came), [shaped(piece[1:], BF16)]
    )
    adapt_last = send(adapt_next, second_axis(1))
    piece = (40, 1280)
    mine, given = call(
        functools.partial(total_kernel, KEEP),
        scalars,
        (keep, came, last),
        [shaped(piece, F32), shaped(piece, BF16)],
        [pltpu.VMEM((2, 40, 1280), F32)],
    )
    came = send(given, beside)
    mine, adapt_last = lax.optimization_barrier((mine, adapt_last))
    adapt_mine, adapt_given = call(
        functools.partial(total_kernel, YL),
        scalars,
        (adapt_keep, adapt_came, adapt_last),
        [shaped(piece, F32), shaped(piece, BF16)],
        [pltpu.VMEM((2, 40, 1280), F32)],
    )
    adapt_came = send(adapt_given, beside)
    came, adapt_mine = lax.optimization_barrier((came, adapt_mine))
    return mine, came, adapt_mine, adapt_came


def block_ids(order, positions, per_image):
    slots = jnp.arange(order.shape[0], dtype=jnp.int32)
    image = jnp.sum(
        jnp.where((positions // per_image)[:, None] == slots[None, :], order[None, :], 0), axis=1
    )
    return image * per_image + positions % per_image


def swap_core(yh, core, z, yl, x):
    return (yh, 1 - core, z, yl, x)


def out_across(yh, core, z, yl, x):
    if yh == 1 and core == 1:
        return (0, core, z, 1 - yl, x)


def exchange_across(yh, core, z, yl, x):
    return (1 - yh, core, z, 1 - yl, x)


def body(acts, block_in, block_out, adapt_in, adapt_out, owner):
    core = lax.axis_index("core")
    group_index = lax.axis_index(GROUP)
    x, yl, z = lax.axis_index("x"), lax.axis_index("yl"), lax.axis_index("z")
    wide_count = lax.axis_size(WIDE)
    token_count = acts.shape[1]
    width = acts.shape[2]
    piece = token_count // wide_count
    half = token_count // 2
    per_image = PATCHES // token_count
    loss_scale = 1.0 / (token_count * wide_count) ** 0.5
    scalars = jnp.stack(
        [
            core,
            1 - lax.axis_index("yh"),
            group_index,
            jnp.minimum(group_index, 2),
            yl,
            jnp.where(lax.axis_index("yh") == 0, 1 - yl, yl),
            jnp.where(core == 0, x, z),
            jnp.where(core == 0, z, x),
        ]
    ).astype(jnp.int32)

    own_order = lax.dynamic_index_in_dim(owner, group_index, 0, keepdims=False)
    positions = jnp.arange(token_count, dtype=jnp.int32) // piece
    wanted = block_ids(owner[3], positions, per_image)
    present = block_ids(own_order, positions, per_image)
    inner = jnp.arange(token_count, dtype=jnp.int32) % piece
    sorter = (wanted[:, None] == present[None, :]) & (inner[:, None] == inner[None, :])
    sorter = sorter.astype(BF16)

    hidden, hand, slope, output, outgoing = block_forward(scalars, acts, block_in, block_out)

    crossed = send(output, out_across)
    handed = send(hand, swap_core)
    hidden_crossed = send(hidden, out_across)
    arrived = lax.all_to_all(outgoing, WIDE, split_axis=0, concat_axis=0, tiled=True)
    (shared,) = call(
        pick_kernel, scalars, (output, crossed), [shaped((token_count, width), BF16)]
    )
    features = send(shared, swap_core)
    student, gamma, mixed = adapt_call(
        adapt_forward_kernel,
        scalars,
        (shared, features),
        adapt_in,
        adapt_out,
        [
            shaped((token_count, width), BF16),
            shaped((token_count, 640), BF16),
            shaped((token_count, width + 640), F32),
        ],
    )
    mixed, handed = lax.optimization_barrier((mixed, handed))
    grad_pred, grad_zeta, kept, given = adapt_call(
        functools.partial(adapt_backward_kernel, loss_scale),
        scalars,
        (sorter, arrived, mixed),
        adapt_in,
        adapt_out,
        [
            shaped((token_count, width), BF16),
            shaped((token_count, 640), BF16),
            shaped((half, width), F32),
            shaped((half, width), BF16),
        ],
    )

    came = send(given, swap_core)
    adapt_keep_a, adapt_give_a, adapt_keep_b, adapt_give_b = call(
        adapt_partial_kernel,
        scalars,
        (student, grad_zeta, gamma, grad_pred),
        [shaped((2, 8, 40, 640), BF16)] * 4,
        [pltpu.VMEM((32, 40, 1280), F32)],
        24,
        4 * token_count * width * 640,
    )
    came, adapt_keep_a = lax.optimization_barrier((came, adapt_keep_a))
    pair, pair_b = call(
        pair_kernel,
        scalars,
        (kept, came),
        [shaped((half, width), F32), shaped((half, width), BF16)],
    )
    pair, hidden_crossed = lax.optimization_barrier((pair, hidden_crossed))
    hidden_core = send(hidden_crossed, swap_core)
    across = send(pair_b, exchange_across)
    left, slopes, weights = stage(
        scalars, (hidden_crossed, hidden_core, hand, handed, slope, block_out)
    )
    across, left = lax.optimization_barrier((across, left))
    adapt_came_a = send(adapt_give_a, first_axis(1))
    adapt_came_b = send(adapt_give_b, first_axis(3))
    (mine,) = call(half_kernel, scalars, (pair, across), [shaped((half, width), BF16)])
    other = send(mine, swap_core)
    other, adapt_came_a, adapt_came_b = lax.optimization_barrier(
        (other, adapt_came_a, adapt_came_b)
    )
    keep_a, give_a, keep_b, give_b = student_partial(
        scalars, (left, slopes, weights), mine, other
    )
    mine, came, adapt_mine, adapt_came = both_axes(
        scalars,
        (keep_a, give_a, keep_b, give_b),
        (adapt_keep_a, adapt_came_a, adapt_keep_b, adapt_came_b),
    )
    piece, piece_b = call(
        piece_kernel, scalars, (mine, came), [shaped((40, 1280), F32), shaped((40, 1280), BF16)]
    )
    out_high = send(piece_b, exchange_across)
    low_piece = send(piece, swap_core)
    out_low = send(out_high, swap_core)
    piece, adapt_came = lax.optimization_barrier((piece, adapt_came))
    grad_first, grad_second = call(
        adapt_last_kernel,
        scalars,
        (adapt_mine, adapt_came),
        [shaped((1, 40, 640), F32), shaped((1, 20, 1280), F32)],
    )
    grad_in_sum, grad_out_sum = call(
        last_kernel,
        scalars,
        (piece, low_piece, out_low, out_high),
        [shaped((1, 40, 2560), F32), shaped((1, 80, 1280), F32)],
    )
    return (grad_first, grad_second, grad_in_sum, grad_out_sum)


def solution(mesh):
    fine = Mesh(mesh.devices.reshape(SIZES), ALL)
    placed = (
        P(GROUP, WIDE, None),
        P(GROUP, None, None),
        P(GROUP, None, None),
        P(),
        P(),
        P(),
    )
    return jax.shard_map(
        body,
        mesh=fine,
        in_specs=placed,
        out_specs=(P(GROUP, WIDE, None),) * 4,
        check_vma=False,
    )
```

time: 740 us -> 125 us (0.17)
  waiting for transfers between devices: 531 us -> 52.7 us
  blocking collectives: 105 us -> 0 us
  matrix products: 48.6 us -> 0 us
  Pallas kernels: 0 us -> 36 us
  between operations: 14.8 us -> 0.93 us
  starting transfers between devices: 22.1 us -> 31.9 us
  other arithmetic: 8.63 us -> 0.24 us
    reduce_scatter x2 -> x0, waiting for transfers between devices: 382 us -> none  [the longest x1 191 us: body(): lax.psum_scatter(term_block_out, 'wide', scatter_dimension=0, tiled=True)]
    unnamed x1 -> x0, blocking collectives: 105 us -> none
    psum x2 -> x0, waiting for transfers between devices: 86.9 us -> none  [the longest x1 45 us: broadcast(): return lax.psum(kept, axis)]
    ppermute x0 -> x25, waiting for transfers between devices: none -> 48.9 us  [send(): return lax.ppermute(value, ALL, route(move))]
    dot_general x10 -> x0, matrix products: 48.6 us -> none  [the longest x4 27.1 us: contract_rows(): lax.dot_general(left, right, (((0,), (0,)), ((), ())), preferred_element_...]
    pallas_call x0 -> x20, Pallas kernels: none -> 36 us  [the longest x16 15.2 us: call(): pl.pallas_call(kernel, out_shape=list(outputs), in_specs=[smem()] + vmem(...]
    unnamed x12 -> x0, waiting for transfers between devices: 30.2 us -> none
    all_to_all x2 -> x1, waiting for transfers between devices: 31.3 us -> 3.75 us  [body(): lax.all_to_all(outgoing, WIDE, split_axis=0, concat_axis=0, tiled=True)]
  transfers between devices with their start and end apart: 13 -> 26, of which waited for: 8 -> 15; matrix products, arithmetic and copies ran while one was open for 18% -> 1% of each run, Pallas kernels for 0% -> 15%
where the time goes in v1:
time: 125 us; the launch traced here: 124 us
  waiting for transfers between devices  52.7 us (42%)
  Pallas kernels  36 us (29%)
  starting transfers between devices  31.9 us (26%)
  local copies, waits for them, and re-layouts  2.62 us (2%)
    ppermute x25, waiting for transfers between devices, send(): return lax.ppermute(value, ALL, route(move))  48.9 us
    ppermute x25, starting transfers between devices, send(): return lax.ppermute(value, ALL, route(move))  22.6 us
    pallas_call x16, Pallas kernels, call(): pl.pallas_call(kernel, out_shape=list(outputs), in_specs=[smem()] + vmem(...  15.2 us
    pallas_call x1, Pallas kernels, block_forward(): pl.pallas_call(forward_kernel, out_shape=[pltpu.HBM((tokens, hidden), BF1...  11.2 us
    all_to_all x1, starting transfers between devices, body(): lax.all_to_all(outgoing, WIDE, split_axis=0, concat_axis=0, tiled=True)  9.27 us
    pallas_call x2, Pallas kernels, adapt_call(): pl.pallas_call(kernel, out_shape=list(outputs), in_specs=[smem()] + vmem(...  7.69 us
    all_to_all x1, waiting for transfers between devices, body(): lax.all_to_all(outgoing, WIDE, split_axis=0, concat_axis=0, tiled=True)  3.75 us
    unnamed x9, local copies, waits for them, and re-layouts  2.52 us
  transfers between devices with their start and end apart: 26, of which 15 were waited for; matrix products, arithmetic and copies ran while one was open for 1% of the time, Pallas kernels for 15%

profile of v1, /device:TPU:0, one launch (start us, length us, event | category | flops | bytes accessed | tf_op | source)
XLA Modules:
  0.0 124.3 jit_solution(4298678032845235269)
XLA Ops:
  0.7 11.2 %shard_map.93 = (bf16[256,2560]{1,0:T(8,128)(2,1)}, bf16[1792,1280]{1,0:T(8,128)(2,1)}, bf16[256,1280]{1,0:T(8,128)(2,1)}, bf16[256,1280]{1,0:T(8,128)(2,1)S(1)}, bf16[256,1280]{1,0:T(8,128)(2,1)}) custom-call(s32[8]{0:T(128)S(1)} %stack.35.at, bf16[1,256,1280]{2,1,0:T(8,128)(2,1)} %acts_hbm.1, bf16[1,1280,2560]{2,1,0:T(8,128)(2,1)} %first_hbm.3, ...), custom_call_target="tpu_custom_call" | custom-call | flops 3355443200 | bytes 16777216 | tf_op jit(solution)/shard_map/pallas_call | solution.py:199
  12.7 9.3 %all-to-all-start = ((bf16[32,8,1280]{2,1,0:T(8,128)(2,1)}), bf16[32,8,1280]{2,1,0:T(8,128)(2,1)S(1)}, u32[]{:S(2)}, u32[]{:S(2)}) async-start(bf16[32,8,1280]{2,1,0:T(8,128)(2,1)} %bitcast.10), calls=%async_computation | async-start | bytes 1310720 | tf_op jit(solution)/shard_map/all_to_all | solution.py:671
  22.0 1.7 %collective-permute-start.5 = (bf16[256,2560]{1,0:T(8,128)(2,1)}, bf16[256,2560]{1,0:T(8,128)(2,1)}, u32[]{:S(2)}, u32[]{:S(2)}) collective-permute-start(bf16[256,2560]{1,0:T(8,128)(2,1)} %get-tuple-element.85), channel_id=1, source_target_pairs={{96,36},{97,37},{98,38},{99,39},{100,32},{101,33},{102,34},{103,35... | collective-permute-start | bytes 3932168 | tf_op jit(solution)/shard_map/ppermute | solution.py:43
  24.4 1.3 %collective-permute-start.1 = (bf16[256,1280]{1,0:T(8,128)(2,1)S(1)}, bf16[256,1280]{1,0:T(8,128)(2,1)S(1)}, u32[]{:S(2)}, u32[]{:S(2)}) collective-permute-start(bf16[256,1280]{1,0:T(8,128)(2,1)S(1)} %shard_map.94.shared_ref), channel_id=1, source_target_pairs={{0,32},{1,33},{2,34},{3,35},{4,36},{5,37},{6,38},{7,39},{8,40},{9,... | collective-permute-start | bytes 1966088 | tf_op jit(solution)/shard_map/ppermute | solution.py:43
  26.0 1.5 %collective-permute-done.1.handed_ref = bf16[256,1280]{1,0:T(8,128)(2,1)S(1)} collective-permute-done((bf16[256,1280]{1,0:T(8,128)(2,1)S(1)}, bf16[256,1280]{1,0:T(8,128)(2,1)S(1)}, u32[]{:S(2)}, u32[]{:S(2)}) %collective-permute-start.1) | collective-permute-done | bytes 655392 | tf_op jit(solution)/shard_map/ppermute | solution.py:43
  27.4 3.7 %shard_map.95 = (bf16[256,1280]{1,0:T(8,128)(2,1)S(1)}, bf16[256,640]{1,0:T(8,128)(2,1)S(1)}, f32[256,1920]{1,0:T(8,128)S(1)}) custom-call(s32[8]{0:T(128)S(1)} %stack.35.at, bf16[256,1280]{1,0:T(8,128)(2,1)S(1)} %shard_map.94.shared_ref, bf16[256,1280]{1,0:T(8,128)(2,1)S(1)} %collective-permute-done.1.handed_ref, bf16[3,1280,640]{2,1,0:T(8,128)(2,1)} %first_hbm.5, ...), custom_call_target="tpu_custom_call" | custom-call | flops 1024 | bytes 1024 | tf_op jit(solution)/shard_map/pallas_call | solution.py:269
  31.9 3.8 %all-to-all-done = bf16[32,8,1280]{2,1,0:T(8,128)(2,1)S(1)} async-done(((bf16[32,8,1280]{2,1,0:T(8,128)(2,1)}), bf16[32,8,1280]{2,1,0:T(8,128)(2,1)S(1)}, u32[]{:S(2)}, u32[]{:S(2)}) %all-to-all-start) | async-done | bytes 655392 | tf_op jit(solution)/shard_map/all_to_all | solution.py:671
  35.7 3.9 %shard_map.96 = (bf16[256,1280]{1,0:T(8,128)(2,1)S(1)}, bf16[256,640]{1,0:T(8,128)(2,1)S(1)}, f32[128,1280]{1,0:T(8,128)S(1)}, bf16[128,1280]{1,0:T(8,128)(2,1)S(1)}) custom-call(s32[8]{0:T(128)S(1)} %stack.35.at, bf16[256,256]{1,0:T(8,128)(2,1)S(1)} %and_convert_fusion.sorter_ref, bf16[256,1280]{1,0:T(8,128)(2,1)S(1)} %bitcast.14, ...), custom_call_target="tpu_custom_call" | custom-call | flops 1024 | bytes 1024 | tf_op jit(solution)/shard_map/pallas_call | solution.py:269
  39.7 2.0 %shard_map.97 = (bf16[2,8,40,640]{3,2,1,0:T(8,128)(2,1)S(1)}, bf16[2,8,40,640]{3,2,1,0:T(8,128)(2,1)S(1)}, bf16[2,8,40,640]{3,2,1,0:T(8,128)(2,1)S(1)}, bf16[2,8,40,640]{3,2,1,0:T(8,128)(2,1)S(1)}) custom-call(s32[8]{0:T(128)S(1)} %stack.35.at, bf16[256,1280]{1,0:T(8,128)(2,1)S(1)} %get-tuple-element.77.student_ref, ...), custom_call_target="tpu_custom_call" | custom-call | flops 838860800 | bytes 5242880 | tf_op jit(solution)/shard_map/pallas_call | solution.py:64
  44.2 2.1 %collective-permute-start.9 = (bf16[2,8,40,640]{3,2,1,0:T(8,128)(2,1)S(1)}, bf16[2,8,40,640]{3,2,1,0:T(8,128)(2,1)S(1)}, u32[]{:S(2)}, u32[]{:S(2)}) collective-permute-start(bf16[2,8,40,640]{3,2,1,0:T(8,128)(2,1)S(1)} %get-tuple-element.96), channel_id=1, source_target_pairs={{0,3},{1,2},{2,1},{3,0},{4,7},{5,6},{6,5},{7,4},{8,11},{9,10},{10,... | collective-permute-start | bytes 2457608 | tf_op jit(solution)/shard_map/ppermute | solution.py:43
  46.2 1.4 %collective-permute-start.4 = (bf16[128,1280]{1,0:T(8,128)(2,1)S(1)}, bf16[128,1280]{1,0:T(8,128)(2,1)S(1)}, u32[]{:S(2)}, u32[]{:S(2)}) collective-permute-start(bf16[128,1280]{1,0:T(8,128)(2,1)S(1)} %get-tuple-element.83), channel_id=1, source_target_pairs={{0,68},{1,69},{2,70},{3,71},{4,64},{5,65},{6,66},{7,67},{8,76},{9,... | collective-permute-start | bytes 983048 | tf_op jit(solution)/shard_map/ppermute | solution.py:43
  48.7 1.9 %shard_map.99 = (bf16[256,2560]{1,0:T(8,128)(2,1)S(1)}, bf16[256,1280]{1,0:T(8,128)(2,1)S(1)}, bf16[1280,1280]{1,0:T(8,128)(2,1)S(1)}) custom-call(s32[8]{0:T(128)S(1)} %stack.35.at, bf16[256,2560]{1,0:T(8,128)(2,1)} %collective-permute-done.5.crossed_hbm, bf16[256,2560]{1,0:T(8,128)(2,1)} %copy-done.2, bf16[1792,1280]{1,0:T(8,128)(2,1)} %get-tuple-element.73.hand_hbm, ...), custom_call_target="tpu_custom_call" | custom-call | bytes 8388608 | tf_op jit(solution)/shard_map/pallas_call | solution.py:398
  50.6 5.9 %collective-permute-done.4.across_ref = bf16[128,1280]{1,0:T(8,128)(2,1)S(1)} collective-permute-done((bf16[128,1280]{1,0:T(8,128)(2,1)S(1)}, bf16[128,1280]{1,0:T(8,128)(2,1)S(1)}, u32[]{:S(2)}, u32[]{:S(2)}) %collective-permute-start.4) | collective-permute-done | bytes 327712 | tf_op jit(solution)/shard_map/ppermute | solution.py:43
  58.8 2.1 %shard_map.101 = (bf16[2,8,40,640]{3,2,1,0:T(8,128)(2,1)S(1)}, bf16[2,8,40,640]{3,2,1,0:T(8,128)(2,1)S(1)}, bf16[2,8,40,640]{3,2,1,0:T(8,128)(2,1)S(1)}, bf16[2,8,40,640]{3,2,1,0:T(8,128)(2,1)S(1)}) custom-call(s32[8]{0:T(128)S(1)} %stack.35.at, bf16[256,2560]{1,0:T(8,128)(2,1)S(1)} %get-tuple-element.90.left, ...), custom_call_target="tpu_custom_call" | custom-call | flops 1677721600 | bytes 9175040 | tf_op jit(solution)/shard_map/pallas_call | solution.py:64
  60.9 1.5 %collective-permute-start.10 = (bf16[2,8,40,640]{3,2,1,0:T(8,128)(2,1)S(1)}, bf16[2,8,40,640]{3,2,1,0:T(8,128)(2,1)S(1)}, u32[]{:S(2)}, u32[]{:S(2)}) collective-permute-start(bf16[2,8,40,640]{3,2,1,0:T(8,128)(2,1)S(1)} %get-tuple-element.99), channel_id=1, source_target_pairs={{0,1},{1,0},{2,3},{3,2},{4,5},{5,4},{6,7},{7,6},{8,9},{9,8},{10,11... | collective-permute-start | bytes 2457608 | tf_op jit(solution)/shard_map/ppermute | solution.py:43
  62.5 1.3 %collective-permute-start.13 = (bf16[2,8,40,640]{3,2,1,0:T(8,128)(2,1)S(1)}, bf16[2,8,40,640]{3,2,1,0:T(8,128)(2,1)S(1)}, u32[]{:S(2)}, u32[]{:S(2)}) collective-permute-start(bf16[2,8,40,640]{3,2,1,0:T(8,128)(2,1)S(1)} %get-tuple-element.108), channel_id=1, source_target_pairs={{0,3},{1,2},{2,1},{3,0},{4,7},{5,6},{6,5},{7,4},{8,11},{9,10},{10,... | collective-permute-start | bytes 2457608 | tf_op jit(solution)/shard_map/ppermute | solution.py:43
  64.5 2.0 %collective-permute-start.11 = (bf16[8,40,640]{2,1,0:T(8,128)(2,1)S(1)}, bf16[8,40,640]{2,1,0:T(8,128)(2,1)S(1)}, u32[]{:S(2)}, u32[]{:S(2)}) collective-permute-start(bf16[8,40,640]{2,1,0:T(8,128)(2,1)S(1)} %get-tuple-element.105), channel_id=1, source_target_pairs={{0,3},{1,2},{2,1},{3,0},{4,7},{5,6},{6,5},{7,4},{8,11},{9,10},{10,... | collective-permute-start | bytes 1228808 | tf_op jit(solution)/shard_map/ppermute | solution.py:43
  66.5 13.9 %collective-permute-done.11.last_a = bf16[8,40,640]{2,1,0:T(8,128)(2,1)S(1)} collective-permute-done((bf16[8,40,640]{2,1,0:T(8,128)(2,1)S(1)}, bf16[8,40,640]{2,1,0:T(8,128)(2,1)S(1)}, u32[]{:S(2)}, u32[]{:S(2)}) %collective-permute-start.11) | collective-permute-done | bytes 409632 | tf_op jit(solution)/shard_map/ppermute | solution.py:43
  81.2 1.4 %collective-permute-start.14 = (bf16[8,40,640]{2,1,0:T(8,128)(2,1)S(1)}, bf16[8,40,640]{2,1,0:T(8,128)(2,1)S(1)}, u32[]{:S(2)}, u32[]{:S(2)}) collective-permute-start(bf16[8,40,640]{2,1,0:T(8,128)(2,1)S(1)} %get-tuple-element.109), channel_id=1, source_target_pairs={{0,3},{1,2},{2,1},{3,0},{4,7},{5,6},{6,5},{7,4},{8,11},{9,10},{10,... | collective-permute-start | bytes 1228808 | tf_op jit(solution)/shard_map/ppermute | solution.py:43
  82.7 7.7 %collective-permute-done.14.last_a = bf16[8,40,640]{2,1,0:T(8,128)(2,1)S(1)} collective-permute-done((bf16[8,40,640]{2,1,0:T(8,128)(2,1)S(1)}, bf16[8,40,640]{2,1,0:T(8,128)(2,1)S(1)}, u32[]{:S(2)}, u32[]{:S(2)}) %collective-permute-start.14) | collective-permute-done | bytes 409632 | tf_op jit(solution)/shard_map/ppermute | solution.py:43
  91.6 2.0 %collective-permute-start.16 = (bf16[2,2,40,1280]{3,2,1,0:T(8,128)(2,1)S(1)}, bf16[2,2,40,1280]{3,2,1,0:T(8,128)(2,1)S(1)}, u32[]{:S(2)}, u32[]{:S(2)}) collective-permute-start(bf16[2,2,40,1280]{3,2,1,0:T(8,128)(2,1)S(1)} %get-tuple-element.114), channel_id=1, source_target_pairs={{0,8},{1,9},{2,10},{3,11},{4,12},{5,13},{6,14},{7,15},{8,0},{9,1},... | collective-permute-start | bytes 1228808 | tf_op jit(solution)/shard_map/ppermute | solution.py:43
  95.1 4.6 %collective-permute-done.16.came_ref.came = bf16[2,2,40,1280]{3,2,1,0:T(8,128)(2,1)S(1)} collective-permute-done((bf16[2,2,40,1280]{3,2,1,0:T(8,128)(2,1)S(1)}, bf16[2,2,40,1280]{3,2,1,0:T(8,128)(2,1)S(1)}, u32[]{:S(2)}, u32[]{:S(2)}) %collective-permute-start.16) | collective-permute-done | bytes 409632 | tf_op jit(solution)/shard_map/ppermute | solution.py:43
  100.2 2.0 %collective-permute-start.17 = (bf16[2,40,1280]{2,1,0:T(8,128)(2,1)S(1)}, bf16[2,40,1280]{2,1,0:T(8,128)(2,1)S(1)}, u32[]{:S(2)}, u32[]{:S(2)}) collective-permute-start(bf16[2,40,1280]{2,1,0:T(8,128)(2,1)S(1)} %shard_map.105), channel_id=1, source_target_pairs={{0,24},{1,25},{2,26},{3,27},{4,28},{5,29},{6,30},{7,31},{8,16},{9,... | collective-permute-start | bytes 614408 | tf_op jit(solution)/shard_map/ppermute | solution.py:43
  102.2 1.7 %collective-permute-done.19.came_ref.came = bf16[2,2,40,1280]{3,2,1,0:T(8,128)(2,1)S(1)} collective-permute-done((bf16[2,2,40,1280]{3,2,1,0:T(8,128)(2,1)S(1)}, bf16[2,2,40,1280]{3,2,1,0:T(8,128)(2,1)S(1)}, u32[]{:S(2)}, u32[]{:S(2)}) %collective-permute-start.19) | collective-permute-done | bytes 409632 | tf_op jit(solution)/shard_map/ppermute | solution.py:43
  104.5 2.7 %collective-permute-done.17.last = bf16[2,40,1280]{2,1,0:T(8,128)(2,1)S(1)} collective-permute-done((bf16[2,40,1280]{2,1,0:T(8,128)(2,1)S(1)}, bf16[2,40,1280]{2,1,0:T(8,128)(2,1)S(1)}, u32[]{:S(2)}, u32[]{:S(2)}) %collective-permute-start.17) | collective-permute-done | bytes 204832 | tf_op jit(solution)/shard_map/ppermute | solution.py:43
  108.0 2.3 %collective-permute-done.20.last = bf16[2,40,1280]{2,1,0:T(8,128)(2,1)S(1)} collective-permute-done((bf16[2,40,1280]{2,1,0:T(8,128)(2,1)S(1)}, bf16[2,40,1280]{2,1,0:T(8,128)(2,1)S(1)}, u32[]{:S(2)}, u32[]{:S(2)}) %collective-permute-start.20) | collective-permute-done | bytes 204832 | tf_op jit(solution)/shard_map/ppermute | solution.py:43
  110.9 1.7 %collective-permute-done.18.beside_ref = bf16[40,1280]{1,0:T(8,128)(2,1)S(1)} collective-permute-done((bf16[40,1280]{1,0:T(8,128)(2,1)S(1)}, bf16[40,1280]{1,0:T(8,128)(2,1)S(1)}, u32[]{:S(2)}, u32[]{:S(2)}) %collective-permute-start.18) | collective-permute-done | bytes 102432 | tf_op jit(solution)/shard_map/ppermute | solution.py:43
  113.2 2.4 %collective-permute-start.23 = (bf16[40,1280]{1,0:T(8,128)(2,1)S(1)}, bf16[40,1280]{1,0:T(8,128)(2,1)S(1)}, u32[]{:S(2)}, u32[]{:S(2)}) collective-permute-start(bf16[40,1280]{1,0:T(8,128)(2,1)S(1)} %get-tuple-element.133), channel_id=1, source_target_pairs={{0,68},{1,69},{2,70},{3,71},{4,64},{5,65},{6,66},{7,67},{8,76},{9,... | collective-permute-start | bytes 307208 | tf_op jit(solution)/shard_map/ppermute | solution.py:43
  115.6 3.5 %collective-permute-done.23.out_high_ref = bf16[40,1280]{1,0:T(8,128)(2,1)S(1)} collective-permute-done((bf16[40,1280]{1,0:T(8,128)(2,1)S(1)}, bf16[40,1280]{1,0:T(8,128)(2,1)S(1)}, u32[]{:S(2)}, u32[]{:S(2)}) %collective-permute-start.23) | collective-permute-done | bytes 102432 | tf_op jit(solution)/shard_map/ppermute | solution.py:43
  119.2 1.8 %collective-permute-done.21.beside_ref = bf16[40,1280]{1,0:T(8,128)(2,1)S(1)} collective-permute-done((bf16[40,1280]{1,0:T(8,128)(2,1)S(1)}, bf16[40,1280]{1,0:T(8,128)(2,1)S(1)}, u32[]{:S(2)}, u32[]{:S(2)}) %collective-permute-start.21) | collective-permute-done | bytes 102432 | tf_op jit(solution)/shard_map/ppermute | solution.py:43
  120.9 1.2 shard_map.111
  122.9 1.5 %shard_map.112 = (f32[1,40,2560]{2,1,0:T(8,128)}, f32[1,80,1280]{2,1,0:T(8,128)}) custom-call(s32[8]{0:T(128)S(1)} %stack.35.at, f32[40,1280]{1,0:T(8,128)S(1)} %get-tuple-element.132.high_ref, f32[40,1280]{1,0:T(8,128)S(1)} %collective-permute-done.22.low_ref, bf16[40,1280]{1,0:T(8,128)(2,1)S(1)} %collective-permute-done.24.out_low_ref, ...), custom_call_target="tpu_custom_call" | custom-call | bytes 1433600 | tf_op jit(solution)/shard_map/pallas_call | solution.py:64
  (56 shorter events, 16.4 us)
Async XLA Ops:
  0.7 23.0 %copy-start.3 = (s32[4,8]{1,0:T(4,128)S(1)}, s32[4,8]{1,0:T(4,128)}, u32[]{:S(2)}) copy-start(s32[4,8]{1,0:T(4,128)} %param.11) | copy-start | bytes 388
  11.9 20.0 %collective-permute-start.2 = (bf16[1792,1280]{1,0:T(8,128)(2,1)}, bf16[1792,1280]{1,0:T(8,128)(2,1)}, u32[]{:S(2)}, u32[]{:S(2)}) collective-permute-start(bf16[1792,1280]{1,0:T(8,128)(2,1)} %get-tuple-element.73.hand_hbm), channel_id=1, source_target_pairs={{0,32},{1,33},{2,34},{3,35},{4,36},{5,37},{6,38},{7,39},{8,40},{9,... | collective-permute-start | bytes 13762568 | tf_op jit(solution)/shard_map/ppermute | solution.py:43
  12.0 11.8 %collective-permute-start = (bf16[256,1280]{1,0:T(8,128)(2,1)S(1)}, bf16[256,1280]{1,0:T(8,128)(2,1)S(1)}, u32[]{:S(2)}, u32[]{:S(2)}) collective-permute-start(bf16[256,1280]{1,0:T(8,128)(2,1)S(1)} %get-tuple-element.71.own_ref), channel_id=1, source_target_pairs={{96,36},{97,37},{98,38},{99,39},{100,32},{101,33},{102,34},{103,35... | collective-permute-start | bytes 1966088 | tf_op jit(solution)/shard_map/ppermute | solution.py:43
  12.7 23.0 %all-to-all-start = ((bf16[32,8,1280]{2,1,0:T(8,128)(2,1)}), bf16[32,8,1280]{2,1,0:T(8,128)(2,1)S(1)}, u32[]{:S(2)}, u32[]{:S(2)}) async-start(bf16[32,8,1280]{2,1,0:T(8,128)(2,1)} %bitcast.10), calls=%async_computation | async-start | bytes 1310720 | tf_op jit(solution)/shard_map/all_to_all | solution.py:671
  22.0 20.4 %collective-permute-start.5 = (bf16[256,2560]{1,0:T(8,128)(2,1)}, bf16[256,2560]{1,0:T(8,128)(2,1)}, u32[]{:S(2)}, u32[]{:S(2)}) collective-permute-start(bf16[256,2560]{1,0:T(8,128)(2,1)} %get-tuple-element.85), channel_id=1, source_target_pairs={{96,36},{97,37},{98,38},{99,39},{100,32},{101,33},{102,34},{103,35... | collective-permute-start | bytes 3932168 | tf_op jit(solution)/shard_map/ppermute | solution.py:43
  24.4 3.1 %collective-permute-start.1 = (bf16[256,1280]{1,0:T(8,128)(2,1)S(1)}, bf16[256,1280]{1,0:T(8,128)(2,1)S(1)}, u32[]{:S(2)}, u32[]{:S(2)}) collective-permute-start(bf16[256,1280]{1,0:T(8,128)(2,1)S(1)} %shard_map.94.shared_ref), channel_id=1, source_target_pairs={{0,32},{1,33},{2,34},{3,35},{4,36},{5,37},{6,38},{7,39},{8,40},{9,... | collective-permute-start | bytes 1966088 | tf_op jit(solution)/shard_map/ppermute | solution.py:43
  31.2 0.7 copy-start
  35.7 4.0 %copy-start.1 = (bf16[256,640]{1,0:T(8,128)(2,1)S(1)}, bf16[256,640]{1,0:T(8,128)(2,1)}, u32[]{:S(2)}) copy-start(bf16[256,640]{1,0:T(8,128)(2,1)} %copy-done) | copy-start | bytes 983044
  39.6 2.2 %collective-permute-start.3 = (bf16[128,1280]{1,0:T(8,128)(2,1)S(1)}, bf16[128,1280]{1,0:T(8,128)(2,1)S(1)}, u32[]{:S(2)}, u32[]{:S(2)}) collective-permute-start(bf16[128,1280]{1,0:T(8,128)(2,1)S(1)} %get-tuple-element.76), channel_id=1, source_target_pairs={{0,32},{1,33},{2,34},{3,35},{4,36},{5,37},{6,38},{7,39},{8,40},{9,... | collective-permute-start | bytes 983048 | tf_op jit(solution)/shard_map/ppermute | solution.py:43
  42.4 5.2 %collective-permute-start.6 = (bf16[256,2560]{1,0:T(8,128)(2,1)}, bf16[256,2560]{1,0:T(8,128)(2,1)S(1)}, u32[]{:S(2)}, u32[]{:S(2)}) collective-permute-start(bf16[256,2560]{1,0:T(8,128)(2,1)} %collective-permute-done.5.crossed_hbm), channel_id=1, source_target_pairs={{0,32},{1,33},{2,34},{3,35},{4,36},{5,37},{6,38},{7,39},{8,40},{9,... | collective-permute-start | bytes 3932168 | tf_op jit(solution)/shard_map/ppermute | solution.py:43
  43.0 14.2 %collective-permute-start.8 = (bf16[2,8,40,640]{3,2,1,0:T(8,128)(2,1)S(1)}, bf16[2,8,40,640]{3,2,1,0:T(8,128)(2,1)S(1)}, u32[]{:S(2)}, u32[]{:S(2)}) collective-permute-start(bf16[2,8,40,640]{3,2,1,0:T(8,128)(2,1)S(1)} %get-tuple-element.95), channel_id=1, source_target_pairs={{0,1},{1,0},{2,3},{3,2},{4,5},{5,4},{6,7},{7,6},{8,9},{9,8},{10,11... | collective-permute-start | bytes 2457608 | tf_op jit(solution)/shard_map/ppermute | solution.py:43
  44.2 13.6 %collective-permute-start.9 = (bf16[2,8,40,640]{3,2,1,0:T(8,128)(2,1)S(1)}, bf16[2,8,40,640]{3,2,1,0:T(8,128)(2,1)S(1)}, u32[]{:S(2)}, u32[]{:S(2)}) collective-permute-start(bf16[2,8,40,640]{3,2,1,0:T(8,128)(2,1)S(1)} %get-tuple-element.96), channel_id=1, source_target_pairs={{0,3},{1,2},{2,1},{3,0},{4,7},{5,6},{6,5},{7,4},{8,11},{9,10},{10,... | collective-permute-start | bytes 2457608 | tf_op jit(solution)/shard_map/ppermute | solution.py:43
  46.2 10.3 %collective-permute-start.4 = (bf16[128,1280]{1,0:T(8,128)(2,1)S(1)}, bf16[128,1280]{1,0:T(8,128)(2,1)S(1)}, u32[]{:S(2)}, u32[]{:S(2)}) collective-permute-start(bf16[128,1280]{1,0:T(8,128)(2,1)S(1)} %get-tuple-element.83), channel_id=1, source_target_pairs={{0,68},{1,69},{2,70},{3,71},{4,64},{5,65},{6,66},{7,67},{8,76},{9,... | collective-permute-start | bytes 983048 | tf_op jit(solution)/shard_map/ppermute | solution.py:43
  47.7 1.1 copy-start.2
  57.1 1.7 %collective-permute-start.7 = (bf16[128,1280]{1,0:T(8,128)(2,1)S(1)}, bf16[128,1280]{1,0:T(8,128)(2,1)S(1)}, u32[]{:S(2)}, u32[]{:S(2)}) collective-permute-start(bf16[128,1280]{1,0:T(8,128)(2,1)S(1)} %shard_map.100.mine_ref), channel_id=1, source_target_pairs={{0,32},{1,33},{2,34},{3,35},{4,36},{5,37},{6,38},{7,39},{8,40},{9,... | collective-permute-start | bytes 983048 | tf_op jit(solution)/shard_map/ppermute | solution.py:43
  60.9 19.5 %collective-permute-start.10 = (bf16[2,8,40,640]{3,2,1,0:T(8,128)(2,1)S(1)}, bf16[2,8,40,640]{3,2,1,0:T(8,128)(2,1)S(1)}, u32[]{:S(2)}, u32[]{:S(2)}) collective-permute-start(bf16[2,8,40,640]{3,2,1,0:T(8,128)(2,1)S(1)} %get-tuple-element.99), channel_id=1, source_target_pairs={{0,1},{1,0},{2,3},{3,2},{4,5},{5,4},{6,7},{7,6},{8,9},{9,8},{10,11... | collective-permute-start | bytes 2457608 | tf_op jit(solution)/shard_map/ppermute | solution.py:43
  62.5 17.9 %collective-permute-start.13 = (bf16[2,8,40,640]{3,2,1,0:T(8,128)(2,1)S(1)}, bf16[2,8,40,640]{3,2,1,0:T(8,128)(2,1)S(1)}, u32[]{:S(2)}, u32[]{:S(2)}) collective-permute-start(bf16[2,8,40,640]{3,2,1,0:T(8,128)(2,1)S(1)} %get-tuple-element.108), channel_id=1, source_target_pairs={{0,3},{1,2},{2,1},{3,0},{4,7},{5,6},{6,5},{7,4},{8,11},{9,10},{10,... | collective-permute-start | bytes 2457608 | tf_op jit(solution)/shard_map/ppermute | solution.py:43
  64.5 15.9 %collective-permute-start.11 = (bf16[8,40,640]{2,1,0:T(8,128)(2,1)S(1)}, bf16[8,40,640]{2,1,0:T(8,128)(2,1)S(1)}, u32[]{:S(2)}, u32[]{:S(2)}) collective-permute-start(bf16[8,40,640]{2,1,0:T(8,128)(2,1)S(1)} %get-tuple-element.105), channel_id=1, source_target_pairs={{0,3},{1,2},{2,1},{3,0},{4,7},{5,6},{6,5},{7,4},{8,11},{9,10},{10,... | collective-permute-start | bytes 1228808 | tf_op jit(solution)/shard_map/ppermute | solution.py:43
  66.5 13.9 %collective-permute-start.12 = (bf16[8,40,640]{2,1,0:T(8,128)(2,1)S(1)}, bf16[8,40,640]{2,1,0:T(8,128)(2,1)S(1)}, u32[]{:S(2)}, u32[]{:S(2)}) collective-permute-start(bf16[8,40,640]{2,1,0:T(8,128)(2,1)S(1)} %get-tuple-element.106), channel_id=1, source_target_pairs={{0,1},{1,0},{2,3},{3,2},{4,5},{5,4},{6,7},{7,6},{8,9},{9,8},{10,11... | collective-permute-start | bytes 1228808 | tf_op jit(solution)/shard_map/ppermute | solution.py:43
  81.2 9.2 %collective-permute-start.14 = (bf16[8,40,640]{2,1,0:T(8,128)(2,1)S(1)}, bf16[8,40,640]{2,1,0:T(8,128)(2,1)S(1)}, u32[]{:S(2)}, u32[]{:S(2)}) collective-permute-start(bf16[8,40,640]{2,1,0:T(8,128)(2,1)S(1)} %get-tuple-element.109), channel_id=1, source_target_pairs={{0,3},{1,2},{2,1},{3,0},{4,7},{5,6},{6,5},{7,4},{8,11},{9,10},{10,... | collective-permute-start | bytes 1228808 | tf_op jit(solution)/shard_map/ppermute | solution.py:43
  82.6 8.0 %collective-permute-start.15 = (bf16[8,40,640]{2,1,0:T(8,128)(2,1)S(1)}, bf16[8,40,640]{2,1,0:T(8,128)(2,1)S(1)}, u32[]{:S(2)}, u32[]{:S(2)}) collective-permute-start(bf16[8,40,640]{2,1,0:T(8,128)(2,1)S(1)} %get-tuple-element.110), channel_id=1, source_target_pairs={{0,1},{1,0},{2,3},{3,2},{4,5},{5,4},{6,7},{7,6},{8,9},{9,8},{10,11... | collective-permute-start | bytes 1228808 | tf_op jit(solution)/shard_map/ppermute | solution.py:43
  91.6 8.0 %collective-permute-start.16 = (bf16[2,2,40,1280]{3,2,1,0:T(8,128)(2,1)S(1)}, bf16[2,2,40,1280]{3,2,1,0:T(8,128)(2,1)S(1)}, u32[]{:S(2)}, u32[]{:S(2)}) collective-permute-start(bf16[2,2,40,1280]{3,2,1,0:T(8,128)(2,1)S(1)} %get-tuple-element.114), channel_id=1, source_target_pairs={{0,8},{1,9},{2,10},{3,11},{4,12},{5,13},{6,14},{7,15},{8,0},{9,1},... | collective-permute-start | bytes 1228808 | tf_op jit(solution)/shard_map/ppermute | solution.py:43
  94.6 9.2 %collective-permute-start.19 = (bf16[2,2,40,1280]{3,2,1,0:T(8,128)(2,1)S(1)}, bf16[2,2,40,1280]{3,2,1,0:T(8,128)(2,1)S(1)}, u32[]{:S(2)}, u32[]{:S(2)}) collective-permute-start(bf16[2,2,40,1280]{3,2,1,0:T(8,128)(2,1)S(1)} %get-tuple-element.119), channel_id=1, source_target_pairs={{0,24},{1,25},{2,26},{3,27},{4,28},{5,29},{6,30},{7,31},{8,16},{9,... | collective-permute-start | bytes 1228808 | tf_op jit(solution)/shard_map/ppermute | solution.py:43
  100.2 7.0 %collective-permute-start.17 = (bf16[2,40,1280]{2,1,0:T(8,128)(2,1)S(1)}, bf16[2,40,1280]{2,1,0:T(8,128)(2,1)S(1)}, u32[]{:S(2)}, u32[]{:S(2)}) collective-permute-start(bf16[2,40,1280]{2,1,0:T(8,128)(2,1)S(1)} %shard_map.105), channel_id=1, source_target_pairs={{0,24},{1,25},{2,26},{3,27},{4,28},{5,29},{6,30},{7,31},{8,16},{9,... | collective-permute-start | bytes 614408 | tf_op jit(solution)/shard_map/ppermute | solution.py:43
  104.4 5.8 %collective-permute-start.20 = (bf16[2,40,1280]{2,1,0:T(8,128)(2,1)S(1)}, bf16[2,40,1280]{2,1,0:T(8,128)(2,1)S(1)}, u32[]{:S(2)}, u32[]{:S(2)}) collective-permute-start(bf16[2,40,1280]{2,1,0:T(8,128)(2,1)S(1)} %shard_map.108), channel_id=1, source_target_pairs={{0,8},{1,9},{2,10},{3,11},{4,12},{5,13},{6,14},{7,15},{8,0},{9,1},... | collective-permute-start | bytes 614408 | tf_op jit(solution)/shard_map/ppermute | solution.py:43
  107.9 4.7 %collective-permute-start.18 = (bf16[40,1280]{1,0:T(8,128)(2,1)S(1)}, bf16[40,1280]{1,0:T(8,128)(2,1)S(1)}, u32[]{:S(2)}, u32[]{:S(2)}) collective-permute-start(bf16[40,1280]{1,0:T(8,128)(2,1)S(1)} %get-tuple-element.115), channel_id=1, source_target_pairs={{0,4},{1,5},{2,6},{3,7},{4,0},{5,1},{6,2},{7,3},{8,12},{9,13},{10,... | collective-permute-start | bytes 307208 | tf_op jit(solution)/shard_map/ppermute | solution.py:43
  113.2 6.0 %collective-permute-start.23 = (bf16[40,1280]{1,0:T(8,128)(2,1)S(1)}, bf16[40,1280]{1,0:T(8,128)(2,1)S(1)}, u32[]{:S(2)}, u32[]{:S(2)}) collective-permute-start(bf16[40,1280]{1,0:T(8,128)(2,1)S(1)} %get-tuple-element.133), channel_id=1, source_target_pairs={{0,68},{1,69},{2,70},{3,71},{4,64},{5,65},{6,66},{7,67},{8,76},{9,... | collective-permute-start | bytes 307208 | tf_op jit(solution)/shard_map/ppermute | solution.py:43
  115.6 7.3 %collective-permute-start.22 = (f32[40,1280]{1,0:T(8,128)S(1)}, f32[40,1280]{1,0:T(8,128)S(1)}, u32[]{:S(2)}, u32[]{:S(2)}) collective-permute-start(f32[40,1280]{1,0:T(8,128)S(1)} %get-tuple-element.132.high_ref), channel_id=1, source_target_pairs={{0,32},{1,33},{2,34},{3,35},{4,36},{5,37},{6,38},{7,39},{8,40},{9,... | collective-permute-start | bytes 614408 | tf_op jit(solution)/shard_map/ppermute | solution.py:43
  115.6 5.3 %collective-permute-start.21 = (bf16[40,1280]{1,0:T(8,128)(2,1)S(1)}, bf16[40,1280]{1,0:T(8,128)(2,1)S(1)}, u32[]{:S(2)}, u32[]{:S(2)}) collective-permute-start(bf16[40,1280]{1,0:T(8,128)(2,1)S(1)} %get-tuple-element.128), channel_id=1, source_target_pairs={{0,4},{1,5},{2,6},{3,7},{4,0},{5,1},{6,2},{7,3},{8,12},{9,13},{10,... | collective-permute-start | bytes 307208 | tf_op jit(solution)/shard_map/ppermute | solution.py:43
  119.2 3.7 %collective-permute-start.24 = (bf16[40,1280]{1,0:T(8,128)(2,1)S(1)}, bf16[40,1280]{1,0:T(8,128)(2,1)S(1)}, u32[]{:S(2)}, u32[]{:S(2)}) collective-permute-start(bf16[40,1280]{1,0:T(8,128)(2,1)S(1)} %collective-permute-done.23.out_high_ref), channel_id=1, source_target_pairs={{0,32},{1,33},{2,34},{3,35},{4,36},{5,37},{6,38},{7,39},{8,40},{9,... | collective-permute-start | bytes 307208 | tf_op jit(solution)/shard_map/ppermute | solution.py:43

commit v2 on v1

--- a/solution.py
+++ b/solution.py
@@ -459,7 +459,7 @@
 
 
 def adapt_partial_kernel(
-    at, student_ref, grad_zeta_ref, gamma_ref, grad_pred_ref, keep_a, give_a, keep_b, give_b, terms
+    turn, at, student_ref, grad_zeta_ref, gamma_ref, grad_pred_ref, keep_ref, give_ref, terms
 ):
     first = contract_rows(student_ref[...], grad_zeta_ref[...])
     second = contract_rows(gamma_ref[...], grad_pred_ref[...])
@@ -467,8 +467,7 @@
         terms[wide, :, :640] = first[wide * 40 : wide * 40 + 40]
         terms[wide, :20, 640:] = second[wide * 20 : wide * 20 + 20, :640]
         terms[wide, 20:, 640:] = second[wide * 20 : wide * 20 + 20, 640:]
-    hand_out(at, terms, 1, keep_a, give_a, slice(0, 640))
-    hand_out(at, terms, 3, keep_b, give_b, slice(640, 1280))
+    hand_out(at, terms, turn, keep_ref, give_ref)
 
 
 def next_kernel(at, keep_ref, came_ref, give_ref):
@@ -496,24 +495,36 @@
                 ref[slot, yl] = total[line * 2 + yl].astype(ref.dtype)
 
 
-def total_kernel(own_at, at, keep, came, last, mine_ref, given_ref, total):
-    total[...] = keep[0] + came[0].astype(F32) + last[...].astype(F32)
-    mine_ref[...] = total[at[own_at]]
-    given_ref[...] = total[1 - at[own_at]].astype(BF16)
-
-
-def piece_kernel(at, mine_ref, beside_ref, piece_ref, sent_ref):
-    piece = mine_ref[...] + beside_ref[...].astype(F32)
+def axis_kernel(turn, at, keep_ref, came_ref, last_ref, next_keep_ref, next_give_ref, total):
+    total[...] = (
+        keep_ref[0].astype(F32) + came_ref[0].astype(F32) + last_ref[...].astype(F32)
+    )
+    for ref, lines in ((next_keep_ref, (0, turn ^ 2)), (next_give_ref, (turn, 2))):
+        for slot, mask in enumerate(lines):
+            line = at[SECOND] ^ mask
+            for yl in range(2):
+                ref[slot, yl] = total[line * 2 + yl].astype(ref.dtype)
+
+
+def both_kernel(
+    at, keep, came, last, adapt_keep, adapt_came, adapt_last, mine_ref, given_ref, total
+):
+    total[0] = keep[0] + came[0].astype(F32) + last[...].astype(F32)
+    total[1] = adapt_keep[0] + adapt_came[0].astype(F32) + adapt_last[...].astype(F32)
+    for slot, own in ((0, at[KEEP]), (1, at[YL])):
+        mine_ref[slot] = total[slot, own]
+        given_ref[slot] = total[slot, 1 - own].astype(BF16)
+
+
+def piece_kernel(at, mine_ref, beside_ref, piece_ref, sent_ref, first_ref, second_ref):
+    piece = mine_ref[0] + beside_ref[0].astype(F32)
     piece_ref[...] = piece
     sent_ref[...] = piece.astype(BF16)
-
-
-def adapt_last_kernel(at, mine_ref, beside_ref, first_ref, second_ref):
-    total = mine_ref[...] + beside_ref[...].astype(F32)
+    total = mine_ref[1] + beside_ref[1].astype(F32)
     total = jnp.where(at[GROUP_AT] < 3, total, 0.0)
     first_ref[0] = total[:, :640]
-    second_ref[0, :, :640] = total[:20, 640:]
-    second_ref[0, :, 640:] = total[20:, 640:]
+    second_ref[:, 0, :640] = total[:20, 640:]
+    second_ref[:, 0, 640:] = total[20:, 640:]
 
 
 def last_kernel(at, high_ref, low_ref, out_low_ref, out_high_ref, in_ref, out_ref):
@@ -544,7 +555,14 @@
     return (yh, core, z, 1 - yl, x)
 
 
-def first_next(scalars, keep_a, came_a, keep_b, came_b):
+def both_axes(scalars, keep_a, give_a, keep_b, give_b, adapt_keep, adapt_came):
+    came_a = send(give_a, first_axis(1))
+    came_b = send(give_b, first_axis(3))
+    keep_b, adapt_came = lax.optimization_barrier((keep_b, adapt_came))
+    (adapt_next,) = call(
+        next_kernel, scalars, (adapt_keep, adapt_came), [shaped(adapt_keep.shape[1:], BF16)]
+    )
+    adapt_last = send(adapt_next, first_axis(1))
     next_a, next_b = call(
         next_two_kernel,
         scalars,
@@ -553,32 +571,20 @@
     )
     last_a = send(next_a, first_axis(3))
     last_b = send(next_b, first_axis(1))
-    return keep_a, came_a, last_a, keep_b, came_b, last_b
-
-
-def both_axes(scalars, student, adaptor):
-    keep_a, give_a, keep_b, give_b = student
-    came_a = send(give_a, first_axis(1))
-    came_b = send(give_b, first_axis(3))
-    adapt_keep_a, adapt_came_a, adapt_keep_b, adapt_came_b = adaptor
-    adapt_parts = first_next(scalars, adapt_keep_a, adapt_came_a, adapt_keep_b, adapt_came_b)
-    keep_b, *adapt_lasts = lax.optimization_barrier((keep_b, adapt_parts[2], adapt_parts[5]))
-    parts = first_next(scalars, keep_a, came_a, keep_b, came_b)
     piece = (2, 2, 40, 1280)
     shapes = [shaped(piece, F32), shaped(piece, BF16)]
     scratch = [pltpu.VMEM((8, 40, 1280), F32)]
     keep, give = call(
         functools.partial(axis_two_kernel, 1),
         scalars,
-        parts,
+        (keep_a, came_a, last_a, keep_b, came_b, last_b),
         shapes,
         scratch,
     )
     came = send(give, second_axis(1))
-    keep, adapt_last = lax.optimization_barrier((keep, adapt_lasts[0]))
-    adapt_parts = (*adapt_parts[:2], adapt_last, *adapt_parts[3:5], adapt_lasts[1])
+    keep, adapt_last = lax.optimization_barrier((keep, adapt_last))
     adapt_keep, adapt_give = call(
-        functools.partial(axis_two_kernel, 3), scalars, adapt_parts, shapes, scratch
+        functools.partial(axis_kernel, 3), scalars, (adapt_keep, adapt_came, adapt_last), shapes, scratch
     )
     adapt_came = send(adapt_give, second_axis(3))
     (onward,) = call(next_kernel, scalars, (keep, came), [shaped(piece[1:], BF16)])
@@ -588,26 +594,15 @@
         next_kernel, scalars, (adapt_keep, adapt_came), [shaped(piece[1:], BF16)]
     )
     adapt_last = send(adapt_next, second_axis(1))
-    piece = (40, 1280)
+    piece = (2, 40, 1280)
     mine, given = call(
-        functools.partial(total_kernel, KEEP),
-        scalars,
-        (keep, came, last),
+        both_kernel,
+        scalars,
+        (keep, came, last, adapt_keep, adapt_came, adapt_last),
         [shaped(piece, F32), shaped(piece, BF16)],
-        [pltpu.VMEM((2, 40, 1280), F32)],
-    )
-    came = send(given, beside)
-    mine, adapt_last = lax.optimization_barrier((mine, adapt_last))
-    adapt_mine, adapt_given = call(
-        functools.partial(total_kernel, YL),
-        scalars,
-        (adapt_keep, adapt_came, adapt_last),
-        [shaped(piece, F32), shaped(piece, BF16)],
-        [pltpu.VMEM((2, 40, 1280), F32)],
-    )
-    adapt_came = send(adapt_given, beside)
-    came, adapt_mine = lax.optimization_barrier((came, adapt_mine))
-    return mine, came, adapt_mine, adapt_came
+        [pltpu.VMEM((2, *piece), F32)],
+    )
+    return mine, send(given, beside)
 
 
 def block_ids(order, positions, per_image):
@@ -701,16 +696,16 @@
     )
 
     came = send(given, swap_core)
-    adapt_keep_a, adapt_give_a, adapt_keep_b, adapt_give_b = call(
-        adapt_partial_kernel,
+    adapt_keep, adapt_give = call(
+        functools.partial(adapt_partial_kernel, 3),
         scalars,
         (student, grad_zeta, gamma, grad_pred),
-        [shaped((2, 8, 40, 640), BF16)] * 4,
+        [shaped((2, 8, 40, 1280), BF16)] * 2,
         [pltpu.VMEM((32, 40, 1280), F32)],
         24,
         4 * token_count * width * 640,
     )
-    came, adapt_keep_a = lax.optimization_barrier((came, adapt_keep_a))
+    came, adapt_keep = lax.optimization_barrier((came, adapt_keep))
     pair, pair_b = call(
         pair_kernel,
         scalars,
@@ -724,34 +719,28 @@
         scalars, (hidden_crossed, hidden_core, hand, handed, slope, block_out)
     )
     across, left = lax.optimization_barrier((across, left))
-    adapt_came_a = send(adapt_give_a, first_axis(1))
-    adapt_came_b = send(adapt_give_b, first_axis(3))
+    adapt_came = send(adapt_give, first_axis(3))
     (mine,) = call(half_kernel, scalars, (pair, across), [shaped((half, width), BF16)])
     other = send(mine, swap_core)
-    other, adapt_came_a, adapt_came_b = lax.optimization_barrier(
-        (other, adapt_came_a, adapt_came_b)
-    )
     keep_a, give_a, keep_b, give_b = student_partial(
         scalars, (left, slopes, weights), mine, other
     )
-    mine, came, adapt_mine, adapt_came = both_axes(
-        scalars,
-        (keep_a, give_a, keep_b, give_b),
-        (adapt_keep_a, adapt_came_a, adapt_keep_b, adapt_came_b),
-    )
-    piece, piece_b = call(
-        piece_kernel, scalars, (mine, came), [shaped((40, 1280), F32), shaped((40, 1280), BF16)]
-    )
+    mine, came = both_axes(scalars, keep_a, give_a, keep_b, give_b, adapt_keep, adapt_came)
+    piece, piece_b, grad_first, grad_second = call(
+        piece_kernel,
+        scalars,
+        (mine, came),
+        [
+            shaped((40, 1280), F32),
+            shaped((40, 1280), BF16),
+            shaped((1, 40, 640), F32),
+            shaped((20, 1, 1280), F32),
+        ],
+    )
+    grad_second = jnp.swapaxes(grad_second, 0, 1)
     out_high = send(piece_b, exchange_across)
     low_piece = send(piece, swap_core)
     out_low = send(out_high, swap_core)
-    piece, adapt_came = lax.optimization_barrier((piece, adapt_came))
-    grad_first, grad_second = call(
-        adapt_last_kernel,
-        scalars,
-        (adapt_mine, adapt_came),
-        [shaped((1, 40, 640), F32), shaped((1, 20, 1280), F32)],
-    )
     grad_in_sum, grad_out_sum = call(
         last_kernel,
         scalars,

time: 125 us -> 123 us (0.984)
  starting transfers between devices: 31.9 us -> 28.7 us
  waiting for transfers between devices: 52.7 us -> 54.5 us
    ppermute x25 -> x22, starting transfers between devices: 22.6 us -> 19.5 us  [send(): return lax.ppermute(value, ALL, route(move))]
    ppermute x25 -> x22, waiting for transfers between devices: 48.9 us -> 50.7 us  [send(): return lax.ppermute(value, ALL, route(move))]
    pallas_call x16 -> x14, Pallas kernels: 15.2 us -> 14.2 us  [call(): pl.pallas_call(kernel, out_shape=list(outputs), in_specs=[smem()] + vmem(...]
    unnamed x9 -> x8, local copies, waits for them, and re-layouts: 2.52 us -> 1.77 us
  transfers between devices with their start and end apart: 26 -> 23, of which waited for: 15 -> 16; matrix products, arithmetic and copies ran while one was open for 1% -> 0% of each run, Pallas kernels for 15% -> 17%
where the time goes in v2:
time: 123 us; the launch traced here: 121 us
  waiting for transfers between devices  54.5 us (44%)
  Pallas kernels  34.9 us (28%)
  starting transfers between devices  28.7 us (23%)
  local copies, waits for them, and re-layouts  1.87 us (2%)
    ppermute x22, waiting for transfers between devices, send(): return lax.ppermute(value, ALL, route(move))  50.7 us
    ppermute x22, starting transfers between devices, send(): return lax.ppermute(value, ALL, route(move))  19.5 us
    pallas_call x14, Pallas kernels, call(): pl.pallas_call(kernel, out_shape=list(outputs), in_specs=[smem()] + vmem(...  14.2 us
    pallas_call x1, Pallas kernels, block_forward(): pl.pallas_call(forward_kernel, out_shape=[pltpu.HBM((tokens, hidden), BF1...  11.2 us
    all_to_all x1, starting transfers between devices, body(): lax.all_to_all(outgoing, WIDE, split_axis=0, concat_axis=0, tiled=True)  9.27 us
    pallas_call x2, Pallas kernels, adapt_call(): pl.pallas_call(kernel, out_shape=list(outputs), in_specs=[smem()] + vmem(...  7.69 us
    all_to_all x1, waiting for transfers between devices, body(): lax.all_to_all(outgoing, WIDE, split_axis=0, concat_axis=0, tiled=True)  3.75 us
  transfers between devices with their start and end apart: 23, of which 16 were waited for; matrix products, arithmetic and copies ran while one was open for 0% of the time, Pallas kernels for 17%

profile of v2, /device:TPU:0, one launch (start us, length us, event | category | flops | bytes accessed | tf_op | source)
XLA Modules:
  0.0 121.2 jit_solution(12832889664602089915)
XLA Ops:
  0.7 11.2 %shard_map.93 = (bf16[256,2560]{1,0:T(8,128)(2,1)}, bf16[1792,1280]{1,0:T(8,128)(2,1)}, bf16[256,1280]{1,0:T(8,128)(2,1)}, bf16[256,1280]{1,0:T(8,128)(2,1)S(1)}, bf16[256,1280]{1,0:T(8,128)(2,1)}) custom-call(s32[8]{0:T(128)S(1)} %stack.35.at, bf16[1,256,1280]{2,1,0:T(8,128)(2,1)} %acts_hbm.1, bf16[1,1280,2560]{2,1,0:T(8,128)(2,1)} %first_hbm.3, ...), custom_call_target="tpu_custom_call" | custom-call | flops 3355443200 | bytes 16777216 | tf_op jit(solution)/shard_map/pallas_call | solution.py:199
  12.7 9.3 %all-to-all-start = ((bf16[32,8,1280]{2,1,0:T(8,128)(2,1)}), bf16[32,8,1280]{2,1,0:T(8,128)(2,1)S(1)}, u32[]{:S(2)}, u32[]{:S(2)}) async-start(bf16[32,8,1280]{2,1,0:T(8,128)(2,1)} %bitcast.10), calls=%async_computation | async-start | bytes 1310720 | tf_op jit(solution)/shard_map/all_to_all | solution.py:666
  22.0 1.8 %collective-permute-start.5 = (bf16[256,2560]{1,0:T(8,128)(2,1)}, bf16[256,2560]{1,0:T(8,128)(2,1)}, u32[]{:S(2)}, u32[]{:S(2)}) collective-permute-start(bf16[256,2560]{1,0:T(8,128)(2,1)} %get-tuple-element.69), channel_id=1, source_target_pairs={{96,36},{97,37},{98,38},{99,39},{100,32},{101,33},{102,34},{103,35... | collective-permute-start | bytes 3932168 | tf_op jit(solution)/shard_map/ppermute | solution.py:43
  24.4 1.3 %collective-permute-start.1 = (bf16[256,1280]{1,0:T(8,128)(2,1)S(1)}, bf16[256,1280]{1,0:T(8,128)(2,1)S(1)}, u32[]{:S(2)}, u32[]{:S(2)}) collective-permute-start(bf16[256,1280]{1,0:T(8,128)(2,1)S(1)} %shard_map.94.shared_ref), channel_id=1, source_target_pairs={{0,32},{1,33},{2,34},{3,35},{4,36},{5,37},{6,38},{7,39},{8,40},{9,... | collective-permute-start | bytes 1966088 | tf_op jit(solution)/shard_map/ppermute | solution.py:43
  25.9 1.5 %collective-permute-done.1.handed_ref = bf16[256,1280]{1,0:T(8,128)(2,1)S(1)} collective-permute-done((bf16[256,1280]{1,0:T(8,128)(2,1)S(1)}, bf16[256,1280]{1,0:T(8,128)(2,1)S(1)}, u32[]{:S(2)}, u32[]{:S(2)}) %collective-permute-start.1) | collective-permute-done | bytes 655392 | tf_op jit(solution)/shard_map/ppermute | solution.py:43
  27.4 3.7 %shard_map.95 = (bf16[256,1280]{1,0:T(8,128)(2,1)S(1)}, bf16[256,640]{1,0:T(8,128)(2,1)S(1)}, f32[256,1920]{1,0:T(8,128)S(1)}) custom-call(s32[8]{0:T(128)S(1)} %stack.35.at, bf16[256,1280]{1,0:T(8,128)(2,1)S(1)} %shard_map.94.shared_ref, bf16[256,1280]{1,0:T(8,128)(2,1)S(1)} %collective-permute-done.1.handed_ref, bf16[3,1280,640]{2,1,0:T(8,128)(2,1)} %first_hbm.5, ...), custom_call_target="tpu_custom_call" | custom-call | flops 1024 | bytes 1024 | tf_op jit(solution)/shard_map/pallas_call | solution.py:269
  31.9 3.8 %all-to-all-done = bf16[32,8,1280]{2,1,0:T(8,128)(2,1)S(1)} async-done(((bf16[32,8,1280]{2,1,0:T(8,128)(2,1)}), bf16[32,8,1280]{2,1,0:T(8,128)(2,1)S(1)}, u32[]{:S(2)}, u32[]{:S(2)}) %all-to-all-start) | async-done | bytes 655392 | tf_op jit(solution)/shard_map/all_to_all | solution.py:666
  35.7 3.9 %shard_map.96 = (bf16[256,1280]{1,0:T(8,128)(2,1)S(1)}, bf16[256,640]{1,0:T(8,128)(2,1)S(1)}, f32[128,1280]{1,0:T(8,128)S(1)}, bf16[128,1280]{1,0:T(8,128)(2,1)S(1)}) custom-call(s32[8]{0:T(128)S(1)} %stack.35.at, bf16[256,256]{1,0:T(8,128)(2,1)S(1)} %and_convert_fusion.sorter_ref, bf16[256,1280]{1,0:T(8,128)(2,1)S(1)} %bitcast.15, ...), custom_call_target="tpu_custom_call" | custom-call | flops 1024 | bytes 1024 | tf_op jit(solution)/shard_map/pallas_call | solution.py:269
  39.7 2.0 %shard_map.97 = (bf16[2,8,40,1280]{3,2,1,0:T(8,128)(2,1)S(1)}, bf16[2,8,40,1280]{3,2,1,0:T(8,128)(2,1)S(1)}) custom-call(s32[8]{0:T(128)S(1)} %stack.35.at, bf16[256,1280]{1,0:T(8,128)(2,1)S(1)} %get-tuple-element.61.student_ref, bf16[256,640]{1,0:T(8,128)(2,1)S(1)} %get-tuple-element.62.grad_zeta_ref, bf16[256,640]{1,0:T(8,128)(2,1)S(1)} %copy-done.1, ...), custom_call_target="tpu_custom_call" | custom-call | flops 838860800 | bytes 5242880 | tf_op jit(solution)/shard_map/pallas_call | solution.py:64
  43.0 2.4 %collective-permute-start.9 = (bf16[2,8,40,1280]{3,2,1,0:T(8,128)(2,1)S(1)}, bf16[2,8,40,1280]{3,2,1,0:T(8,128)(2,1)S(1)}, u32[]{:S(2)}, u32[]{:S(2)}) collective-permute-start(bf16[2,8,40,1280]{3,2,1,0:T(8,128)(2,1)S(1)} %get-tuple-element.82), channel_id=1, source_target_pairs={{0,3},{1,2},{2,1},{3,0},{4,7},{5,6},{6,5},{7,4},{8,11},{9,10},{10,... | collective-permute-start | bytes 4915208 | tf_op jit(solution)/shard_map/ppermute | solution.py:43
  45.4 1.5 %collective-permute-start.4 = (bf16[128,1280]{1,0:T(8,128)(2,1)S(1)}, bf16[128,1280]{1,0:T(8,128)(2,1)S(1)}, u32[]{:S(2)}, u32[]{:S(2)}) collective-permute-start(bf16[128,1280]{1,0:T(8,128)(2,1)S(1)} %get-tuple-element.67), channel_id=1, source_target_pairs={{0,68},{1,69},{2,70},{3,71},{4,64},{5,65},{6,66},{7,67},{8,76},{9,... | collective-permute-start | bytes 983048 | tf_op jit(solution)/shard_map/ppermute | solution.py:43
  47.9 1.9 %shard_map.99 = (bf16[256,2560]{1,0:T(8,128)(2,1)S(1)}, bf16[256,1280]{1,0:T(8,128)(2,1)S(1)}, bf16[1280,1280]{1,0:T(8,128)(2,1)S(1)}) custom-call(s32[8]{0:T(128)S(1)} %stack.35.at, bf16[256,2560]{1,0:T(8,128)(2,1)} %collective-permute-done.5.crossed_hbm, bf16[256,2560]{1,0:T(8,128)(2,1)} %copy-done.2, bf16[1792,1280]{1,0:T(8,128)(2,1)} %get-tuple-element.57.hand_hbm, ...), custom_call_target="tpu_custom_call" | custom-call | bytes 8388608 | tf_op jit(solution)/shard_map/pallas_call | solution.py:398
  49.8 6.1 %collective-permute-done.4.across_ref = bf16[128,1280]{1,0:T(8,128)(2,1)S(1)} collective-permute-done((bf16[128,1280]{1,0:T(8,128)(2,1)S(1)}, bf16[128,1280]{1,0:T(8,128)(2,1)S(1)}, u32[]{:S(2)}, u32[]{:S(2)}) %collective-permute-start.4) | collective-permute-done | bytes 327712 | tf_op jit(solution)/shard_map/ppermute | solution.py:43
  56.7 1.6 %collective-permute-done.7.other_ref = bf16[128,1280]{1,0:T(8,128)(2,1)S(1)} collective-permute-done((bf16[128,1280]{1,0:T(8,128)(2,1)S(1)}, bf16[128,1280]{1,0:T(8,128)(2,1)S(1)}, u32[]{:S(2)}, u32[]{:S(2)}) %collective-permute-start.7) | collective-permute-done | bytes 327712 | tf_op jit(solution)/shard_map/ppermute | solution.py:43
  58.3 2.1 %shard_map.101 = (bf16[2,8,40,640]{3,2,1,0:T(8,128)(2,1)S(1)}, bf16[2,8,40,640]{3,2,1,0:T(8,128)(2,1)S(1)}, bf16[2,8,40,640]{3,2,1,0:T(8,128)(2,1)S(1)}, bf16[2,8,40,640]{3,2,1,0:T(8,128)(2,1)S(1)}) custom-call(s32[8]{0:T(128)S(1)} %stack.35.at, bf16[256,2560]{1,0:T(8,128)(2,1)S(1)} %get-tuple-element.74.left, ...), custom_call_target="tpu_custom_call" | custom-call | flops 1677721600 | bytes 9175040 | tf_op jit(solution)/shard_map/pallas_call | solution.py:64
  60.4 1.5 %collective-permute-start.8 = (bf16[2,8,40,640]{3,2,1,0:T(8,128)(2,1)S(1)}, bf16[2,8,40,640]{3,2,1,0:T(8,128)(2,1)S(1)}, u32[]{:S(2)}, u32[]{:S(2)}) collective-permute-start(bf16[2,8,40,640]{3,2,1,0:T(8,128)(2,1)S(1)} %get-tuple-element.80), channel_id=1, source_target_pairs={{0,1},{1,0},{2,3},{3,2},{4,5},{5,4},{6,7},{7,6},{8,9},{9,8},{10,11... | collective-permute-start | bytes 2457608 | tf_op jit(solution)/shard_map/ppermute | solution.py:43
  62.5 2.8 %collective-permute-done.9.came_ref = bf16[2,8,40,1280]{3,2,1,0:T(8,128)(2,1)S(1)} collective-permute-done((bf16[2,8,40,1280]{3,2,1,0:T(8,128)(2,1)S(1)}, bf16[2,8,40,1280]{3,2,1,0:T(8,128)(2,1)S(1)}, u32[]{:S(2)}, u32[]{:S(2)}) %collective-permute-start.9) | collective-permute-done | bytes 1638432 | tf_op jit(solution)/shard_map/ppermute | solution.py:43
  66.1 6.7 %collective-permute-done.8.came_a = bf16[2,8,40,640]{3,2,1,0:T(8,128)(2,1)S(1)} collective-permute-done((bf16[2,8,40,640]{3,2,1,0:T(8,128)(2,1)S(1)}, bf16[2,8,40,640]{3,2,1,0:T(8,128)(2,1)S(1)}, u32[]{:S(2)}, u32[]{:S(2)}) %collective-permute-start.8) | collective-permute-done | bytes 819232 | tf_op jit(solution)/shard_map/ppermute | solution.py:43
  72.8 2.6 %collective-permute-done.10.came_b = bf16[2,8,40,640]{3,2,1,0:T(8,128)(2,1)S(1)} collective-permute-done((bf16[2,8,40,640]{3,2,1,0:T(8,128)(2,1)S(1)}, bf16[2,8,40,640]{3,2,1,0:T(8,128)(2,1)S(1)}, u32[]{:S(2)}, u32[]{:S(2)}) %collective-permute-start.10) | collective-permute-done | bytes 819232 | tf_op jit(solution)/shard_map/ppermute | solution.py:43
  77.3 8.1 %collective-permute-done.11.last_a = bf16[8,40,640]{2,1,0:T(8,128)(2,1)S(1)} collective-permute-done((bf16[8,40,640]{2,1,0:T(8,128)(2,1)S(1)}, bf16[8,40,640]{2,1,0:T(8,128)(2,1)S(1)}, u32[]{:S(2)}, u32[]{:S(2)}) %collective-permute-start.11) | collective-permute-done | bytes 409632 | tf_op jit(solution)/shard_map/ppermute | solution.py:43
  87.9 1.2 shard_map.106
  89.0 2.2 %collective-permute-start.16 = (bf16[2,2,40,1280]{3,2,1,0:T(8,128)(2,1)S(1)}, bf16[2,2,40,1280]{3,2,1,0:T(8,128)(2,1)S(1)}, u32[]{:S(2)}, u32[]{:S(2)}) collective-permute-start(bf16[2,2,40,1280]{3,2,1,0:T(8,128)(2,1)S(1)} %get-tuple-element.94), channel_id=1, source_target_pairs={{0,24},{1,25},{2,26},{3,27},{4,28},{5,29},{6,30},{7,31},{8,16},{9,... | collective-permute-start | bytes 1228808 | tf_op jit(solution)/shard_map/ppermute | solution.py:43
  91.2 3.9 %collective-permute-done.14.came_ref.came = bf16[2,2,40,1280]{3,2,1,0:T(8,128)(2,1)S(1)} collective-permute-done((bf16[2,2,40,1280]{3,2,1,0:T(8,128)(2,1)S(1)}, bf16[2,2,40,1280]{3,2,1,0:T(8,128)(2,1)S(1)}, u32[]{:S(2)}, u32[]{:S(2)}) %collective-permute-start.14) | collective-permute-done | bytes 409632 | tf_op jit(solution)/shard_map/ppermute | solution.py:43
  95.7 2.1 %collective-permute-start.15 = (bf16[2,40,1280]{2,1,0:T(8,128)(2,1)S(1)}, bf16[2,40,1280]{2,1,0:T(8,128)(2,1)S(1)}, u32[]{:S(2)}, u32[]{:S(2)}) collective-permute-start(bf16[2,40,1280]{2,1,0:T(8,128)(2,1)S(1)} %shard_map.105), channel_id=1, source_target_pairs={{0,24},{1,25},{2,26},{3,27},{4,28},{5,29},{6,30},{7,31},{8,16},{9,... | collective-permute-start | bytes 614408 | tf_op jit(solution)/shard_map/ppermute | solution.py:43
  99.0 3.7 %collective-permute-done.15.last = bf16[2,40,1280]{2,1,0:T(8,128)(2,1)S(1)} collective-permute-done((bf16[2,40,1280]{2,1,0:T(8,128)(2,1)S(1)}, bf16[2,40,1280]{2,1,0:T(8,128)(2,1)S(1)}, u32[]{:S(2)}, u32[]{:S(2)}) %collective-permute-start.15) | collective-permute-done | bytes 204832 | tf_op jit(solution)/shard_map/ppermute | solution.py:43
  102.7 2.0 %collective-permute-done.17.adapt_last = bf16[2,40,1280]{2,1,0:T(8,128)(2,1)S(1)} collective-permute-done((bf16[2,40,1280]{2,1,0:T(8,128)(2,1)S(1)}, bf16[2,40,1280]{2,1,0:T(8,128)(2,1)S(1)}, u32[]{:S(2)}, u32[]{:S(2)}) %collective-permute-start.17) | collective-permute-done | bytes 204832 | tf_op jit(solution)/shard_map/ppermute | solution.py:43
  105.8 5.5 %collective-permute-done.18.beside_ref = bf16[2,40,1280]{2,1,0:T(8,128)(2,1)S(1)} collective-permute-done((bf16[2,40,1280]{2,1,0:T(8,128)(2,1)S(1)}, bf16[2,40,1280]{2,1,0:T(8,128)(2,1)S(1)}, u32[]{:S(2)}, u32[]{:S(2)}) %collective-permute-start.18) | collective-permute-done | bytes 204832 | tf_op jit(solution)/shard_map/ppermute | solution.py:43
  111.3 1.2 %shard_map.109 = (f32[40,1280]{1,0:T(8,128)S(1)}, bf16[40,1280]{1,0:T(8,128)(2,1)S(1)}, f32[1,40,640]{2,1,0:T(8,128)}, f32[20,1,1280]{2,1,0:T(1,128)}) custom-call(s32[8]{0:T(128)S(1)} %stack.35.at, f32[2,40,1280]{2,1,0:T(8,128)S(1)} %get-tuple-element.96.mine_ref, bf16[2,40,1280]{2,1,0:T(8,128)(2,1)S(1)} %collective-permute-done.18.beside_ref), custom_call_target="tpu_custom_call" | custom-call | bytes 1126400 | tf_op jit(solution)/shard_map/pallas_call | solution.py:64
  112.5 2.0 %collective-permute-start.20 = (bf16[40,1280]{1,0:T(8,128)(2,1)S(1)}, bf16[40,1280]{1,0:T(8,128)(2,1)S(1)}, u32[]{:S(2)}, u32[]{:S(2)}) collective-permute-start(bf16[40,1280]{1,0:T(8,128)(2,1)S(1)} %get-tuple-element.101), channel_id=1, source_target_pairs={{0,68},{1,69},{2,70},{3,71},{4,64},{5,65},{6,66},{7,67},{8,76},{9,... | collective-permute-start | bytes 307208 | tf_op jit(solution)/shard_map/ppermute | solution.py:43
  114.6 3.8 %collective-permute-done.20.out_high_ref = bf16[40,1280]{1,0:T(8,128)(2,1)S(1)} collective-permute-done((bf16[40,1280]{1,0:T(8,128)(2,1)S(1)}, bf16[40,1280]{1,0:T(8,128)(2,1)S(1)}, u32[]{:S(2)}, u32[]{:S(2)}) %collective-permute-start.20) | collective-permute-done | bytes 102432 | tf_op jit(solution)/shard_map/ppermute | solution.py:43
  118.4 1.3 %collective-permute-done.21.out_low_ref = bf16[40,1280]{1,0:T(8,128)(2,1)S(1)} collective-permute-done((bf16[40,1280]{1,0:T(8,128)(2,1)S(1)}, bf16[40,1280]{1,0:T(8,128)(2,1)S(1)}, u32[]{:S(2)}, u32[]{:S(2)}) %collective-permute-start.21) | collective-permute-done | bytes 102432 | tf_op jit(solution)/shard_map/ppermute | solution.py:43
  119.7 1.5 %shard_map.110 = (f32[1,40,2560]{2,1,0:T(8,128)}, f32[1,80,1280]{2,1,0:T(8,128)}) custom-call(s32[8]{0:T(128)S(1)} %stack.35.at, f32[40,1280]{1,0:T(8,128)S(1)} %get-tuple-element.100.high_ref, f32[40,1280]{1,0:T(8,128)S(1)} %collective-permute-done.19.low_ref, bf16[40,1280]{1,0:T(8,128)(2,1)S(1)} %collective-permute-done.21.out_low_ref, ...), custom_call_target="tpu_custom_call" | custom-call | bytes 1433600 | tf_op jit(solution)/shard_map/pallas_call | solution.py:64
  (47 shorter events, 14.1 us)
Async XLA Ops:
  0.7 23.0 %copy-start.3 = (s32[4,8]{1,0:T(4,128)S(1)}, s32[4,8]{1,0:T(4,128)}, u32[]{:S(2)}) copy-start(s32[4,8]{1,0:T(4,128)} %param.11) | copy-start | bytes 388
  11.9 20.0 %collective-permute-start.2 = (bf16[1792,1280]{1,0:T(8,128)(2,1)}, bf16[1792,1280]{1,0:T(8,128)(2,1)}, u32[]{:S(2)}, u32[]{:S(2)}) collective-permute-start(bf16[1792,1280]{1,0:T(8,128)(2,1)} %get-tuple-element.57.hand_hbm), channel_id=1, source_target_pairs={{0,32},{1,33},{2,34},{3,35},{4,36},{5,37},{6,38},{7,39},{8,40},{9,... | collective-permute-start | bytes 13762568 | tf_op jit(solution)/shard_map/ppermute | solution.py:43
  12.0 11.8 %collective-permute-start = (bf16[256,1280]{1,0:T(8,128)(2,1)S(1)}, bf16[256,1280]{1,0:T(8,128)(2,1)S(1)}, u32[]{:S(2)}, u32[]{:S(2)}) collective-permute-start(bf16[256,1280]{1,0:T(8,128)(2,1)S(1)} %get-tuple-element.55.own_ref), channel_id=1, source_target_pairs={{96,36},{97,37},{98,38},{99,39},{100,32},{101,33},{102,34},{103,35... | collective-permute-start | bytes 1966088 | tf_op jit(solution)/shard_map/ppermute | solution.py:43
  12.7 23.0 %all-to-all-start = ((bf16[32,8,1280]{2,1,0:T(8,128)(2,1)}), bf16[32,8,1280]{2,1,0:T(8,128)(2,1)S(1)}, u32[]{:S(2)}, u32[]{:S(2)}) async-start(bf16[32,8,1280]{2,1,0:T(8,128)(2,1)} %bitcast.10), calls=%async_computation | async-start | bytes 1310720 | tf_op jit(solution)/shard_map/all_to_all | solution.py:666
  22.0 20.4 %collective-permute-start.5 = (bf16[256,2560]{1,0:T(8,128)(2,1)}, bf16[256,2560]{1,0:T(8,128)(2,1)}, u32[]{:S(2)}, u32[]{:S(2)}) collective-permute-start(bf16[256,2560]{1,0:T(8,128)(2,1)} %get-tuple-element.69), channel_id=1, source_target_pairs={{96,36},{97,37},{98,38},{99,39},{100,32},{101,33},{102,34},{103,35... | collective-permute-start | bytes 3932168 | tf_op jit(solution)/shard_map/ppermute | solution.py:43
  24.4 3.0 %collective-permute-start.1 = (bf16[256,1280]{1,0:T(8,128)(2,1)S(1)}, bf16[256,1280]{1,0:T(8,128)(2,1)S(1)}, u32[]{:S(2)}, u32[]{:S(2)}) collective-permute-start(bf16[256,1280]{1,0:T(8,128)(2,1)S(1)} %shard_map.94.shared_ref), channel_id=1, source_target_pairs={{0,32},{1,33},{2,34},{3,35},{4,36},{5,37},{6,38},{7,39},{8,40},{9,... | collective-permute-start | bytes 1966088 | tf_op jit(solution)/shard_map/ppermute | solution.py:43
  31.2 0.7 copy-start
  35.7 4.0 %copy-start.1 = (bf16[256,640]{1,0:T(8,128)(2,1)S(1)}, bf16[256,640]{1,0:T(8,128)(2,1)}, u32[]{:S(2)}) copy-start(bf16[256,640]{1,0:T(8,128)(2,1)} %copy-done) | copy-start | bytes 983044
  39.6 2.1 %collective-permute-start.3 = (bf16[128,1280]{1,0:T(8,128)(2,1)S(1)}, bf16[128,1280]{1,0:T(8,128)(2,1)S(1)}, u32[]{:S(2)}, u32[]{:S(2)}) collective-permute-start(bf16[128,1280]{1,0:T(8,128)(2,1)S(1)} %get-tuple-element.60), channel_id=1, source_target_pairs={{0,32},{1,33},{2,34},{3,35},{4,36},{5,37},{6,38},{7,39},{8,40},{9,... | collective-permute-start | bytes 983048 | tf_op jit(solution)/shard_map/ppermute | solution.py:43
  42.4 4.5 %collective-permute-start.6 = (bf16[256,2560]{1,0:T(8,128)(2,1)}, bf16[256,2560]{1,0:T(8,128)(2,1)S(1)}, u32[]{:S(2)}, u32[]{:S(2)}) collective-permute-start(bf16[256,2560]{1,0:T(8,128)(2,1)} %collective-permute-done.5.crossed_hbm), channel_id=1, source_target_pairs={{0,32},{1,33},{2,34},{3,35},{4,36},{5,37},{6,38},{7,39},{8,40},{9,... | collective-permute-start | bytes 3932168 | tf_op jit(solution)/shard_map/ppermute | solution.py:43
  43.0 22.3 %collective-permute-start.9 = (bf16[2,8,40,1280]{3,2,1,0:T(8,128)(2,1)S(1)}, bf16[2,8,40,1280]{3,2,1,0:T(8,128)(2,1)S(1)}, u32[]{:S(2)}, u32[]{:S(2)}) collective-permute-start(bf16[2,8,40,1280]{3,2,1,0:T(8,128)(2,1)S(1)} %get-tuple-element.82), channel_id=1, source_target_pairs={{0,3},{1,2},{2,1},{3,0},{4,7},{5,6},{6,5},{7,4},{8,11},{9,10},{10,... | collective-permute-start | bytes 4915208 | tf_op jit(solution)/shard_map/ppermute | solution.py:43
  45.4 10.6 %collective-permute-start.4 = (bf16[128,1280]{1,0:T(8,128)(2,1)S(1)}, bf16[128,1280]{1,0:T(8,128)(2,1)S(1)}, u32[]{:S(2)}, u32[]{:S(2)}) collective-permute-start(bf16[128,1280]{1,0:T(8,128)(2,1)S(1)} %get-tuple-element.67), channel_id=1, source_target_pairs={{0,68},{1,69},{2,70},{3,71},{4,64},{5,65},{6,66},{7,67},{8,76},{9,... | collective-permute-start | bytes 983048 | tf_op jit(solution)/shard_map/ppermute | solution.py:43
  46.9 1.0 copy-start.2
  56.6 1.7 %collective-permute-start.7 = (bf16[128,1280]{1,0:T(8,128)(2,1)S(1)}, bf16[128,1280]{1,0:T(8,128)(2,1)S(1)}, u32[]{:S(2)}, u32[]{:S(2)}) collective-permute-start(bf16[128,1280]{1,0:T(8,128)(2,1)S(1)} %shard_map.100.mine_ref), channel_id=1, source_target_pairs={{0,32},{1,33},{2,34},{3,35},{4,36},{5,37},{6,38},{7,39},{8,40},{9,... | collective-permute-start | bytes 983048 | tf_op jit(solution)/shard_map/ppermute | solution.py:43
  60.4 12.4 %collective-permute-start.8 = (bf16[2,8,40,640]{3,2,1,0:T(8,128)(2,1)S(1)}, bf16[2,8,40,640]{3,2,1,0:T(8,128)(2,1)S(1)}, u32[]{:S(2)}, u32[]{:S(2)}) collective-permute-start(bf16[2,8,40,640]{3,2,1,0:T(8,128)(2,1)S(1)} %get-tuple-element.80), channel_id=1, source_target_pairs={{0,1},{1,0},{2,3},{3,2},{4,5},{5,4},{6,7},{7,6},{8,9},{9,8},{10,11... | collective-permute-start | bytes 2457608 | tf_op jit(solution)/shard_map/ppermute | solution.py:43
  61.9 13.6 %collective-permute-start.10 = (bf16[2,8,40,640]{3,2,1,0:T(8,128)(2,1)S(1)}, bf16[2,8,40,640]{3,2,1,0:T(8,128)(2,1)S(1)}, u32[]{:S(2)}, u32[]{:S(2)}) collective-permute-start(bf16[2,8,40,640]{3,2,1,0:T(8,128)(2,1)S(1)} %get-tuple-element.84), channel_id=1, source_target_pairs={{0,3},{1,2},{2,1},{3,0},{4,7},{5,6},{6,5},{7,4},{8,11},{9,10},{10,... | collective-permute-start | bytes 2457608 | tf_op jit(solution)/shard_map/ppermute | solution.py:43
  66.0 21.8 %collective-permute-start.13 = (bf16[8,40,1280]{2,1,0:T(8,128)(2,1)S(1)}, bf16[8,40,1280]{2,1,0:T(8,128)(2,1)S(1)}, u32[]{:S(2)}, u32[]{:S(2)}) collective-permute-start(bf16[8,40,1280]{2,1,0:T(8,128)(2,1)S(1)} %shard_map.104), channel_id=1, source_target_pairs={{0,1},{1,0},{2,3},{3,2},{4,5},{5,4},{6,7},{7,6},{8,9},{9,8},{10,11... | collective-permute-start | bytes 2457608 | tf_op jit(solution)/shard_map/ppermute | solution.py:43
  76.2 9.2 %collective-permute-start.11 = (bf16[8,40,640]{2,1,0:T(8,128)(2,1)S(1)}, bf16[8,40,640]{2,1,0:T(8,128)(2,1)S(1)}, u32[]{:S(2)}, u32[]{:S(2)}) collective-permute-start(bf16[8,40,640]{2,1,0:T(8,128)(2,1)S(1)} %get-tuple-element.85), channel_id=1, source_target_pairs={{0,3},{1,2},{2,1},{3,0},{4,7},{5,6},{6,5},{7,4},{8,11},{9,10},{10,... | collective-permute-start | bytes 1228808 | tf_op jit(solution)/shard_map/ppermute | solution.py:43
  77.3 8.7 %collective-permute-start.12 = (bf16[8,40,640]{2,1,0:T(8,128)(2,1)S(1)}, bf16[8,40,640]{2,1,0:T(8,128)(2,1)S(1)}, u32[]{:S(2)}, u32[]{:S(2)}) collective-permute-start(bf16[8,40,640]{2,1,0:T(8,128)(2,1)S(1)} %get-tuple-element.86), channel_id=1, source_target_pairs={{0,1},{1,0},{2,3},{3,2},{4,5},{5,4},{6,7},{7,6},{8,9},{9,8},{10,11... | collective-permute-start | bytes 1228808 | tf_op jit(solution)/shard_map/ppermute | solution.py:43
  87.0 8.0 %collective-permute-start.14 = (bf16[2,2,40,1280]{3,2,1,0:T(8,128)(2,1)S(1)}, bf16[2,2,40,1280]{3,2,1,0:T(8,128)(2,1)S(1)}, u32[]{:S(2)}, u32[]{:S(2)}) collective-permute-start(bf16[2,2,40,1280]{3,2,1,0:T(8,128)(2,1)S(1)} %get-tuple-element.91), channel_id=1, source_target_pairs={{0,8},{1,9},{2,10},{3,11},{4,12},{5,13},{6,14},{7,15},{8,0},{9,1},... | collective-permute-start | bytes 1228808 | tf_op jit(solution)/shard_map/ppermute | solution.py:43
  89.0 9.2 %collective-permute-start.16 = (bf16[2,2,40,1280]{3,2,1,0:T(8,128)(2,1)S(1)}, bf16[2,2,40,1280]{3,2,1,0:T(8,128)(2,1)S(1)}, u32[]{:S(2)}, u32[]{:S(2)}) collective-permute-start(bf16[2,2,40,1280]{3,2,1,0:T(8,128)(2,1)S(1)} %get-tuple-element.94), channel_id=1, source_target_pairs={{0,24},{1,25},{2,26},{3,27},{4,28},{5,29},{6,30},{7,31},{8,16},{9,... | collective-permute-start | bytes 1228808 | tf_op jit(solution)/shard_map/ppermute | solution.py:43
  95.7 7.0 %collective-permute-start.15 = (bf16[2,40,1280]{2,1,0:T(8,128)(2,1)S(1)}, bf16[2,40,1280]{2,1,0:T(8,128)(2,1)S(1)}, u32[]{:S(2)}, u32[]{:S(2)}) collective-permute-start(bf16[2,40,1280]{2,1,0:T(8,128)(2,1)S(1)} %shard_map.105), channel_id=1, source_target_pairs={{0,24},{1,25},{2,26},{3,27},{4,28},{5,29},{6,30},{7,31},{8,16},{9,... | collective-permute-start | bytes 614408 | tf_op jit(solution)/shard_map/ppermute | solution.py:43
  98.8 5.8 %collective-permute-start.17 = (bf16[2,40,1280]{2,1,0:T(8,128)(2,1)S(1)}, bf16[2,40,1280]{2,1,0:T(8,128)(2,1)S(1)}, u32[]{:S(2)}, u32[]{:S(2)}) collective-permute-start(bf16[2,40,1280]{2,1,0:T(8,128)(2,1)S(1)} %shard_map.107), channel_id=1, source_target_pairs={{0,8},{1,9},{2,10},{3,11},{4,12},{5,13},{6,14},{7,15},{8,0},{9,1},... | collective-permute-start | bytes 614408 | tf_op jit(solution)/shard_map/ppermute | solution.py:43
  105.4 5.8 %collective-permute-start.18 = (bf16[2,40,1280]{2,1,0:T(8,128)(2,1)S(1)}, bf16[2,40,1280]{2,1,0:T(8,128)(2,1)S(1)}, u32[]{:S(2)}, u32[]{:S(2)}) collective-permute-start(bf16[2,40,1280]{2,1,0:T(8,128)(2,1)S(1)} %get-tuple-element.97), channel_id=1, source_target_pairs={{0,4},{1,5},{2,6},{3,7},{4,0},{5,1},{6,2},{7,3},{8,12},{9,13},{10,... | collective-permute-start | bytes 614408 | tf_op jit(solution)/shard_map/ppermute | solution.py:43
  112.5 5.9 %collective-permute-start.20 = (bf16[40,1280]{1,0:T(8,128)(2,1)S(1)}, bf16[40,1280]{1,0:T(8,128)(2,1)S(1)}, u32[]{:S(2)}, u32[]{:S(2)}) collective-permute-start(bf16[40,1280]{1,0:T(8,128)(2,1)S(1)} %get-tuple-element.101), channel_id=1, source_target_pairs={{0,68},{1,69},{2,70},{3,71},{4,64},{5,65},{6,66},{7,67},{8,76},{9,... | collective-permute-start | bytes 307208 | tf_op jit(solution)/shard_map/ppermute | solution.py:43
  114.6 5.1 %collective-permute-start.19 = (f32[40,1280]{1,0:T(8,128)S(1)}, f32[40,1280]{1,0:T(8,128)S(1)}, u32[]{:S(2)}, u32[]{:S(2)}) collective-permute-start(f32[40,1280]{1,0:T(8,128)S(1)} %get-tuple-element.100.high_ref), channel_id=1, source_target_pairs={{0,32},{1,33},{2,34},{3,35},{4,36},{5,37},{6,38},{7,39},{8,40},{9,... | collective-permute-start | bytes 614408 | tf_op jit(solution)/shard_map/ppermute | solution.py:43
  118.4 1.3 %collective-permute-start.21 = (bf16[40,1280]{1,0:T(8,128)(2,1)S(1)}, bf16[40,1280]{1,0:T(8,128)(2,1)S(1)}, u32[]{:S(2)}, u32[]{:S(2)}) collective-permute-start(bf16[40,1280]{1,0:T(8,128)(2,1)S(1)} %collective-permute-done.20.out_high_ref), channel_id=1, source_target_pairs={{0,32},{1,33},{2,34},{3,35},{4,36},{5,37},{6,38},{7,39},{8,40},{9,... | collective-permute-start | bytes 307208 | tf_op jit(solution)/shard_map/ppermute | solution.py:43

commit v3 on v2

--- a/solution.py
+++ b/solution.py
@@ -25,7 +25,7 @@
 
 
 F32 = jnp.float32
-CORE, FLIP, GROUP_AT, CHOSEN, YL, KEEP, FIRST, SECOND = range(8)
+CORE, FLIP, GROUP_AT, CHOSEN, YL, FIRST, SECOND = range(7)
 
 
 def route(move):
@@ -507,19 +507,27 @@
 
 
 def both_kernel(
-    at, keep, came, last, adapt_keep, adapt_came, adapt_last, mine_ref, given_ref, total
+    at, keep, came, last, adapt_keep, adapt_came, adapt_last, mine_ref, given_ref, near_ref, far_ref,
+    total,
 ):
     total[0] = keep[0] + came[0].astype(F32) + last[...].astype(F32)
     total[1] = adapt_keep[0] + adapt_came[0].astype(F32) + adapt_last[...].astype(F32)
-    for slot, own in ((0, at[KEEP]), (1, at[YL])):
-        mine_ref[slot] = total[slot, own]
-        given_ref[slot] = total[slot, 1 - own].astype(BF16)
-
-
-def piece_kernel(at, mine_ref, beside_ref, piece_ref, sent_ref, first_ref, second_ref):
+    for slot in range(2):
+        mine_ref[slot] = total[slot, at[YL]]
+        given_ref[slot] = total[slot, 1 - at[YL]].astype(BF16)
+    near_ref[...] = total[0, 1 - at[YL]].astype(BF16)
+    far_ref[...] = total[0, at[YL]].astype(BF16)
+
+
+def piece_kernel(
+    at, mine_ref, beside_ref, near_ref, far_ref, piece_ref, sent_ref, first_ref, second_ref
+):
     piece = mine_ref[0] + beside_ref[0].astype(F32)
-    piece_ref[...] = piece
-    sent_ref[...] = piece.astype(BF16)
+    piece_ref[0] = piece
+    sent_ref[0] = piece.astype(BF16)
+    piece = near_ref[...].astype(F32) + far_ref[...].astype(F32)
+    piece_ref[1] = piece
+    sent_ref[1] = piece.astype(BF16)
     total = mine_ref[1] + beside_ref[1].astype(F32)
     total = jnp.where(at[GROUP_AT] < 3, total, 0.0)
     first_ref[0] = total[:, :640]
@@ -527,14 +535,13 @@
     second_ref[:, 0, 640:] = total[20:, 640:]
 
 
-def last_kernel(at, high_ref, low_ref, out_low_ref, out_high_ref, in_ref, out_ref):
+def last_kernel(at, high_ref, low_ref, in_ref, out_ref):
     student = at[GROUP_AT] == 3
-    in_ref[0, :, :1280] = jnp.where(student, low_ref[...], 0.0)
-    in_ref[0, :, 1280:] = jnp.where(student, high_ref[...], 0.0)
-    for start, ref in ((0, out_low_ref), (640, out_high_ref)):
+    for part, ref in enumerate((low_ref, high_ref)):
         total = jnp.where(student, ref[...].astype(F32), 0.0)
-        out_ref[0, :40, start : start + 640] = total[:, :640]
-        out_ref[0, 40:, start : start + 640] = total[:, 640:]
+        in_ref[0, :, part * 1280 : part * 1280 + 1280] = total[0]
+        out_ref[0, :40, part * 640 : part * 640 + 640] = total[1, :, :640]
+        out_ref[0, 40:, part * 640 : part * 640 + 640] = total[1, :, 640:]
 
 
 def first_axis(mask):
@@ -595,14 +602,14 @@
     )
     adapt_last = send(adapt_next, second_axis(1))
     piece = (2, 40, 1280)
-    mine, given = call(
+    mine, given, near, far = call(
         both_kernel,
         scalars,
         (keep, came, last, adapt_keep, adapt_came, adapt_last),
-        [shaped(piece, F32), shaped(piece, BF16)],
+        [shaped(piece, F32), shaped(piece, BF16)] + [shaped(piece[1:], BF16)] * 2,
         [pltpu.VMEM((2, *piece), F32)],
     )
-    return mine, send(given, beside)
+    return mine, send(given, beside), send(near, exchange_across), send(far, exchange_far)
 
 
 def block_ids(order, positions, per_image):
@@ -620,6 +627,10 @@
 def out_across(yh, core, z, yl, x):
     if yh == 1 and core == 1:
         return (0, core, z, 1 - yl, x)
+
+
+def exchange_far(yh, core, z, yl, x):
+    return (1 - yh, core, z, yl, x)
 
 
 def exchange_across(yh, core, z, yl, x):
@@ -644,7 +655,6 @@
             group_index,
             jnp.minimum(group_index, 2),
             yl,
-            jnp.where(lax.axis_index("yh") == 0, 1 - yl, yl),
             jnp.where(core == 0, x, z),
             jnp.where(core == 0, z, x),
         ]
@@ -725,26 +735,23 @@
     keep_a, give_a, keep_b, give_b = student_partial(
         scalars, (left, slopes, weights), mine, other
     )
-    mine, came = both_axes(scalars, keep_a, give_a, keep_b, give_b, adapt_keep, adapt_came)
+    parts = both_axes(scalars, keep_a, give_a, keep_b, give_b, adapt_keep, adapt_came)
     piece, piece_b, grad_first, grad_second = call(
         piece_kernel,
         scalars,
-        (mine, came),
+        parts,
         [
-            shaped((40, 1280), F32),
-            shaped((40, 1280), BF16),
+            shaped((2, 40, 1280), F32),
+            shaped((2, 40, 1280), BF16),
             shaped((1, 40, 640), F32),
             shaped((20, 1, 1280), F32),
         ],
     )
     grad_second = jnp.swapaxes(grad_second, 0, 1)
-    out_high = send(piece_b, exchange_across)
-    low_piece = send(piece, swap_core)
-    out_low = send(out_high, swap_core)
     grad_in_sum, grad_out_sum = call(
         last_kernel,
         scalars,
-        (piece, low_piece, out_low, out_high),
+        (piece, send(piece_b, swap_core)),
         [shaped((1, 40, 2560), F32), shaped((1, 80, 1280), F32)],
     )
     return (grad_first, grad_second, grad_in_sum, grad_out_sum)

time: 123 us -> 119 us (0.967)
  waiting for transfers between devices: 54.5 us -> 49.5 us
  starting transfers between devices: 28.7 us -> 30.6 us
    ppermute x22, waiting for transfers between devices: 50.7 us -> 45.8 us  [send(): return lax.ppermute(value, ALL, route(move))]
    ppermute x22, starting transfers between devices: 19.5 us -> 21.3 us  [send(): return lax.ppermute(value, ALL, route(move))]
where the time goes in v3:
time: 119 us; the launch traced here: 118 us
  waiting for transfers between devices  49.5 us (42%)
  Pallas kernels  34.9 us (29%)
  starting transfers between devices  30.6 us (26%)
  local copies, waits for them, and re-layouts  1.87 us (2%)
    ppermute x22, waiting for transfers between devices, send(): return lax.ppermute(value, ALL, route(move))  45.8 us
    ppermute x22, starting transfers between devices, send(): return lax.ppermute(value, ALL, route(move))  21.3 us
    pallas_call x14, Pallas kernels, call(): pl.pallas_call(kernel, out_shape=list(outputs), in_specs=[smem()] + vmem(...  14.2 us
    pallas_call x1, Pallas kernels, block_forward(): pl.pallas_call(forward_kernel, out_shape=[pltpu.HBM((tokens, hidden), BF1...  11.1 us
    all_to_all x1, starting transfers between devices, body(): lax.all_to_all(outgoing, WIDE, split_axis=0, concat_axis=0, tiled=True)  9.27 us
    pallas_call x2, Pallas kernels, adapt_call(): pl.pallas_call(kernel, out_shape=list(outputs), in_specs=[smem()] + vmem(...  7.69 us
    all_to_all x1, waiting for transfers between devices, body(): lax.all_to_all(outgoing, WIDE, split_axis=0, concat_axis=0, tiled=True)  3.75 us
  transfers between devices with their start and end apart: 23, of which 16 were waited for; matrix products, arithmetic and copies ran while one was open for 0% of the time, Pallas kernels for 17%

profile of v3, /device:TPU:0, one launch (start us, length us, event | category | flops | bytes accessed | tf_op | source)
XLA Modules:
  0.0 118.0 jit_solution(5445643776333183512)
XLA Ops:
  0.7 11.1 %shard_map.93 = (bf16[256,2560]{1,0:T(8,128)(2,1)}, bf16[1792,1280]{1,0:T(8,128)(2,1)}, bf16[256,1280]{1,0:T(8,128)(2,1)}, bf16[256,1280]{1,0:T(8,128)(2,1)S(1)}, bf16[256,1280]{1,0:T(8,128)(2,1)}) custom-call(s32[7]{0:T(128)S(1)} %stack.31.at, bf16[1,256,1280]{2,1,0:T(8,128)(2,1)} %acts_hbm.1, bf16[1,1280,2560]{2,1,0:T(8,128)(2,1)} %first_hbm.3, ...), custom_call_target="tpu_custom_call" | custom-call | flops 3355443200 | bytes 16777216 | tf_op jit(solution)/shard_map/pallas_call | solution.py:199
  12.7 9.3 %all-to-all-start = ((bf16[32,8,1280]{2,1,0:T(8,128)(2,1)}), bf16[32,8,1280]{2,1,0:T(8,128)(2,1)S(1)}, u32[]{:S(2)}, u32[]{:S(2)}) async-start(bf16[32,8,1280]{2,1,0:T(8,128)(2,1)} %bitcast.9), calls=%async_computation | async-start | bytes 1310720 | tf_op jit(solution)/shard_map/all_to_all | solution.py:676
  22.0 1.8 %collective-permute-start.5 = (bf16[256,2560]{1,0:T(8,128)(2,1)}, bf16[256,2560]{1,0:T(8,128)(2,1)}, u32[]{:S(2)}, u32[]{:S(2)}) collective-permute-start(bf16[256,2560]{1,0:T(8,128)(2,1)} %get-tuple-element.71), channel_id=1, source_target_pairs={{96,36},{97,37},{98,38},{99,39},{100,32},{101,33},{102,34},{103,35... | collective-permute-start | bytes 3932168 | tf_op jit(solution)/shard_map/ppermute | solution.py:43
  24.4 1.3 %collective-permute-start.1 = (bf16[256,1280]{1,0:T(8,128)(2,1)S(1)}, bf16[256,1280]{1,0:T(8,128)(2,1)S(1)}, u32[]{:S(2)}, u32[]{:S(2)}) collective-permute-start(bf16[256,1280]{1,0:T(8,128)(2,1)S(1)} %shard_map.94.shared_ref), channel_id=1, source_target_pairs={{0,32},{1,33},{2,34},{3,35},{4,36},{5,37},{6,38},{7,39},{8,40},{9,... | collective-permute-start | bytes 1966088 | tf_op jit(solution)/shard_map/ppermute | solution.py:43
  25.9 1.5 %collective-permute-done.1.handed_ref = bf16[256,1280]{1,0:T(8,128)(2,1)S(1)} collective-permute-done((bf16[256,1280]{1,0:T(8,128)(2,1)S(1)}, bf16[256,1280]{1,0:T(8,128)(2,1)S(1)}, u32[]{:S(2)}, u32[]{:S(2)}) %collective-permute-start.1) | collective-permute-done | bytes 655392 | tf_op jit(solution)/shard_map/ppermute | solution.py:43
  27.4 3.8 %shard_map.95 = (bf16[256,1280]{1,0:T(8,128)(2,1)S(1)}, bf16[256,640]{1,0:T(8,128)(2,1)S(1)}, f32[256,1920]{1,0:T(8,128)S(1)}) custom-call(s32[7]{0:T(128)S(1)} %stack.31.at, bf16[256,1280]{1,0:T(8,128)(2,1)S(1)} %shard_map.94.shared_ref, bf16[256,1280]{1,0:T(8,128)(2,1)S(1)} %collective-permute-done.1.handed_ref, bf16[3,1280,640]{2,1,0:T(8,128)(2,1)} %first_hbm.5, ...), custom_call_target="tpu_custom_call" | custom-call | flops 1024 | bytes 1024 | tf_op jit(solution)/shard_map/pallas_call | solution.py:269
  31.9 3.7 %all-to-all-done = bf16[32,8,1280]{2,1,0:T(8,128)(2,1)S(1)} async-done(((bf16[32,8,1280]{2,1,0:T(8,128)(2,1)}), bf16[32,8,1280]{2,1,0:T(8,128)(2,1)S(1)}, u32[]{:S(2)}, u32[]{:S(2)}) %all-to-all-start) | async-done | bytes 655392 | tf_op jit(solution)/shard_map/all_to_all | solution.py:676
  35.7 3.9 %shard_map.96 = (bf16[256,1280]{1,0:T(8,128)(2,1)S(1)}, bf16[256,640]{1,0:T(8,128)(2,1)S(1)}, f32[128,1280]{1,0:T(8,128)S(1)}, bf16[128,1280]{1,0:T(8,128)(2,1)S(1)}) custom-call(s32[7]{0:T(128)S(1)} %stack.31.at, bf16[256,256]{1,0:T(8,128)(2,1)S(1)} %and_convert_fusion.sorter_ref, bf16[256,1280]{1,0:T(8,128)(2,1)S(1)} %bitcast.14, ...), custom_call_target="tpu_custom_call" | custom-call | flops 1024 | bytes 1024 | tf_op jit(solution)/shard_map/pallas_call | solution.py:269
  39.7 2.0 %shard_map.97 = (bf16[2,8,40,1280]{3,2,1,0:T(8,128)(2,1)S(1)}, bf16[2,8,40,1280]{3,2,1,0:T(8,128)(2,1)S(1)}) custom-call(s32[7]{0:T(128)S(1)} %stack.31.at, bf16[256,1280]{1,0:T(8,128)(2,1)S(1)} %get-tuple-element.63.student_ref, bf16[256,640]{1,0:T(8,128)(2,1)S(1)} %get-tuple-element.64.grad_zeta_ref, bf16[256,640]{1,0:T(8,128)(2,1)S(1)} %copy-done.1, ...), custom_call_target="tpu_custom_call" | custom-call | flops 838860800 | bytes 5242880 | tf_op jit(solution)/shard_map/pallas_call | solution.py:64
  43.0 2.4 %collective-permute-start.9 = (bf16[2,8,40,1280]{3,2,1,0:T(8,128)(2,1)S(1)}, bf16[2,8,40,1280]{3,2,1,0:T(8,128)(2,1)S(1)}, u32[]{:S(2)}, u32[]{:S(2)}) collective-permute-start(bf16[2,8,40,1280]{3,2,1,0:T(8,128)(2,1)S(1)} %get-tuple-element.84), channel_id=1, source_target_pairs={{0,3},{1,2},{2,1},{3,0},{4,7},{5,6},{6,5},{7,4},{8,11},{9,10},{10,... | collective-permute-start | bytes 4915208 | tf_op jit(solution)/shard_map/ppermute | solution.py:43
  45.4 1.5 %collective-permute-start.4 = (bf16[128,1280]{1,0:T(8,128)(2,1)S(1)}, bf16[128,1280]{1,0:T(8,128)(2,1)S(1)}, u32[]{:S(2)}, u32[]{:S(2)}) collective-permute-start(bf16[128,1280]{1,0:T(8,128)(2,1)S(1)} %get-tuple-element.69), channel_id=1, source_target_pairs={{0,68},{1,69},{2,70},{3,71},{4,64},{5,65},{6,66},{7,67},{8,76},{9,... | collective-permute-start | bytes 983048 | tf_op jit(solution)/shard_map/ppermute | solution.py:43
  47.9 1.9 %shard_map.99 = (bf16[256,2560]{1,0:T(8,128)(2,1)S(1)}, bf16[256,1280]{1,0:T(8,128)(2,1)S(1)}, bf16[1280,1280]{1,0:T(8,128)(2,1)S(1)}) custom-call(s32[7]{0:T(128)S(1)} %stack.31.at, bf16[256,2560]{1,0:T(8,128)(2,1)} %collective-permute-done.5.crossed_hbm, bf16[256,2560]{1,0:T(8,128)(2,1)} %copy-done.2, bf16[1792,1280]{1,0:T(8,128)(2,1)} %get-tuple-element.59.hand_hbm, ...), custom_call_target="tpu_custom_call" | custom-call | bytes 8388608 | tf_op jit(solution)/shard_map/pallas_call | solution.py:398
  49.8 6.1 %collective-permute-done.4.across_ref = bf16[128,1280]{1,0:T(8,128)(2,1)S(1)} collective-permute-done((bf16[128,1280]{1,0:T(8,128)(2,1)S(1)}, bf16[128,1280]{1,0:T(8,128)(2,1)S(1)}, u32[]{:S(2)}, u32[]{:S(2)}) %collective-permute-start.4) | collective-permute-done | bytes 327712 | tf_op jit(solution)/shard_map/ppermute | solution.py:43
  56.7 1.6 %collective-permute-done.7.other_ref = bf16[128,1280]{1,0:T(8,128)(2,1)S(1)} collective-permute-done((bf16[128,1280]{1,0:T(8,128)(2,1)S(1)}, bf16[128,1280]{1,0:T(8,128)(2,1)S(1)}, u32[]{:S(2)}, u32[]{:S(2)}) %collective-permute-start.7) | collective-permute-done | bytes 327712 | tf_op jit(solution)/shard_map/ppermute | solution.py:43
  58.3 2.1 %shard_map.101 = (bf16[2,8,40,640]{3,2,1,0:T(8,128)(2,1)S(1)}, bf16[2,8,40,640]{3,2,1,0:T(8,128)(2,1)S(1)}, bf16[2,8,40,640]{3,2,1,0:T(8,128)(2,1)S(1)}, bf16[2,8,40,640]{3,2,1,0:T(8,128)(2,1)S(1)}) custom-call(s32[7]{0:T(128)S(1)} %stack.31.at, bf16[256,2560]{1,0:T(8,128)(2,1)S(1)} %get-tuple-element.76.left, ...), custom_call_target="tpu_custom_call" | custom-call | flops 1677721600 | bytes 9175040 | tf_op jit(solution)/shard_map/pallas_call | solution.py:64
  60.4 1.5 %collective-permute-start.8 = (bf16[2,8,40,640]{3,2,1,0:T(8,128)(2,1)S(1)}, bf16[2,8,40,640]{3,2,1,0:T(8,128)(2,1)S(1)}, u32[]{:S(2)}, u32[]{:S(2)}) collective-permute-start(bf16[2,8,40,640]{3,2,1,0:T(8,128)(2,1)S(1)} %get-tuple-element.82), channel_id=1, source_target_pairs={{0,1},{1,0},{2,3},{3,2},{4,5},{5,4},{6,7},{7,6},{8,9},{9,8},{10,11... | collective-permute-start | bytes 2457608 | tf_op jit(solution)/shard_map/ppermute | solution.py:43
  62.5 2.8 %collective-permute-done.9.came_ref = bf16[2,8,40,1280]{3,2,1,0:T(8,128)(2,1)S(1)} collective-permute-done((bf16[2,8,40,1280]{3,2,1,0:T(8,128)(2,1)S(1)}, bf16[2,8,40,1280]{3,2,1,0:T(8,128)(2,1)S(1)}, u32[]{:S(2)}, u32[]{:S(2)}) %collective-permute-start.9) | collective-permute-done | bytes 1638432 | tf_op jit(solution)/shard_map/ppermute | solution.py:43
  66.1 6.7 %collective-permute-done.8.came_a = bf16[2,8,40,640]{3,2,1,0:T(8,128)(2,1)S(1)} collective-permute-done((bf16[2,8,40,640]{3,2,1,0:T(8,128)(2,1)S(1)}, bf16[2,8,40,640]{3,2,1,0:T(8,128)(2,1)S(1)}, u32[]{:S(2)}, u32[]{:S(2)}) %collective-permute-start.8) | collective-permute-done | bytes 819232 | tf_op jit(solution)/shard_map/ppermute | solution.py:43
  72.8 2.6 %collective-permute-done.10.came_b = bf16[2,8,40,640]{3,2,1,0:T(8,128)(2,1)S(1)} collective-permute-done((bf16[2,8,40,640]{3,2,1,0:T(8,128)(2,1)S(1)}, bf16[2,8,40,640]{3,2,1,0:T(8,128)(2,1)S(1)}, u32[]{:S(2)}, u32[]{:S(2)}) %collective-permute-start.10) | collective-permute-done | bytes 819232 | tf_op jit(solution)/shard_map/ppermute | solution.py:43
  77.3 8.1 %collective-permute-done.11.last_a = bf16[8,40,640]{2,1,0:T(8,128)(2,1)S(1)} collective-permute-done((bf16[8,40,640]{2,1,0:T(8,128)(2,1)S(1)}, bf16[8,40,640]{2,1,0:T(8,128)(2,1)S(1)}, u32[]{:S(2)}, u32[]{:S(2)}) %collective-permute-start.11) | collective-permute-done | bytes 409632 | tf_op jit(solution)/shard_map/ppermute | solution.py:43
  89.0 2.2 %collective-permute-start.16 = (bf16[2,2,40,1280]{3,2,1,0:T(8,128)(2,1)S(1)}, bf16[2,2,40,1280]{3,2,1,0:T(8,128)(2,1)S(1)}, u32[]{:S(2)}, u32[]{:S(2)}) collective-permute-start(bf16[2,2,40,1280]{3,2,1,0:T(8,128)(2,1)S(1)} %get-tuple-element.96), channel_id=1, source_target_pairs={{0,24},{1,25},{2,26},{3,27},{4,28},{5,29},{6,30},{7,31},{8,16},{9,... | collective-permute-start | bytes 1228808 | tf_op jit(solution)/shard_map/ppermute | solution.py:43
  91.1 3.9 %collective-permute-done.14.came_ref.came = bf16[2,2,40,1280]{3,2,1,0:T(8,128)(2,1)S(1)} collective-permute-done((bf16[2,2,40,1280]{3,2,1,0:T(8,128)(2,1)S(1)}, bf16[2,2,40,1280]{3,2,1,0:T(8,128)(2,1)S(1)}, u32[]{:S(2)}, u32[]{:S(2)}) %collective-permute-start.14) | collective-permute-done | bytes 409632 | tf_op jit(solution)/shard_map/ppermute | solution.py:43
  95.6 2.1 %collective-permute-start.15 = (bf16[2,40,1280]{2,1,0:T(8,128)(2,1)S(1)}, bf16[2,40,1280]{2,1,0:T(8,128)(2,1)S(1)}, u32[]{:S(2)}, u32[]{:S(2)}) collective-permute-start(bf16[2,40,1280]{2,1,0:T(8,128)(2,1)S(1)} %shard_map.105), channel_id=1, source_target_pairs={{0,24},{1,25},{2,26},{3,27},{4,28},{5,29},{6,30},{7,31},{8,16},{9,... | collective-permute-start | bytes 614408 | tf_op jit(solution)/shard_map/ppermute | solution.py:43
  99.0 3.7 %collective-permute-done.15.last = bf16[2,40,1280]{2,1,0:T(8,128)(2,1)S(1)} collective-permute-done((bf16[2,40,1280]{2,1,0:T(8,128)(2,1)S(1)}, bf16[2,40,1280]{2,1,0:T(8,128)(2,1)S(1)}, u32[]{:S(2)}, u32[]{:S(2)}) %collective-permute-start.15) | collective-permute-done | bytes 204832 | tf_op jit(solution)/shard_map/ppermute | solution.py:43
  102.7 2.0 %collective-permute-done.17.adapt_last = bf16[2,40,1280]{2,1,0:T(8,128)(2,1)S(1)} collective-permute-done((bf16[2,40,1280]{2,1,0:T(8,128)(2,1)S(1)}, bf16[2,40,1280]{2,1,0:T(8,128)(2,1)S(1)}, u32[]{:S(2)}, u32[]{:S(2)}) %collective-permute-start.17) | collective-permute-done | bytes 204832 | tf_op jit(solution)/shard_map/ppermute | solution.py:43
  105.8 1.9 %collective-permute-start.19 = (bf16[40,1280]{1,0:T(8,128)(2,1)S(1)}, bf16[40,1280]{1,0:T(8,128)(2,1)S(1)}, u32[]{:S(2)}, u32[]{:S(2)}) collective-permute-start(bf16[40,1280]{1,0:T(8,128)(2,1)S(1)} %get-tuple-element.100), channel_id=1, source_target_pairs={{0,68},{1,69},{2,70},{3,71},{4,64},{5,65},{6,66},{7,67},{8,76},{9,... | collective-permute-start | bytes 307208 | tf_op jit(solution)/shard_map/ppermute | solution.py:43
  107.6 2.0 %collective-permute-start.20 = (bf16[40,1280]{1,0:T(8,128)(2,1)S(1)}, bf16[40,1280]{1,0:T(8,128)(2,1)S(1)}, u32[]{:S(2)}, u32[]{:S(2)}) collective-permute-start(bf16[40,1280]{1,0:T(8,128)(2,1)S(1)} %get-tuple-element.101), channel_id=1, source_target_pairs={{0,64},{1,65},{2,66},{3,67},{4,68},{5,69},{6,70},{7,71},{8,72},{9,... | collective-permute-start | bytes 307208 | tf_op jit(solution)/shard_map/ppermute | solution.py:43
  109.6 2.0 %collective-permute-done.19.near_ref = bf16[40,1280]{1,0:T(8,128)(2,1)S(1)} collective-permute-done((bf16[40,1280]{1,0:T(8,128)(2,1)S(1)}, bf16[40,1280]{1,0:T(8,128)(2,1)S(1)}, u32[]{:S(2)}, u32[]{:S(2)}) %collective-permute-start.19) | collective-permute-done | bytes 102432 | tf_op jit(solution)/shard_map/ppermute | solution.py:43
  111.6 2.2 %collective-permute-done.20.far_ref = bf16[40,1280]{1,0:T(8,128)(2,1)S(1)} collective-permute-done((bf16[40,1280]{1,0:T(8,128)(2,1)S(1)}, bf16[40,1280]{1,0:T(8,128)(2,1)S(1)}, u32[]{:S(2)}, u32[]{:S(2)}) %collective-permute-start.20) | collective-permute-done | bytes 102432 | tf_op jit(solution)/shard_map/ppermute | solution.py:43
  113.8 1.2 %shard_map.109 = (f32[2,40,1280]{2,1,0:T(8,128)S(1)}, bf16[2,40,1280]{2,1,0:T(8,128)(2,1)S(1)}, f32[1,40,640]{2,1,0:T(8,128)}, f32[20,1,1280]{2,1,0:T(1,128)}) custom-call(s32[7]{0:T(128)S(1)} %stack.31.at, f32[2,40,1280]{2,1,0:T(8,128)S(1)} %get-tuple-element.98.mine_ref, bf16[2,40,1280]{2,1,0:T(8,128)(2,1)S(1)} %collective-permute-done.18.beside_ref, ...), custom_call_target="tpu_custom_call" | custom-call | bytes 1638400 | tf_op jit(solution)/shard_map/pallas_call | solution.py:64
  115.1 1.5 %collective-permute-done.21.low_ref = bf16[2,40,1280]{2,1,0:T(8,128)(2,1)S(1)} collective-permute-done((bf16[2,40,1280]{2,1,0:T(8,128)(2,1)S(1)}, bf16[2,40,1280]{2,1,0:T(8,128)(2,1)S(1)}, u32[]{:S(2)}, u32[]{:S(2)}) %collective-permute-start.21) | collective-permute-done | bytes 204832 | tf_op jit(solution)/shard_map/ppermute | solution.py:43
  116.5 1.5 %shard_map.110 = (f32[1,40,2560]{2,1,0:T(8,128)}, f32[1,80,1280]{2,1,0:T(8,128)}) custom-call(s32[7]{0:T(128)S(1)} %stack.31.at, f32[2,40,1280]{2,1,0:T(8,128)S(1)} %get-tuple-element.104.high_ref, bf16[2,40,1280]{2,1,0:T(8,128)(2,1)S(1)} %collective-permute-done.21.low_ref), custom_call_target="tpu_custom_call" | custom-call | bytes 1433600 | tf_op jit(solution)/shard_map/pallas_call | solution.py:64
  (47 shorter events, 15.2 us)
Async XLA Ops:
  0.7 23.0 %copy-start.3 = (s32[4,8]{1,0:T(4,128)S(1)}, s32[4,8]{1,0:T(4,128)}, u32[]{:S(2)}) copy-start(s32[4,8]{1,0:T(4,128)} %param.11) | copy-start | bytes 388
  11.9 20.0 %collective-permute-start.2 = (bf16[1792,1280]{1,0:T(8,128)(2,1)}, bf16[1792,1280]{1,0:T(8,128)(2,1)}, u32[]{:S(2)}, u32[]{:S(2)}) collective-permute-start(bf16[1792,1280]{1,0:T(8,128)(2,1)} %get-tuple-element.59.hand_hbm), channel_id=1, source_target_pairs={{0,32},{1,33},{2,34},{3,35},{4,36},{5,37},{6,38},{7,39},{8,40},{9,... | collective-permute-start | bytes 13762568 | tf_op jit(solution)/shard_map/ppermute | solution.py:43
  12.0 11.8 %collective-permute-start = (bf16[256,1280]{1,0:T(8,128)(2,1)S(1)}, bf16[256,1280]{1,0:T(8,128)(2,1)S(1)}, u32[]{:S(2)}, u32[]{:S(2)}) collective-permute-start(bf16[256,1280]{1,0:T(8,128)(2,1)S(1)} %get-tuple-element.57.own_ref), channel_id=1, source_target_pairs={{96,36},{97,37},{98,38},{99,39},{100,32},{101,33},{102,34},{103,35... | collective-permute-start | bytes 1966088 | tf_op jit(solution)/shard_map/ppermute | solution.py:43
  12.7 23.0 %all-to-all-start = ((bf16[32,8,1280]{2,1,0:T(8,128)(2,1)}), bf16[32,8,1280]{2,1,0:T(8,128)(2,1)S(1)}, u32[]{:S(2)}, u32[]{:S(2)}) async-start(bf16[32,8,1280]{2,1,0:T(8,128)(2,1)} %bitcast.9), calls=%async_computation | async-start | bytes 1310720 | tf_op jit(solution)/shard_map/all_to_all | solution.py:676
  22.0 20.4 %collective-permute-start.5 = (bf16[256,2560]{1,0:T(8,128)(2,1)}, bf16[256,2560]{1,0:T(8,128)(2,1)}, u32[]{:S(2)}, u32[]{:S(2)}) collective-permute-start(bf16[256,2560]{1,0:T(8,128)(2,1)} %get-tuple-element.71), channel_id=1, source_target_pairs={{96,36},{97,37},{98,38},{99,39},{100,32},{101,33},{102,34},{103,35... | collective-permute-start | bytes 3932168 | tf_op jit(solution)/shard_map/ppermute | solution.py:43
  24.4 3.0 %collective-permute-start.1 = (bf16[256,1280]{1,0:T(8,128)(2,1)S(1)}, bf16[256,1280]{1,0:T(8,128)(2,1)S(1)}, u32[]{:S(2)}, u32[]{:S(2)}) collective-permute-start(bf16[256,1280]{1,0:T(8,128)(2,1)S(1)} %shard_map.94.shared_ref), channel_id=1, source_target_pairs={{0,32},{1,33},{2,34},{3,35},{4,36},{5,37},{6,38},{7,39},{8,40},{9,... | collective-permute-start | bytes 1966088 | tf_op jit(solution)/shard_map/ppermute | solution.py:43
  31.2 0.7 copy-start
  35.7 4.0 %copy-start.1 = (bf16[256,640]{1,0:T(8,128)(2,1)S(1)}, bf16[256,640]{1,0:T(8,128)(2,1)}, u32[]{:S(2)}) copy-start(bf16[256,640]{1,0:T(8,128)(2,1)} %copy-done) | copy-start | bytes 983044
  39.6 2.1 %collective-permute-start.3 = (bf16[128,1280]{1,0:T(8,128)(2,1)S(1)}, bf16[128,1280]{1,0:T(8,128)(2,1)S(1)}, u32[]{:S(2)}, u32[]{:S(2)}) collective-permute-start(bf16[128,1280]{1,0:T(8,128)(2,1)S(1)} %get-tuple-element.62), channel_id=1, source_target_pairs={{0,32},{1,33},{2,34},{3,35},{4,36},{5,37},{6,38},{7,39},{8,40},{9,... | collective-permute-start | bytes 983048 | tf_op jit(solution)/shard_map/ppermute | solution.py:43
  42.4 4.5 %collective-permute-start.6 = (bf16[256,2560]{1,0:T(8,128)(2,1)}, bf16[256,2560]{1,0:T(8,128)(2,1)S(1)}, u32[]{:S(2)}, u32[]{:S(2)}) collective-permute-start(bf16[256,2560]{1,0:T(8,128)(2,1)} %collective-permute-done.5.crossed_hbm), channel_id=1, source_target_pairs={{0,32},{1,33},{2,34},{3,35},{4,36},{5,37},{6,38},{7,39},{8,40},{9,... | collective-permute-start | bytes 3932168 | tf_op jit(solution)/shard_map/ppermute | solution.py:43
  43.0 22.3 %collective-permute-start.9 = (bf16[2,8,40,1280]{3,2,1,0:T(8,128)(2,1)S(1)}, bf16[2,8,40,1280]{3,2,1,0:T(8,128)(2,1)S(1)}, u32[]{:S(2)}, u32[]{:S(2)}) collective-permute-start(bf16[2,8,40,1280]{3,2,1,0:T(8,128)(2,1)S(1)} %get-tuple-element.84), channel_id=1, source_target_pairs={{0,3},{1,2},{2,1},{3,0},{4,7},{5,6},{6,5},{7,4},{8,11},{9,10},{10,... | collective-permute-start | bytes 4915208 | tf_op jit(solution)/shard_map/ppermute | solution.py:43
  45.4 10.6 %collective-permute-start.4 = (bf16[128,1280]{1,0:T(8,128)(2,1)S(1)}, bf16[128,1280]{1,0:T(8,128)(2,1)S(1)}, u32[]{:S(2)}, u32[]{:S(2)}) collective-permute-start(bf16[128,1280]{1,0:T(8,128)(2,1)S(1)} %get-tuple-element.69), channel_id=1, source_target_pairs={{0,68},{1,69},{2,70},{3,71},{4,64},{5,65},{6,66},{7,67},{8,76},{9,... | collective-permute-start | bytes 983048 | tf_op jit(solution)/shard_map/ppermute | solution.py:43
  46.9 1.0 copy-start.2
  56.6 1.7 %collective-permute-start.7 = (bf16[128,1280]{1,0:T(8,128)(2,1)S(1)}, bf16[128,1280]{1,0:T(8,128)(2,1)S(1)}, u32[]{:S(2)}, u32[]{:S(2)}) collective-permute-start(bf16[128,1280]{1,0:T(8,128)(2,1)S(1)} %shard_map.100.mine_ref), channel_id=1, source_target_pairs={{0,32},{1,33},{2,34},{3,35},{4,36},{5,37},{6,38},{7,39},{8,40},{9,... | collective-permute-start | bytes 983048 | tf_op jit(solution)/shard_map/ppermute | solution.py:43
  60.4 12.4 %collective-permute-start.8 = (bf16[2,8,40,640]{3,2,1,0:T(8,128)(2,1)S(1)}, bf16[2,8,40,640]{3,2,1,0:T(8,128)(2,1)S(1)}, u32[]{:S(2)}, u32[]{:S(2)}) collective-permute-start(bf16[2,8,40,640]{3,2,1,0:T(8,128)(2,1)S(1)} %get-tuple-element.82), channel_id=1, source_target_pairs={{0,1},{1,0},{2,3},{3,2},{4,5},{5,4},{6,7},{7,6},{8,9},{9,8},{10,11... | collective-permute-start | bytes 2457608 | tf_op jit(solution)/shard_map/ppermute | solution.py:43
  61.9 13.6 %collective-permute-start.10 = (bf16[2,8,40,640]{3,2,1,0:T(8,128)(2,1)S(1)}, bf16[2,8,40,640]{3,2,1,0:T(8,128)(2,1)S(1)}, u32[]{:S(2)}, u32[]{:S(2)}) collective-permute-start(bf16[2,8,40,640]{3,2,1,0:T(8,128)(2,1)S(1)} %get-tuple-element.86), channel_id=1, source_target_pairs={{0,3},{1,2},{2,1},{3,0},{4,7},{5,6},{6,5},{7,4},{8,11},{9,10},{10,... | collective-permute-start | bytes 2457608 | tf_op jit(solution)/shard_map/ppermute | solution.py:43
  66.0 21.8 %collective-permute-start.13 = (bf16[8,40,1280]{2,1,0:T(8,128)(2,1)S(1)}, bf16[8,40,1280]{2,1,0:T(8,128)(2,1)S(1)}, u32[]{:S(2)}, u32[]{:S(2)}) collective-permute-start(bf16[8,40,1280]{2,1,0:T(8,128)(2,1)S(1)} %shard_map.104), channel_id=1, source_target_pairs={{0,1},{1,0},{2,3},{3,2},{4,5},{5,4},{6,7},{7,6},{8,9},{9,8},{10,11... | collective-permute-start | bytes 2457608 | tf_op jit(solution)/shard_map/ppermute | solution.py:43
  76.2 9.2 %collective-permute-start.11 = (bf16[8,40,640]{2,1,0:T(8,128)(2,1)S(1)}, bf16[8,40,640]{2,1,0:T(8,128)(2,1)S(1)}, u32[]{:S(2)}, u32[]{:S(2)}) collective-permute-start(bf16[8,40,640]{2,1,0:T(8,128)(2,1)S(1)} %get-tuple-element.87), channel_id=1, source_target_pairs={{0,3},{1,2},{2,1},{3,0},{4,7},{5,6},{6,5},{7,4},{8,11},{9,10},{10,... | collective-permute-start | bytes 1228808 | tf_op jit(solution)/shard_map/ppermute | solution.py:43
  77.3 8.7 %collective-permute-start.12 = (bf16[8,40,640]{2,1,0:T(8,128)(2,1)S(1)}, bf16[8,40,640]{2,1,0:T(8,128)(2,1)S(1)}, u32[]{:S(2)}, u32[]{:S(2)}) collective-permute-start(bf16[8,40,640]{2,1,0:T(8,128)(2,1)S(1)} %get-tuple-element.88), channel_id=1, source_target_pairs={{0,1},{1,0},{2,3},{3,2},{4,5},{5,4},{6,7},{7,6},{8,9},{9,8},{10,11... | collective-permute-start | bytes 1228808 | tf_op jit(solution)/shard_map/ppermute | solution.py:43
  87.0 8.0 %collective-permute-start.14 = (bf16[2,2,40,1280]{3,2,1,0:T(8,128)(2,1)S(1)}, bf16[2,2,40,1280]{3,2,1,0:T(8,128)(2,1)S(1)}, u32[]{:S(2)}, u32[]{:S(2)}) collective-permute-start(bf16[2,2,40,1280]{3,2,1,0:T(8,128)(2,1)S(1)} %get-tuple-element.93), channel_id=1, source_target_pairs={{0,8},{1,9},{2,10},{3,11},{4,12},{5,13},{6,14},{7,15},{8,0},{9,1},... | collective-permute-start | bytes 1228808 | tf_op jit(solution)/shard_map/ppermute | solution.py:43
  89.0 9.2 %collective-permute-start.16 = (bf16[2,2,40,1280]{3,2,1,0:T(8,128)(2,1)S(1)}, bf16[2,2,40,1280]{3,2,1,0:T(8,128)(2,1)S(1)}, u32[]{:S(2)}, u32[]{:S(2)}) collective-permute-start(bf16[2,2,40,1280]{3,2,1,0:T(8,128)(2,1)S(1)} %get-tuple-element.96), channel_id=1, source_target_pairs={{0,24},{1,25},{2,26},{3,27},{4,28},{5,29},{6,30},{7,31},{8,16},{9,... | collective-permute-start | bytes 1228808 | tf_op jit(solution)/shard_map/ppermute | solution.py:43
  95.6 7.0 %collective-permute-start.15 = (bf16[2,40,1280]{2,1,0:T(8,128)(2,1)S(1)}, bf16[2,40,1280]{2,1,0:T(8,128)(2,1)S(1)}, u32[]{:S(2)}, u32[]{:S(2)}) collective-permute-start(bf16[2,40,1280]{2,1,0:T(8,128)(2,1)S(1)} %shard_map.105), channel_id=1, source_target_pairs={{0,24},{1,25},{2,26},{3,27},{4,28},{5,29},{6,30},{7,31},{8,16},{9,... | collective-permute-start | bytes 614408 | tf_op jit(solution)/shard_map/ppermute | solution.py:43
  98.8 5.8 %collective-permute-start.17 = (bf16[2,40,1280]{2,1,0:T(8,128)(2,1)S(1)}, bf16[2,40,1280]{2,1,0:T(8,128)(2,1)S(1)}, u32[]{:S(2)}, u32[]{:S(2)}) collective-permute-start(bf16[2,40,1280]{2,1,0:T(8,128)(2,1)S(1)} %shard_map.107), channel_id=1, source_target_pairs={{0,8},{1,9},{2,10},{3,11},{4,12},{5,13},{6,14},{7,15},{8,0},{9,1},... | collective-permute-start | bytes 614408 | tf_op jit(solution)/shard_map/ppermute | solution.py:43
  105.4 8.4 %collective-permute-start.18 = (bf16[2,40,1280]{2,1,0:T(8,128)(2,1)S(1)}, bf16[2,40,1280]{2,1,0:T(8,128)(2,1)S(1)}, u32[]{:S(2)}, u32[]{:S(2)}) collective-permute-start(bf16[2,40,1280]{2,1,0:T(8,128)(2,1)S(1)} %get-tuple-element.99), channel_id=1, source_target_pairs={{0,4},{1,5},{2,6},{3,7},{4,0},{5,1},{6,2},{7,3},{8,12},{9,13},{10,... | collective-permute-start | bytes 614408 | tf_op jit(solution)/shard_map/ppermute | solution.py:43
  105.8 5.9 %collective-permute-start.19 = (bf16[40,1280]{1,0:T(8,128)(2,1)S(1)}, bf16[40,1280]{1,0:T(8,128)(2,1)S(1)}, u32[]{:S(2)}, u32[]{:S(2)}) collective-permute-start(bf16[40,1280]{1,0:T(8,128)(2,1)S(1)} %get-tuple-element.100), channel_id=1, source_target_pairs={{0,68},{1,69},{2,70},{3,71},{4,64},{5,65},{6,66},{7,67},{8,76},{9,... | collective-permute-start | bytes 307208 | tf_op jit(solution)/shard_map/ppermute | solution.py:43
  107.6 6.2 %collective-permute-start.20 = (bf16[40,1280]{1,0:T(8,128)(2,1)S(1)}, bf16[40,1280]{1,0:T(8,128)(2,1)S(1)}, u32[]{:S(2)}, u32[]{:S(2)}) collective-permute-start(bf16[40,1280]{1,0:T(8,128)(2,1)S(1)} %get-tuple-element.101), channel_id=1, source_target_pairs={{0,64},{1,65},{2,66},{3,67},{4,68},{5,69},{6,70},{7,71},{8,72},{9,... | collective-permute-start | bytes 307208 | tf_op jit(solution)/shard_map/ppermute | solution.py:43
  115.1 1.5 %collective-permute-start.21 = (bf16[2,40,1280]{2,1,0:T(8,128)(2,1)S(1)}, bf16[2,40,1280]{2,1,0:T(8,128)(2,1)S(1)}, u32[]{:S(2)}, u32[]{:S(2)}) collective-permute-start(bf16[2,40,1280]{2,1,0:T(8,128)(2,1)S(1)} %get-tuple-element.105), channel_id=1, source_target_pairs={{0,32},{1,33},{2,34},{3,35},{4,36},{5,37},{6,38},{7,39},{8,40},{9,... | collective-permute-start | bytes 614408 | tf_op jit(solution)/shard_map/ppermute | solution.py:43

commit v4 on v3

--- a/solution.py
+++ b/solution.py
@@ -506,29 +506,29 @@
                 ref[slot, yl] = total[line * 2 + yl].astype(ref.dtype)
 
 
-def both_kernel(
-    at, keep, came, last, adapt_keep, adapt_came, adapt_last, mine_ref, given_ref, near_ref, far_ref,
-    total,
-):
-    total[0] = keep[0] + came[0].astype(F32) + last[...].astype(F32)
-    total[1] = adapt_keep[0] + adapt_came[0].astype(F32) + adapt_last[...].astype(F32)
-    for slot in range(2):
-        mine_ref[slot] = total[slot, at[YL]]
-        given_ref[slot] = total[slot, 1 - at[YL]].astype(BF16)
-    near_ref[...] = total[0, 1 - at[YL]].astype(BF16)
-    far_ref[...] = total[0, at[YL]].astype(BF16)
-
-
-def piece_kernel(
-    at, mine_ref, beside_ref, near_ref, far_ref, piece_ref, sent_ref, first_ref, second_ref
-):
-    piece = mine_ref[0] + beside_ref[0].astype(F32)
-    piece_ref[0] = piece
-    sent_ref[0] = piece.astype(BF16)
-    piece = near_ref[...].astype(F32) + far_ref[...].astype(F32)
-    piece_ref[1] = piece
-    sent_ref[1] = piece.astype(BF16)
-    total = mine_ref[1] + beside_ref[1].astype(F32)
+def total_kernel(at, keep, came, last, mine_ref, given_ref, *refs):
+    *sent, total = refs
+    total[...] = keep[0] + came[0].astype(F32) + last[...].astype(F32)
+    mine_ref[...] = total[at[YL]]
+    other = total[1 - at[YL]].astype(BF16)
+    given_ref[...] = other
+    if sent:
+        sent[0][...] = other
+        sent[1][...] = total[at[YL]].astype(BF16)
+
+
+def piece_kernel(at, mine_ref, beside_ref, near_ref, far_ref, piece_ref, sent_ref):
+    pieces = (
+        mine_ref[...] + beside_ref[...].astype(F32),
+        near_ref[...].astype(F32) + far_ref[...].astype(F32),
+    )
+    for slot, piece in enumerate(pieces):
+        piece_ref[slot] = piece
+        sent_ref[slot] = piece.astype(BF16)
+
+
+def adapt_last_kernel(at, mine_ref, beside_ref, first_ref, second_ref):
+    total = mine_ref[...] + beside_ref[...].astype(F32)
     total = jnp.where(at[GROUP_AT] < 3, total, 0.0)
     first_ref[0] = total[:, :640]
     second_ref[:, 0, :640] = total[:20, 640:]
@@ -601,15 +601,34 @@
         next_kernel, scalars, (adapt_keep, adapt_came), [shaped(piece[1:], BF16)]
     )
     adapt_last = send(adapt_next, second_axis(1))
-    piece = (2, 40, 1280)
+    total = [pltpu.VMEM((2, 40, 1280), F32)]
+    whole, rounded = shaped((40, 1280), F32), shaped((40, 1280), BF16)
     mine, given, near, far = call(
-        both_kernel,
-        scalars,
-        (keep, came, last, adapt_keep, adapt_came, adapt_last),
-        [shaped(piece, F32), shaped(piece, BF16)] + [shaped(piece[1:], BF16)] * 2,
-        [pltpu.VMEM((2, *piece), F32)],
-    )
-    return mine, send(given, beside), send(near, exchange_across), send(far, exchange_far)
+        total_kernel, scalars, (keep, came, last), [whole, rounded, rounded, rounded], total
+    )
+    came, near, far = send(given, beside), send(near, exchange_across), send(far, exchange_far)
+    mine, adapt_last = lax.optimization_barrier((mine, adapt_last))
+    adapt_mine, adapt_given = call(
+        total_kernel, scalars, (adapt_keep, adapt_came, adapt_last), [whole, rounded], total
+    )
+    adapt_came = send(adapt_given, beside)
+    came, adapt_mine = lax.optimization_barrier((came, adapt_mine))
+    piece, piece_b = call(
+        piece_kernel,
+        scalars,
+        (mine, came, near, far),
+        [shaped((2, 40, 1280), F32), shaped((2, 40, 1280), BF16)],
+    )
+    piece_b, adapt_came = lax.optimization_barrier((piece_b, adapt_came))
+    low = send(piece_b, swap_core)
+    grad_first, grad_second = call(
+        adapt_last_kernel,
+        scalars,
+        (adapt_mine, adapt_came),
+        [shaped((1, 40, 640), F32), shaped((20, 1, 1280), F32)],
+    )
+    low, grad_first = lax.optimization_barrier((low, grad_first))
+    return piece, low, grad_first, grad_second
 
 
 def block_ids(order, positions, per_image):
@@ -735,23 +754,14 @@
     keep_a, give_a, keep_b, give_b = student_partial(
         scalars, (left, slopes, weights), mine, other
     )
-    parts = both_axes(scalars, keep_a, give_a, keep_b, give_b, adapt_keep, adapt_came)
-    piece, piece_b, grad_first, grad_second = call(
-        piece_kernel,
-        scalars,
-        parts,
-        [
-            shaped((2, 40, 1280), F32),
-            shaped((2, 40, 1280), BF16),
-            shaped((1, 40, 640), F32),
-            shaped((20, 1, 1280), F32),
-        ],
+    piece, low, grad_first, grad_second = both_axes(
+        scalars, keep_a, give_a, keep_b, give_b, adapt_keep, adapt_came
     )
     grad_second = jnp.swapaxes(grad_second, 0, 1)
     grad_in_sum, grad_out_sum = call(
         last_kernel,
         scalars,
-        (piece, send(piece_b, swap_core)),
+        (piece, low),
         [shaped((1, 40, 2560), F32), shaped((1, 80, 1280), F32)],
     )
     return (grad_first, grad_second, grad_in_sum, grad_out_sum)

time: 119 us -> 117 us (0.983)
  waiting for transfers between devices: 49.5 us -> 46 us
    ppermute x22 -> x23, waiting for transfers between devices: 45.8 us -> 42.3 us  [send(): return lax.ppermute(value, ALL, route(move))]
    pallas_call x14 -> x16, Pallas kernels: 14.2 us -> 15.3 us  [call(): pl.pallas_call(kernel, out_shape=list(outputs), in_specs=[smem()] + vmem(...]
    ppermute x22 -> x23, starting transfers between devices: 21.3 us -> 21.4 us  [send(): return lax.ppermute(value, ALL, route(move))]
  transfers between devices with their start and end apart: 23 -> 24, of which waited for: 16 -> 17; matrix products, arithmetic and copies ran while one was open for 0% -> 0% of each run, Pallas kernels for 17% -> 20%
where the time goes in v4:
time: 117 us; the launch traced here: 116 us
  waiting for transfers between devices  46 us (39%)
  Pallas kernels  36 us (31%)
  starting transfers between devices  30.7 us (26%)
  local copies, waits for them, and re-layouts  1.87 us (2%)
    ppermute x23, waiting for transfers between devices, send(): return lax.ppermute(value, ALL, route(move))  42.3 us
    ppermute x23, starting transfers between devices, send(): return lax.ppermute(value, ALL, route(move))  21.4 us
    pallas_call x16, Pallas kernels, call(): pl.pallas_call(kernel, out_shape=list(outputs), in_specs=[smem()] + vmem(...  15.3 us
    pallas_call x1, Pallas kernels, block_forward(): pl.pallas_call(forward_kernel, out_shape=[pltpu.HBM((tokens, hidden), BF1...  11.1 us
    all_to_all x1, starting transfers between devices, body(): lax.all_to_all(outgoing, WIDE, split_axis=0, concat_axis=0, tiled=True)  9.27 us
    pallas_call x2, Pallas kernels, adapt_call(): pl.pallas_call(kernel, out_shape=list(outputs), in_specs=[smem()] + vmem(...  7.69 us
    all_to_all x1, waiting for transfers between devices, body(): lax.all_to_all(outgoing, WIDE, split_axis=0, concat_axis=0, tiled=True)  3.74 us
  transfers between devices with their start and end apart: 24, of which 17 were waited for; matrix products, arithmetic and copies ran while one was open for 0% of the time, Pallas kernels for 20%

profile of v4, /device:TPU:0, one launch (start us, length us, event | category | flops | bytes accessed | tf_op | source)
XLA Modules:
  0.0 115.8 jit_solution(1475593042320196551)
XLA Ops:
  0.7 11.1 %shard_map.93 = (bf16[256,2560]{1,0:T(8,128)(2,1)}, bf16[1792,1280]{1,0:T(8,128)(2,1)}, bf16[256,1280]{1,0:T(8,128)(2,1)}, bf16[256,1280]{1,0:T(8,128)(2,1)S(1)}, bf16[256,1280]{1,0:T(8,128)(2,1)}) custom-call(s32[7]{0:T(128)S(1)} %stack.31.at, bf16[1,256,1280]{2,1,0:T(8,128)(2,1)} %acts_hbm.1, bf16[1,1280,2560]{2,1,0:T(8,128)(2,1)} %first_hbm.3, ...), custom_call_target="tpu_custom_call" | custom-call | flops 3355443200 | bytes 16777216 | tf_op jit(solution)/shard_map/pallas_call | solution.py:199
  12.7 9.3 %all-to-all-start = ((bf16[32,8,1280]{2,1,0:T(8,128)(2,1)}), bf16[32,8,1280]{2,1,0:T(8,128)(2,1)S(1)}, u32[]{:S(2)}, u32[]{:S(2)}) async-start(bf16[32,8,1280]{2,1,0:T(8,128)(2,1)} %bitcast.9), calls=%async_computation | async-start | bytes 1310720 | tf_op jit(solution)/shard_map/all_to_all | solution.py:695
  21.9 1.7 %collective-permute-start.5 = (bf16[256,2560]{1,0:T(8,128)(2,1)}, bf16[256,2560]{1,0:T(8,128)(2,1)}, u32[]{:S(2)}, u32[]{:S(2)}) collective-permute-start(bf16[256,2560]{1,0:T(8,128)(2,1)} %get-tuple-element.81), channel_id=1, source_target_pairs={{96,36},{97,37},{98,38},{99,39},{100,32},{101,33},{102,34},{103,35... | collective-permute-start | bytes 3932168 | tf_op jit(solution)/shard_map/ppermute | solution.py:43
  24.3 1.3 %collective-permute-start.1 = (bf16[256,1280]{1,0:T(8,128)(2,1)S(1)}, bf16[256,1280]{1,0:T(8,128)(2,1)S(1)}, u32[]{:S(2)}, u32[]{:S(2)}) collective-permute-start(bf16[256,1280]{1,0:T(8,128)(2,1)S(1)} %shard_map.94.shared_ref), channel_id=1, source_target_pairs={{0,32},{1,33},{2,34},{3,35},{4,36},{5,37},{6,38},{7,39},{8,40},{9,... | collective-permute-start | bytes 1966088 | tf_op jit(solution)/shard_map/ppermute | solution.py:43
  25.9 1.5 %collective-permute-done.1.handed_ref = bf16[256,1280]{1,0:T(8,128)(2,1)S(1)} collective-permute-done((bf16[256,1280]{1,0:T(8,128)(2,1)S(1)}, bf16[256,1280]{1,0:T(8,128)(2,1)S(1)}, u32[]{:S(2)}, u32[]{:S(2)}) %collective-permute-start.1) | collective-permute-done | bytes 655392 | tf_op jit(solution)/shard_map/ppermute | solution.py:43
  27.4 3.8 %shard_map.95 = (bf16[256,1280]{1,0:T(8,128)(2,1)S(1)}, bf16[256,640]{1,0:T(8,128)(2,1)S(1)}, f32[256,1920]{1,0:T(8,128)S(1)}) custom-call(s32[7]{0:T(128)S(1)} %stack.31.at, bf16[256,1280]{1,0:T(8,128)(2,1)S(1)} %shard_map.94.shared_ref, bf16[256,1280]{1,0:T(8,128)(2,1)S(1)} %collective-permute-done.1.handed_ref, bf16[3,1280,640]{2,1,0:T(8,128)(2,1)} %first_hbm.5, ...), custom_call_target="tpu_custom_call" | custom-call | flops 1024 | bytes 1024 | tf_op jit(solution)/shard_map/pallas_call | solution.py:269
  31.9 3.7 %all-to-all-done = bf16[32,8,1280]{2,1,0:T(8,128)(2,1)S(1)} async-done(((bf16[32,8,1280]{2,1,0:T(8,128)(2,1)}), bf16[32,8,1280]{2,1,0:T(8,128)(2,1)S(1)}, u32[]{:S(2)}, u32[]{:S(2)}) %all-to-all-start) | async-done | bytes 655392 | tf_op jit(solution)/shard_map/all_to_all | solution.py:695
  35.6 3.9 %shard_map.96 = (bf16[256,1280]{1,0:T(8,128)(2,1)S(1)}, bf16[256,640]{1,0:T(8,128)(2,1)S(1)}, f32[128,1280]{1,0:T(8,128)S(1)}, bf16[128,1280]{1,0:T(8,128)(2,1)S(1)}) custom-call(s32[7]{0:T(128)S(1)} %stack.31.at, bf16[256,256]{1,0:T(8,128)(2,1)S(1)} %and_convert_fusion.sorter_ref, bf16[256,1280]{1,0:T(8,128)(2,1)S(1)} %bitcast.14, ...), custom_call_target="tpu_custom_call" | custom-call | flops 1024 | bytes 1024 | tf_op jit(solution)/shard_map/pallas_call | solution.py:269
  39.7 2.0 %shard_map.97 = (bf16[2,8,40,1280]{3,2,1,0:T(8,128)(2,1)S(1)}, bf16[2,8,40,1280]{3,2,1,0:T(8,128)(2,1)S(1)}) custom-call(s32[7]{0:T(128)S(1)} %stack.31.at, bf16[256,1280]{1,0:T(8,128)(2,1)S(1)} %get-tuple-element.73.student_ref, bf16[256,640]{1,0:T(8,128)(2,1)S(1)} %get-tuple-element.74.grad_zeta_ref, bf16[256,640]{1,0:T(8,128)(2,1)S(1)} %copy-done.1, ...), custom_call_target="tpu_custom_call" | custom-call | flops 838860800 | bytes 5242880 | tf_op jit(solution)/shard_map/pallas_call | solution.py:64
  42.9 2.4 %collective-permute-start.9 = (bf16[2,8,40,1280]{3,2,1,0:T(8,128)(2,1)S(1)}, bf16[2,8,40,1280]{3,2,1,0:T(8,128)(2,1)S(1)}, u32[]{:S(2)}, u32[]{:S(2)}) collective-permute-start(bf16[2,8,40,1280]{3,2,1,0:T(8,128)(2,1)S(1)} %get-tuple-element.94), channel_id=1, source_target_pairs={{0,3},{1,2},{2,1},{3,0},{4,7},{5,6},{6,5},{7,4},{8,11},{9,10},{10,... | collective-permute-start | bytes 4915208 | tf_op jit(solution)/shard_map/ppermute | solution.py:43
  45.3 1.5 %collective-permute-start.4 = (bf16[128,1280]{1,0:T(8,128)(2,1)S(1)}, bf16[128,1280]{1,0:T(8,128)(2,1)S(1)}, u32[]{:S(2)}, u32[]{:S(2)}) collective-permute-start(bf16[128,1280]{1,0:T(8,128)(2,1)S(1)} %get-tuple-element.79), channel_id=1, source_target_pairs={{0,68},{1,69},{2,70},{3,71},{4,64},{5,65},{6,66},{7,67},{8,76},{9,... | collective-permute-start | bytes 983048 | tf_op jit(solution)/shard_map/ppermute | solution.py:43
  47.9 1.9 %shard_map.99 = (bf16[256,2560]{1,0:T(8,128)(2,1)S(1)}, bf16[256,1280]{1,0:T(8,128)(2,1)S(1)}, bf16[1280,1280]{1,0:T(8,128)(2,1)S(1)}) custom-call(s32[7]{0:T(128)S(1)} %stack.31.at, bf16[256,2560]{1,0:T(8,128)(2,1)} %collective-permute-done.5.crossed_hbm, bf16[256,2560]{1,0:T(8,128)(2,1)} %copy-done.2, bf16[1792,1280]{1,0:T(8,128)(2,1)} %get-tuple-element.69.hand_hbm, ...), custom_call_target="tpu_custom_call" | custom-call | bytes 8388608 | tf_op jit(solution)/shard_map/pallas_call | solution.py:398
  49.8 6.1 %collective-permute-done.4.across_ref = bf16[128,1280]{1,0:T(8,128)(2,1)S(1)} collective-permute-done((bf16[128,1280]{1,0:T(8,128)(2,1)S(1)}, bf16[128,1280]{1,0:T(8,128)(2,1)S(1)}, u32[]{:S(2)}, u32[]{:S(2)}) %collective-permute-start.4) | collective-permute-done | bytes 327712 | tf_op jit(solution)/shard_map/ppermute | solution.py:43
  56.6 1.6 %collective-permute-done.7.other_ref = bf16[128,1280]{1,0:T(8,128)(2,1)S(1)} collective-permute-done((bf16[128,1280]{1,0:T(8,128)(2,1)S(1)}, bf16[128,1280]{1,0:T(8,128)(2,1)S(1)}, u32[]{:S(2)}, u32[]{:S(2)}) %collective-permute-start.7) | collective-permute-done | bytes 327712 | tf_op jit(solution)/shard_map/ppermute | solution.py:43
  58.2 2.1 %shard_map.101 = (bf16[2,8,40,640]{3,2,1,0:T(8,128)(2,1)S(1)}, bf16[2,8,40,640]{3,2,1,0:T(8,128)(2,1)S(1)}, bf16[2,8,40,640]{3,2,1,0:T(8,128)(2,1)S(1)}, bf16[2,8,40,640]{3,2,1,0:T(8,128)(2,1)S(1)}) custom-call(s32[7]{0:T(128)S(1)} %stack.31.at, bf16[256,2560]{1,0:T(8,128)(2,1)S(1)} %get-tuple-element.86.left, ...), custom_call_target="tpu_custom_call" | custom-call | flops 1677721600 | bytes 9175040 | tf_op jit(solution)/shard_map/pallas_call | solution.py:64
  60.3 1.5 %collective-permute-start.8 = (bf16[2,8,40,640]{3,2,1,0:T(8,128)(2,1)S(1)}, bf16[2,8,40,640]{3,2,1,0:T(8,128)(2,1)S(1)}, u32[]{:S(2)}, u32[]{:S(2)}) collective-permute-start(bf16[2,8,40,640]{3,2,1,0:T(8,128)(2,1)S(1)} %get-tuple-element.92), channel_id=1, source_target_pairs={{0,1},{1,0},{2,3},{3,2},{4,5},{5,4},{6,7},{7,6},{8,9},{9,8},{10,11... | collective-permute-start | bytes 2457608 | tf_op jit(solution)/shard_map/ppermute | solution.py:43
  62.5 2.8 %collective-permute-done.9.came_ref = bf16[2,8,40,1280]{3,2,1,0:T(8,128)(2,1)S(1)} collective-permute-done((bf16[2,8,40,1280]{3,2,1,0:T(8,128)(2,1)S(1)}, bf16[2,8,40,1280]{3,2,1,0:T(8,128)(2,1)S(1)}, u32[]{:S(2)}, u32[]{:S(2)}) %collective-permute-start.9) | collective-permute-done | bytes 1638432 | tf_op jit(solution)/shard_map/ppermute | solution.py:43
  66.1 6.7 %collective-permute-done.8.came_a = bf16[2,8,40,640]{3,2,1,0:T(8,128)(2,1)S(1)} collective-permute-done((bf16[2,8,40,640]{3,2,1,0:T(8,128)(2,1)S(1)}, bf16[2,8,40,640]{3,2,1,0:T(8,128)(2,1)S(1)}, u32[]{:S(2)}, u32[]{:S(2)}) %collective-permute-start.8) | collective-permute-done | bytes 819232 | tf_op jit(solution)/shard_map/ppermute | solution.py:43
  72.8 2.7 %collective-permute-done.10.came_b = bf16[2,8,40,640]{3,2,1,0:T(8,128)(2,1)S(1)} collective-permute-done((bf16[2,8,40,640]{3,2,1,0:T(8,128)(2,1)S(1)}, bf16[2,8,40,640]{3,2,1,0:T(8,128)(2,1)S(1)}, u32[]{:S(2)}, u32[]{:S(2)}) %collective-permute-start.10) | collective-permute-done | bytes 819232 | tf_op jit(solution)/shard_map/ppermute | solution.py:43
  76.2 1.1 collective-permute-start.11
  77.3 8.1 %collective-permute-done.11.last_a = bf16[8,40,640]{2,1,0:T(8,128)(2,1)S(1)} collective-permute-done((bf16[8,40,640]{2,1,0:T(8,128)(2,1)S(1)}, bf16[8,40,640]{2,1,0:T(8,128)(2,1)S(1)}, u32[]{:S(2)}, u32[]{:S(2)}) %collective-permute-start.11) | collective-permute-done | bytes 409632 | tf_op jit(solution)/shard_map/ppermute | solution.py:43
  85.9 1.0 shard_map.103
  87.8 1.1 shard_map.107
  89.0 2.2 %collective-permute-start.16 = (bf16[2,2,40,1280]{3,2,1,0:T(8,128)(2,1)S(1)}, bf16[2,2,40,1280]{3,2,1,0:T(8,128)(2,1)S(1)}, u32[]{:S(2)}, u32[]{:S(2)}) collective-permute-start(bf16[2,2,40,1280]{3,2,1,0:T(8,128)(2,1)S(1)} %get-tuple-element.107), channel_id=1, source_target_pairs={{0,24},{1,25},{2,26},{3,27},{4,28},{5,29},{6,30},{7,31},{8,16},{9,... | collective-permute-start | bytes 1228808 | tf_op jit(solution)/shard_map/ppermute | solution.py:43
  91.1 3.9 %collective-permute-done.14.came_ref.came = bf16[2,2,40,1280]{3,2,1,0:T(8,128)(2,1)S(1)} collective-permute-done((bf16[2,2,40,1280]{3,2,1,0:T(8,128)(2,1)S(1)}, bf16[2,2,40,1280]{3,2,1,0:T(8,128)(2,1)S(1)}, u32[]{:S(2)}, u32[]{:S(2)}) %collective-permute-start.14) | collective-permute-done | bytes 409632 | tf_op jit(solution)/shard_map/ppermute | solution.py:43
  95.6 2.1 %collective-permute-start.15 = (bf16[2,40,1280]{2,1,0:T(8,128)(2,1)S(1)}, bf16[2,40,1280]{2,1,0:T(8,128)(2,1)S(1)}, u32[]{:S(2)}, u32[]{:S(2)}) collective-permute-start(bf16[2,40,1280]{2,1,0:T(8,128)(2,1)S(1)} %shard_map.105), channel_id=1, source_target_pairs={{0,24},{1,25},{2,26},{3,27},{4,28},{5,29},{6,30},{7,31},{8,16},{9,... | collective-permute-start | bytes 614408 | tf_op jit(solution)/shard_map/ppermute | solution.py:43
  98.9 3.7 %collective-permute-done.15.last = bf16[2,40,1280]{2,1,0:T(8,128)(2,1)S(1)} collective-permute-done((bf16[2,40,1280]{2,1,0:T(8,128)(2,1)S(1)}, bf16[2,40,1280]{2,1,0:T(8,128)(2,1)S(1)}, u32[]{:S(2)}, u32[]{:S(2)}) %collective-permute-start.15) | collective-permute-done | bytes 204832 | tf_op jit(solution)/shard_map/ppermute | solution.py:43
  103.4 2.4 %collective-permute-start.19 = (bf16[40,1280]{1,0:T(8,128)(2,1)S(1)}, bf16[40,1280]{1,0:T(8,128)(2,1)S(1)}, u32[]{:S(2)}, u32[]{:S(2)}) collective-permute-start(bf16[40,1280]{1,0:T(8,128)(2,1)S(1)} %get-tuple-element.114), channel_id=1, source_target_pairs={{0,68},{1,69},{2,70},{3,71},{4,64},{5,65},{6,66},{7,67},{8,76},{9,... | collective-permute-start | bytes 307208 | tf_op jit(solution)/shard_map/ppermute | solution.py:43
  105.8 1.7 %collective-permute-start.20 = (bf16[40,1280]{1,0:T(8,128)(2,1)S(1)}, bf16[40,1280]{1,0:T(8,128)(2,1)S(1)}, u32[]{:S(2)}, u32[]{:S(2)}) collective-permute-start(bf16[40,1280]{1,0:T(8,128)(2,1)S(1)} %get-tuple-element.115), channel_id=1, source_target_pairs={{0,64},{1,65},{2,66},{3,67},{4,68},{5,69},{6,70},{7,71},{8,72},{9,... | collective-permute-start | bytes 307208 | tf_op jit(solution)/shard_map/ppermute | solution.py:43
  109.3 2.6 %collective-permute-done.20.far_ref = bf16[40,1280]{1,0:T(8,128)(2,1)S(1)} collective-permute-done((bf16[40,1280]{1,0:T(8,128)(2,1)S(1)}, bf16[40,1280]{1,0:T(8,128)(2,1)S(1)}, u32[]{:S(2)}, u32[]{:S(2)}) %collective-permute-start.20) | collective-permute-done | bytes 102432 | tf_op jit(solution)/shard_map/ppermute | solution.py:43
  112.9 1.2 %shard_map.111 = (f32[1,40,640]{2,1,0:T(8,128)}, f32[20,1,1280]{2,1,0:T(1,128)}) custom-call(s32[7]{0:T(128)S(1)} %stack.31.at, f32[40,1280]{1,0:T(8,128)S(1)} %get-tuple-element.119.mine_ref, bf16[40,1280]{1,0:T(8,128)(2,1)S(1)} %collective-permute-done.21.beside_ref), custom_call_target="tpu_custom_call" | custom-call | bytes 512000 | tf_op jit(solution)/shard_map/pallas_call | solution.py:64
  114.3 1.5 %shard_map.112 = (f32[1,40,2560]{2,1,0:T(8,128)}, f32[1,80,1280]{2,1,0:T(8,128)}) custom-call(s32[7]{0:T(128)S(1)} %stack.31.at, f32[2,40,1280]{2,1,0:T(8,128)S(1)} %get-tuple-element.124.high_ref, bf16[2,40,1280]{2,1,0:T(8,128)(2,1)S(1)} %collective-permute-done.22.low_ref), custom_call_target="tpu_custom_call" | custom-call | bytes 1433600 | tf_op jit(solution)/shard_map/pallas_call | solution.py:64
  (51 shorter events, 14.5 us)
Async XLA Ops:
  0.7 23.0 %copy-start.3 = (s32[4,8]{1,0:T(4,128)S(1)}, s32[4,8]{1,0:T(4,128)}, u32[]{:S(2)}) copy-start(s32[4,8]{1,0:T(4,128)} %param.11) | copy-start | bytes 388
  11.9 20.0 %collective-permute-start.2 = (bf16[1792,1280]{1,0:T(8,128)(2,1)}, bf16[1792,1280]{1,0:T(8,128)(2,1)}, u32[]{:S(2)}, u32[]{:S(2)}) collective-permute-start(bf16[1792,1280]{1,0:T(8,128)(2,1)} %get-tuple-element.69.hand_hbm), channel_id=1, source_target_pairs={{0,32},{1,33},{2,34},{3,35},{4,36},{5,37},{6,38},{7,39},{8,40},{9,... | collective-permute-start | bytes 13762568 | tf_op jit(solution)/shard_map/ppermute | solution.py:43
  12.0 11.8 %collective-permute-start = (bf16[256,1280]{1,0:T(8,128)(2,1)S(1)}, bf16[256,1280]{1,0:T(8,128)(2,1)S(1)}, u32[]{:S(2)}, u32[]{:S(2)}) collective-permute-start(bf16[256,1280]{1,0:T(8,128)(2,1)S(1)} %get-tuple-element.67.own_ref), channel_id=1, source_target_pairs={{96,36},{97,37},{98,38},{99,39},{100,32},{101,33},{102,34},{103,35... | collective-permute-start | bytes 1966088 | tf_op jit(solution)/shard_map/ppermute | solution.py:43
  12.7 23.0 %all-to-all-start = ((bf16[32,8,1280]{2,1,0:T(8,128)(2,1)}), bf16[32,8,1280]{2,1,0:T(8,128)(2,1)S(1)}, u32[]{:S(2)}, u32[]{:S(2)}) async-start(bf16[32,8,1280]{2,1,0:T(8,128)(2,1)} %bitcast.9), calls=%async_computation | async-start | bytes 1310720 | tf_op jit(solution)/shard_map/all_to_all | solution.py:695
  21.9 20.4 %collective-permute-start.5 = (bf16[256,2560]{1,0:T(8,128)(2,1)}, bf16[256,2560]{1,0:T(8,128)(2,1)}, u32[]{:S(2)}, u32[]{:S(2)}) collective-permute-start(bf16[256,2560]{1,0:T(8,128)(2,1)} %get-tuple-element.81), channel_id=1, source_target_pairs={{96,36},{97,37},{98,38},{99,39},{100,32},{101,33},{102,34},{103,35... | collective-permute-start | bytes 3932168 | tf_op jit(solution)/shard_map/ppermute | solution.py:43
  24.3 3.1 %collective-permute-start.1 = (bf16[256,1280]{1,0:T(8,128)(2,1)S(1)}, bf16[256,1280]{1,0:T(8,128)(2,1)S(1)}, u32[]{:S(2)}, u32[]{:S(2)}) collective-permute-start(bf16[256,1280]{1,0:T(8,128)(2,1)S(1)} %shard_map.94.shared_ref), channel_id=1, source_target_pairs={{0,32},{1,33},{2,34},{3,35},{4,36},{5,37},{6,38},{7,39},{8,40},{9,... | collective-permute-start | bytes 1966088 | tf_op jit(solution)/shard_map/ppermute | solution.py:43
  31.2 0.7 copy-start
  35.6 4.0 %copy-start.1 = (bf16[256,640]{1,0:T(8,128)(2,1)S(1)}, bf16[256,640]{1,0:T(8,128)(2,1)}, u32[]{:S(2)}) copy-start(bf16[256,640]{1,0:T(8,128)(2,1)} %copy-done) | copy-start | bytes 983044
  39.6 2.1 %collective-permute-start.3 = (bf16[128,1280]{1,0:T(8,128)(2,1)S(1)}, bf16[128,1280]{1,0:T(8,128)(2,1)S(1)}, u32[]{:S(2)}, u32[]{:S(2)}) collective-permute-start(bf16[128,1280]{1,0:T(8,128)(2,1)S(1)} %get-tuple-element.72), channel_id=1, source_target_pairs={{0,32},{1,33},{2,34},{3,35},{4,36},{5,37},{6,38},{7,39},{8,40},{9,... | collective-permute-start | bytes 983048 | tf_op jit(solution)/shard_map/ppermute | solution.py:43
  42.4 4.5 %collective-permute-start.6 = (bf16[256,2560]{1,0:T(8,128)(2,1)}, bf16[256,2560]{1,0:T(8,128)(2,1)S(1)}, u32[]{:S(2)}, u32[]{:S(2)}) collective-permute-start(bf16[256,2560]{1,0:T(8,128)(2,1)} %collective-permute-done.5.crossed_hbm), channel_id=1, source_target_pairs={{0,32},{1,33},{2,34},{3,35},{4,36},{5,37},{6,38},{7,39},{8,40},{9,... | collective-permute-start | bytes 3932168 | tf_op jit(solution)/shard_map/ppermute | solution.py:43
  42.9 22.3 %collective-permute-start.9 = (bf16[2,8,40,1280]{3,2,1,0:T(8,128)(2,1)S(1)}, bf16[2,8,40,1280]{3,2,1,0:T(8,128)(2,1)S(1)}, u32[]{:S(2)}, u32[]{:S(2)}) collective-permute-start(bf16[2,8,40,1280]{3,2,1,0:T(8,128)(2,1)S(1)} %get-tuple-element.94), channel_id=1, source_target_pairs={{0,3},{1,2},{2,1},{3,0},{4,7},{5,6},{6,5},{7,4},{8,11},{9,10},{10,... | collective-permute-start | bytes 4915208 | tf_op jit(solution)/shard_map/ppermute | solution.py:43
  45.3 10.6 %collective-permute-start.4 = (bf16[128,1280]{1,0:T(8,128)(2,1)S(1)}, bf16[128,1280]{1,0:T(8,128)(2,1)S(1)}, u32[]{:S(2)}, u32[]{:S(2)}) collective-permute-start(bf16[128,1280]{1,0:T(8,128)(2,1)S(1)} %get-tuple-element.79), channel_id=1, source_target_pairs={{0,68},{1,69},{2,70},{3,71},{4,64},{5,65},{6,66},{7,67},{8,76},{9,... | collective-permute-start | bytes 983048 | tf_op jit(solution)/shard_map/ppermute | solution.py:43
  46.8 1.0 copy-start.2
  56.5 1.7 %collective-permute-start.7 = (bf16[128,1280]{1,0:T(8,128)(2,1)S(1)}, bf16[128,1280]{1,0:T(8,128)(2,1)S(1)}, u32[]{:S(2)}, u32[]{:S(2)}) collective-permute-start(bf16[128,1280]{1,0:T(8,128)(2,1)S(1)} %shard_map.100.mine_ref), channel_id=1, source_target_pairs={{0,32},{1,33},{2,34},{3,35},{4,36},{5,37},{6,38},{7,39},{8,40},{9,... | collective-permute-start | bytes 983048 | tf_op jit(solution)/shard_map/ppermute | solution.py:43
  60.3 12.4 %collective-permute-start.8 = (bf16[2,8,40,640]{3,2,1,0:T(8,128)(2,1)S(1)}, bf16[2,8,40,640]{3,2,1,0:T(8,128)(2,1)S(1)}, u32[]{:S(2)}, u32[]{:S(2)}) collective-permute-start(bf16[2,8,40,640]{3,2,1,0:T(8,128)(2,1)S(1)} %get-tuple-element.92), channel_id=1, source_target_pairs={{0,1},{1,0},{2,3},{3,2},{4,5},{5,4},{6,7},{7,6},{8,9},{9,8},{10,11... | collective-permute-start | bytes 2457608 | tf_op jit(solution)/shard_map/ppermute | solution.py:43
  61.9 13.6 %collective-permute-start.10 = (bf16[2,8,40,640]{3,2,1,0:T(8,128)(2,1)S(1)}, bf16[2,8,40,640]{3,2,1,0:T(8,128)(2,1)S(1)}, u32[]{:S(2)}, u32[]{:S(2)}) collective-permute-start(bf16[2,8,40,640]{3,2,1,0:T(8,128)(2,1)S(1)} %get-tuple-element.96), channel_id=1, source_target_pairs={{0,3},{1,2},{2,1},{3,0},{4,7},{5,6},{6,5},{7,4},{8,11},{9,10},{10,... | collective-permute-start | bytes 2457608 | tf_op jit(solution)/shard_map/ppermute | solution.py:43
  66.0 21.8 %collective-permute-start.13 = (bf16[8,40,1280]{2,1,0:T(8,128)(2,1)S(1)}, bf16[8,40,1280]{2,1,0:T(8,128)(2,1)S(1)}, u32[]{:S(2)}, u32[]{:S(2)}) collective-permute-start(bf16[8,40,1280]{2,1,0:T(8,128)(2,1)S(1)} %shard_map.104), channel_id=1, source_target_pairs={{0,1},{1,0},{2,3},{3,2},{4,5},{5,4},{6,7},{7,6},{8,9},{9,8},{10,11... | collective-permute-start | bytes 2457608 | tf_op jit(solution)/shard_map/ppermute | solution.py:43
  76.2 9.2 %collective-permute-start.11 = (bf16[8,40,640]{2,1,0:T(8,128)(2,1)S(1)}, bf16[8,40,640]{2,1,0:T(8,128)(2,1)S(1)}, u32[]{:S(2)}, u32[]{:S(2)}) collective-permute-start(bf16[8,40,640]{2,1,0:T(8,128)(2,1)S(1)} %get-tuple-element.97), channel_id=1, source_target_pairs={{0,3},{1,2},{2,1},{3,0},{4,7},{5,6},{6,5},{7,4},{8,11},{9,10},{10,... | collective-permute-start | bytes 1228808 | tf_op jit(solution)/shard_map/ppermute | solution.py:43
  77.3 8.7 %collective-permute-start.12 = (bf16[8,40,640]{2,1,0:T(8,128)(2,1)S(1)}, bf16[8,40,640]{2,1,0:T(8,128)(2,1)S(1)}, u32[]{:S(2)}, u32[]{:S(2)}) collective-permute-start(bf16[8,40,640]{2,1,0:T(8,128)(2,1)S(1)} %get-tuple-element.98), channel_id=1, source_target_pairs={{0,1},{1,0},{2,3},{3,2},{4,5},{5,4},{6,7},{7,6},{8,9},{9,8},{10,11... | collective-permute-start | bytes 1228808 | tf_op jit(solution)/shard_map/ppermute | solution.py:43
  87.0 8.0 %collective-permute-start.14 = (bf16[2,2,40,1280]{3,2,1,0:T(8,128)(2,1)S(1)}, bf16[2,2,40,1280]{3,2,1,0:T(8,128)(2,1)S(1)}, u32[]{:S(2)}, u32[]{:S(2)}) collective-permute-start(bf16[2,2,40,1280]{3,2,1,0:T(8,128)(2,1)S(1)} %get-tuple-element.103), channel_id=1, source_target_pairs={{0,8},{1,9},{2,10},{3,11},{4,12},{5,13},{6,14},{7,15},{8,0},{9,1},... | collective-permute-start | bytes 1228808 | tf_op jit(solution)/shard_map/ppermute | solution.py:43
  89.0 9.2 %collective-permute-start.16 = (bf16[2,2,40,1280]{3,2,1,0:T(8,128)(2,1)S(1)}, bf16[2,2,40,1280]{3,2,1,0:T(8,128)(2,1)S(1)}, u32[]{:S(2)}, u32[]{:S(2)}) collective-permute-start(bf16[2,2,40,1280]{3,2,1,0:T(8,128)(2,1)S(1)} %get-tuple-element.107), channel_id=1, source_target_pairs={{0,24},{1,25},{2,26},{3,27},{4,28},{5,29},{6,30},{7,31},{8,16},{9,... | collective-permute-start | bytes 1228808 | tf_op jit(solution)/shard_map/ppermute | solution.py:43
  95.6 7.0 %collective-permute-start.15 = (bf16[2,40,1280]{2,1,0:T(8,128)(2,1)S(1)}, bf16[2,40,1280]{2,1,0:T(8,128)(2,1)S(1)}, u32[]{:S(2)}, u32[]{:S(2)}) collective-permute-start(bf16[2,40,1280]{2,1,0:T(8,128)(2,1)S(1)} %shard_map.105), channel_id=1, source_target_pairs={{0,24},{1,25},{2,26},{3,27},{4,28},{5,29},{6,30},{7,31},{8,16},{9,... | collective-permute-start | bytes 614408 | tf_op jit(solution)/shard_map/ppermute | solution.py:43
  98.8 8.7 %collective-permute-start.17 = (bf16[2,40,1280]{2,1,0:T(8,128)(2,1)S(1)}, bf16[2,40,1280]{2,1,0:T(8,128)(2,1)S(1)}, u32[]{:S(2)}, u32[]{:S(2)}) collective-permute-start(bf16[2,40,1280]{2,1,0:T(8,128)(2,1)S(1)} %shard_map.108), channel_id=1, source_target_pairs={{0,8},{1,9},{2,10},{3,11},{4,12},{5,13},{6,14},{7,15},{8,0},{9,1},... | collective-permute-start | bytes 614408 | tf_op jit(solution)/shard_map/ppermute | solution.py:43
  103.3 5.5 %collective-permute-start.18 = (bf16[40,1280]{1,0:T(8,128)(2,1)S(1)}, bf16[40,1280]{1,0:T(8,128)(2,1)S(1)}, u32[]{:S(2)}, u32[]{:S(2)}) collective-permute-start(bf16[40,1280]{1,0:T(8,128)(2,1)S(1)} %get-tuple-element.110), channel_id=1, source_target_pairs={{0,4},{1,5},{2,6},{3,7},{4,0},{5,1},{6,2},{7,3},{8,12},{9,13},{10,... | collective-permute-start | bytes 307208 | tf_op jit(solution)/shard_map/ppermute | solution.py:43
  103.4 6.0 %collective-permute-start.19 = (bf16[40,1280]{1,0:T(8,128)(2,1)S(1)}, bf16[40,1280]{1,0:T(8,128)(2,1)S(1)}, u32[]{:S(2)}, u32[]{:S(2)}) collective-permute-start(bf16[40,1280]{1,0:T(8,128)(2,1)S(1)} %get-tuple-element.114), channel_id=1, source_target_pairs={{0,68},{1,69},{2,70},{3,71},{4,64},{5,65},{6,66},{7,67},{8,76},{9,... | collective-permute-start | bytes 307208 | tf_op jit(solution)/shard_map/ppermute | solution.py:43
  105.8 6.2 %collective-permute-start.20 = (bf16[40,1280]{1,0:T(8,128)(2,1)S(1)}, bf16[40,1280]{1,0:T(8,128)(2,1)S(1)}, u32[]{:S(2)}, u32[]{:S(2)}) collective-permute-start(bf16[40,1280]{1,0:T(8,128)(2,1)S(1)} %get-tuple-element.115), channel_id=1, source_target_pairs={{0,64},{1,65},{2,66},{3,67},{4,68},{5,69},{6,70},{7,71},{8,72},{9,... | collective-permute-start | bytes 307208 | tf_op jit(solution)/shard_map/ppermute | solution.py:43
  108.1 4.7 %collective-permute-start.21 = (bf16[40,1280]{1,0:T(8,128)(2,1)S(1)}, bf16[40,1280]{1,0:T(8,128)(2,1)S(1)}, u32[]{:S(2)}, u32[]{:S(2)}) collective-permute-start(bf16[40,1280]{1,0:T(8,128)(2,1)S(1)} %get-tuple-element.117), channel_id=1, source_target_pairs={{0,4},{1,5},{2,6},{3,7},{4,0},{5,1},{6,2},{7,3},{8,12},{9,13},{10,... | collective-permute-start | bytes 307208 | tf_op jit(solution)/shard_map/ppermute | solution.py:43
  112.9 1.5 %collective-permute-start.22 = (bf16[2,40,1280]{2,1,0:T(8,128)(2,1)S(1)}, bf16[2,40,1280]{2,1,0:T(8,128)(2,1)S(1)}, u32[]{:S(2)}, u32[]{:S(2)}) collective-permute-start(bf16[2,40,1280]{2,1,0:T(8,128)(2,1)S(1)} %get-tuple-element.118), channel_id=1, source_target_pairs={{0,32},{1,33},{2,34},{3,35},{4,36},{5,37},{6,38},{7,39},{8,40},{9,... | collective-permute-start | bytes 614408 | tf_op jit(solution)/shard_map/ppermute | solution.py:43

commit v5 on v4

--- a/solution.py
+++ b/solution.py
@@ -93,7 +93,8 @@
     return point * share, slope
 
 
-CHUNK = 512
+CHUNK = 256
+AHEAD = 3
 
 
 def forward_kernel(
@@ -141,9 +142,9 @@
         normed_ref, hand_hbm.at[pl.ds(width, tokens)], other_sem.at[1]
     )
     acts_copy.start()
-    first_copy(0).start()
-    second_copy(0).start()
-    first_copy(1).start()
+    for j in range(AHEAD):
+        first_copy(j).start()
+        second_copy(j).start()
     acts_copy.wait()
     values = acts_ref[...].astype(F32)
     center = values - jnp.mean(values, axis=-1, keepdims=True)
@@ -155,10 +156,9 @@
     first_copy(0).wait()
     before = jnp.dot(normed, first_ref[0], preferred_element_type=F32)
     for j in range(count):
-        if j + 1 < count:
-            second_copy(j + 1).start()
-        if j + 2 < count:
-            first_copy(j + 2).start()
+        if j + AHEAD < count:
+            first_copy(j + AHEAD).start()
+            second_copy(j + AHEAD).start()
         second_copy(j).wait()
         if j * CHUNK < width:
             weight_copy(j).start()

time: 117 us -> 118 us (level)
  no operation moved by 1% of the time
where the time goes in v5:
time: 118 us; the launch traced here: 116 us
  waiting for transfers between devices  45.8 us (39%)
  Pallas kernels  36.3 us (31%)
  starting transfers between devices  30.9 us (26%)
  local copies, waits for them, and re-layouts  1.87 us (2%)
    ppermute x23, waiting for transfers between devices, send(): return lax.ppermute(value, ALL, route(move))  42.1 us
    ppermute x23, starting transfers between devices, send(): return lax.ppermute(value, ALL, route(move))  21.7 us
    pallas_call x16, Pallas kernels, call(): pl.pallas_call(kernel, out_shape=list(outputs), in_specs=[smem()] + vmem(...  15.3 us
    pallas_call x1, Pallas kernels, block_forward(): pl.pallas_call(forward_kernel, out_shape=[pltpu.HBM((tokens, hidden), BF1...  11.4 us
    all_to_all x1, starting transfers between devices, body(): lax.all_to_all(outgoing, WIDE, split_axis=0, concat_axis=0, tiled=True)  9.27 us
    pallas_call x2, Pallas kernels, adapt_call(): pl.pallas_call(kernel, out_shape=list(outputs), in_specs=[smem()] + vmem(...  7.69 us
    all_to_all x1, waiting for transfers between devices, body(): lax.all_to_all(outgoing, WIDE, split_axis=0, concat_axis=0, tiled=True)  3.75 us
  transfers between devices with their start and end apart: 24, of which 17 were waited for; matrix products, arithmetic and copies ran while one was open for 0% of the time, Pallas kernels for 20%

profile of v5, /device:TPU:0, one launch (start us, length us, event | category | flops | bytes accessed | tf_op | source)
XLA Modules:
  0.0 116.1 jit_solution(13811424490850871074)
XLA Ops:
  0.7 11.4 %shard_map.93 = (bf16[256,2560]{1,0:T(8,128)(2,1)}, bf16[1792,1280]{1,0:T(8,128)(2,1)}, bf16[256,1280]{1,0:T(8,128)(2,1)}, bf16[256,1280]{1,0:T(8,128)(2,1)S(1)}, bf16[256,1280]{1,0:T(8,128)(2,1)}) custom-call(s32[7]{0:T(128)S(1)} %stack.31.at, bf16[1,256,1280]{2,1,0:T(8,128)(2,1)} %acts_hbm.1, bf16[1,1280,2560]{2,1,0:T(8,128)(2,1)} %first_hbm.3, ...), custom_call_target="tpu_custom_call" | custom-call | flops 3355443200 | bytes 16777216 | tf_op jit(solution)/shard_map/pallas_call | solution.py:199
  13.0 9.3 %all-to-all-start = ((bf16[32,8,1280]{2,1,0:T(8,128)(2,1)}), bf16[32,8,1280]{2,1,0:T(8,128)(2,1)S(1)}, u32[]{:S(2)}, u32[]{:S(2)}) async-start(bf16[32,8,1280]{2,1,0:T(8,128)(2,1)} %bitcast.9), calls=%async_computation | async-start | bytes 1310720 | tf_op jit(solution)/shard_map/all_to_all | solution.py:695
  22.3 1.7 %collective-permute-start.5 = (bf16[256,2560]{1,0:T(8,128)(2,1)}, bf16[256,2560]{1,0:T(8,128)(2,1)}, u32[]{:S(2)}, u32[]{:S(2)}) collective-permute-start(bf16[256,2560]{1,0:T(8,128)(2,1)} %get-tuple-element.81), channel_id=1, source_target_pairs={{96,36},{97,37},{98,38},{99,39},{100,32},{101,33},{102,34},{103,35... | collective-permute-start | bytes 3932168 | tf_op jit(solution)/shard_map/ppermute | solution.py:43
  24.6 1.3 %collective-permute-start.1 = (bf16[256,1280]{1,0:T(8,128)(2,1)S(1)}, bf16[256,1280]{1,0:T(8,128)(2,1)S(1)}, u32[]{:S(2)}, u32[]{:S(2)}) collective-permute-start(bf16[256,1280]{1,0:T(8,128)(2,1)S(1)} %shard_map.94.shared_ref), channel_id=1, source_target_pairs={{0,32},{1,33},{2,34},{3,35},{4,36},{5,37},{6,38},{7,39},{8,40},{9,... | collective-permute-start | bytes 1966088 | tf_op jit(solution)/shard_map/ppermute | solution.py:43
  26.2 1.5 %collective-permute-done.1.handed_ref = bf16[256,1280]{1,0:T(8,128)(2,1)S(1)} collective-permute-done((bf16[256,1280]{1,0:T(8,128)(2,1)S(1)}, bf16[256,1280]{1,0:T(8,128)(2,1)S(1)}, u32[]{:S(2)}, u32[]{:S(2)}) %collective-permute-start.1) | collective-permute-done | bytes 655392 | tf_op jit(solution)/shard_map/ppermute | solution.py:43
  27.7 3.8 %shard_map.95 = (bf16[256,1280]{1,0:T(8,128)(2,1)S(1)}, bf16[256,640]{1,0:T(8,128)(2,1)S(1)}, f32[256,1920]{1,0:T(8,128)S(1)}) custom-call(s32[7]{0:T(128)S(1)} %stack.31.at, bf16[256,1280]{1,0:T(8,128)(2,1)S(1)} %shard_map.94.shared_ref, bf16[256,1280]{1,0:T(8,128)(2,1)S(1)} %collective-permute-done.1.handed_ref, bf16[3,1280,640]{2,1,0:T(8,128)(2,1)} %first_hbm.5, ...), custom_call_target="tpu_custom_call" | custom-call | flops 1024 | bytes 1024 | tf_op jit(solution)/shard_map/pallas_call | solution.py:269
  32.2 3.8 %all-to-all-done = bf16[32,8,1280]{2,1,0:T(8,128)(2,1)S(1)} async-done(((bf16[32,8,1280]{2,1,0:T(8,128)(2,1)}), bf16[32,8,1280]{2,1,0:T(8,128)(2,1)S(1)}, u32[]{:S(2)}, u32[]{:S(2)}) %all-to-all-start) | async-done | bytes 655392 | tf_op jit(solution)/shard_map/all_to_all | solution.py:695
  35.9 3.9 %shard_map.96 = (bf16[256,1280]{1,0:T(8,128)(2,1)S(1)}, bf16[256,640]{1,0:T(8,128)(2,1)S(1)}, f32[128,1280]{1,0:T(8,128)S(1)}, bf16[128,1280]{1,0:T(8,128)(2,1)S(1)}) custom-call(s32[7]{0:T(128)S(1)} %stack.31.at, bf16[256,256]{1,0:T(8,128)(2,1)S(1)} %and_convert_fusion.sorter_ref, bf16[256,1280]{1,0:T(8,128)(2,1)S(1)} %bitcast.14, ...), custom_call_target="tpu_custom_call" | custom-call | flops 1024 | bytes 1024 | tf_op jit(solution)/shard_map/pallas_call | solution.py:269
  40.2 2.0 %shard_map.97 = (bf16[2,8,40,1280]{3,2,1,0:T(8,128)(2,1)S(1)}, bf16[2,8,40,1280]{3,2,1,0:T(8,128)(2,1)S(1)}) custom-call(s32[7]{0:T(128)S(1)} %stack.31.at, bf16[256,1280]{1,0:T(8,128)(2,1)S(1)} %get-tuple-element.73.student_ref, bf16[256,640]{1,0:T(8,128)(2,1)S(1)} %get-tuple-element.74.grad_zeta_ref, bf16[256,640]{1,0:T(8,128)(2,1)S(1)} %copy-done.1, ...), custom_call_target="tpu_custom_call" | custom-call | flops 838860800 | bytes 5242880 | tf_op jit(solution)/shard_map/pallas_call | solution.py:64
  43.4 2.2 %collective-permute-start.9 = (bf16[2,8,40,1280]{3,2,1,0:T(8,128)(2,1)S(1)}, bf16[2,8,40,1280]{3,2,1,0:T(8,128)(2,1)S(1)}, u32[]{:S(2)}, u32[]{:S(2)}) collective-permute-start(bf16[2,8,40,1280]{3,2,1,0:T(8,128)(2,1)S(1)} %get-tuple-element.94), channel_id=1, source_target_pairs={{0,3},{1,2},{2,1},{3,0},{4,7},{5,6},{6,5},{7,4},{8,11},{9,10},{10,... | collective-permute-start | bytes 4915208 | tf_op jit(solution)/shard_map/ppermute | solution.py:43
  45.7 1.7 %collective-permute-start.4 = (bf16[128,1280]{1,0:T(8,128)(2,1)S(1)}, bf16[128,1280]{1,0:T(8,128)(2,1)S(1)}, u32[]{:S(2)}, u32[]{:S(2)}) collective-permute-start(bf16[128,1280]{1,0:T(8,128)(2,1)S(1)} %get-tuple-element.79), channel_id=1, source_target_pairs={{0,68},{1,69},{2,70},{3,71},{4,64},{5,65},{6,66},{7,67},{8,76},{9,... | collective-permute-start | bytes 983048 | tf_op jit(solution)/shard_map/ppermute | solution.py:43
  48.4 1.9 %shard_map.99 = (bf16[256,2560]{1,0:T(8,128)(2,1)S(1)}, bf16[256,1280]{1,0:T(8,128)(2,1)S(1)}, bf16[1280,1280]{1,0:T(8,128)(2,1)S(1)}) custom-call(s32[7]{0:T(128)S(1)} %stack.31.at, bf16[256,2560]{1,0:T(8,128)(2,1)} %collective-permute-done.5.crossed_hbm, bf16[256,2560]{1,0:T(8,128)(2,1)} %copy-done.2, bf16[1792,1280]{1,0:T(8,128)(2,1)} %get-tuple-element.69.hand_hbm, ...), custom_call_target="tpu_custom_call" | custom-call | bytes 8388608 | tf_op jit(solution)/shard_map/pallas_call | solution.py:398
  50.3 6.0 %collective-permute-done.4.across_ref = bf16[128,1280]{1,0:T(8,128)(2,1)S(1)} collective-permute-done((bf16[128,1280]{1,0:T(8,128)(2,1)S(1)}, bf16[128,1280]{1,0:T(8,128)(2,1)S(1)}, u32[]{:S(2)}, u32[]{:S(2)}) %collective-permute-start.4) | collective-permute-done | bytes 327712 | tf_op jit(solution)/shard_map/ppermute | solution.py:43
  56.9 1.6 %collective-permute-done.7.other_ref = bf16[128,1280]{1,0:T(8,128)(2,1)S(1)} collective-permute-done((bf16[128,1280]{1,0:T(8,128)(2,1)S(1)}, bf16[128,1280]{1,0:T(8,128)(2,1)S(1)}, u32[]{:S(2)}, u32[]{:S(2)}) %collective-permute-start.7) | collective-permute-done | bytes 327712 | tf_op jit(solution)/shard_map/ppermute | solution.py:43
  58.6 2.1 %shard_map.101 = (bf16[2,8,40,640]{3,2,1,0:T(8,128)(2,1)S(1)}, bf16[2,8,40,640]{3,2,1,0:T(8,128)(2,1)S(1)}, bf16[2,8,40,640]{3,2,1,0:T(8,128)(2,1)S(1)}, bf16[2,8,40,640]{3,2,1,0:T(8,128)(2,1)S(1)}) custom-call(s32[7]{0:T(128)S(1)} %stack.31.at, bf16[256,2560]{1,0:T(8,128)(2,1)S(1)} %get-tuple-element.86.left, ...), custom_call_target="tpu_custom_call" | custom-call | flops 1677721600 | bytes 9175040 | tf_op jit(solution)/shard_map/pallas_call | solution.py:64
  60.6 1.5 %collective-permute-start.8 = (bf16[2,8,40,640]{3,2,1,0:T(8,128)(2,1)S(1)}, bf16[2,8,40,640]{3,2,1,0:T(8,128)(2,1)S(1)}, u32[]{:S(2)}, u32[]{:S(2)}) collective-permute-start(bf16[2,8,40,640]{3,2,1,0:T(8,128)(2,1)S(1)} %get-tuple-element.92), channel_id=1, source_target_pairs={{0,1},{1,0},{2,3},{3,2},{4,5},{5,4},{6,7},{7,6},{8,9},{9,8},{10,11... | collective-permute-start | bytes 2457608 | tf_op jit(solution)/shard_map/ppermute | solution.py:43
  62.8 2.9 %collective-permute-done.9.came_ref = bf16[2,8,40,1280]{3,2,1,0:T(8,128)(2,1)S(1)} collective-permute-done((bf16[2,8,40,1280]{3,2,1,0:T(8,128)(2,1)S(1)}, bf16[2,8,40,1280]{3,2,1,0:T(8,128)(2,1)S(1)}, u32[]{:S(2)}, u32[]{:S(2)}) %collective-permute-start.9) | collective-permute-done | bytes 1638432 | tf_op jit(solution)/shard_map/ppermute | solution.py:43
  66.6 6.5 %collective-permute-done.8.came_a = bf16[2,8,40,640]{3,2,1,0:T(8,128)(2,1)S(1)} collective-permute-done((bf16[2,8,40,640]{3,2,1,0:T(8,128)(2,1)S(1)}, bf16[2,8,40,640]{3,2,1,0:T(8,128)(2,1)S(1)}, u32[]{:S(2)}, u32[]{:S(2)}) %collective-permute-start.8) | collective-permute-done | bytes 819232 | tf_op jit(solution)/shard_map/ppermute | solution.py:43
  73.1 2.6 %collective-permute-done.10.came_b = bf16[2,8,40,640]{3,2,1,0:T(8,128)(2,1)S(1)} collective-permute-done((bf16[2,8,40,640]{3,2,1,0:T(8,128)(2,1)S(1)}, bf16[2,8,40,640]{3,2,1,0:T(8,128)(2,1)S(1)}, u32[]{:S(2)}, u32[]{:S(2)}) %collective-permute-start.10) | collective-permute-done | bytes 819232 | tf_op jit(solution)/shard_map/ppermute | solution.py:43
  76.5 1.1 collective-permute-start.11
  77.6 8.1 %collective-permute-done.11.last_a = bf16[8,40,640]{2,1,0:T(8,128)(2,1)S(1)} collective-permute-done((bf16[8,40,640]{2,1,0:T(8,128)(2,1)S(1)}, bf16[8,40,640]{2,1,0:T(8,128)(2,1)S(1)}, u32[]{:S(2)}, u32[]{:S(2)}) %collective-permute-start.11) | collective-permute-done | bytes 409632 | tf_op jit(solution)/shard_map/ppermute | solution.py:43
  86.2 1.0 shard_map.103
  88.1 1.1 shard_map.107
  89.3 2.2 %collective-permute-start.16 = (bf16[2,2,40,1280]{3,2,1,0:T(8,128)(2,1)S(1)}, bf16[2,2,40,1280]{3,2,1,0:T(8,128)(2,1)S(1)}, u32[]{:S(2)}, u32[]{:S(2)}) collective-permute-start(bf16[2,2,40,1280]{3,2,1,0:T(8,128)(2,1)S(1)} %get-tuple-element.107), channel_id=1, source_target_pairs={{0,24},{1,25},{2,26},{3,27},{4,28},{5,29},{6,30},{7,31},{8,16},{9,... | collective-permute-start | bytes 1228808 | tf_op jit(solution)/shard_map/ppermute | solution.py:43
  91.4 3.9 %collective-permute-done.14.came_ref.came = bf16[2,2,40,1280]{3,2,1,0:T(8,128)(2,1)S(1)} collective-permute-done((bf16[2,2,40,1280]{3,2,1,0:T(8,128)(2,1)S(1)}, bf16[2,2,40,1280]{3,2,1,0:T(8,128)(2,1)S(1)}, u32[]{:S(2)}, u32[]{:S(2)}) %collective-permute-start.14) | collective-permute-done | bytes 409632 | tf_op jit(solution)/shard_map/ppermute | solution.py:43
  95.9 2.1 %collective-permute-start.15 = (bf16[2,40,1280]{2,1,0:T(8,128)(2,1)S(1)}, bf16[2,40,1280]{2,1,0:T(8,128)(2,1)S(1)}, u32[]{:S(2)}, u32[]{:S(2)}) collective-permute-start(bf16[2,40,1280]{2,1,0:T(8,128)(2,1)S(1)} %shard_map.105), channel_id=1, source_target_pairs={{0,24},{1,25},{2,26},{3,27},{4,28},{5,29},{6,30},{7,31},{8,16},{9,... | collective-permute-start | bytes 614408 | tf_op jit(solution)/shard_map/ppermute | solution.py:43
  99.2 3.7 %collective-permute-done.15.last = bf16[2,40,1280]{2,1,0:T(8,128)(2,1)S(1)} collective-permute-done((bf16[2,40,1280]{2,1,0:T(8,128)(2,1)S(1)}, bf16[2,40,1280]{2,1,0:T(8,128)(2,1)S(1)}, u32[]{:S(2)}, u32[]{:S(2)}) %collective-permute-start.15) | collective-permute-done | bytes 204832 | tf_op jit(solution)/shard_map/ppermute | solution.py:43
  103.7 2.5 %collective-permute-start.19 = (bf16[40,1280]{1,0:T(8,128)(2,1)S(1)}, bf16[40,1280]{1,0:T(8,128)(2,1)S(1)}, u32[]{:S(2)}, u32[]{:S(2)}) collective-permute-start(bf16[40,1280]{1,0:T(8,128)(2,1)S(1)} %get-tuple-element.114), channel_id=1, source_target_pairs={{0,68},{1,69},{2,70},{3,71},{4,64},{5,65},{6,66},{7,67},{8,76},{9,... | collective-permute-start | bytes 307208 | tf_op jit(solution)/shard_map/ppermute | solution.py:43
  106.3 1.5 %collective-permute-start.20 = (bf16[40,1280]{1,0:T(8,128)(2,1)S(1)}, bf16[40,1280]{1,0:T(8,128)(2,1)S(1)}, u32[]{:S(2)}, u32[]{:S(2)}) collective-permute-start(bf16[40,1280]{1,0:T(8,128)(2,1)S(1)} %get-tuple-element.115), channel_id=1, source_target_pairs={{0,64},{1,65},{2,66},{3,67},{4,68},{5,69},{6,70},{7,71},{8,72},{9,... | collective-permute-start | bytes 307208 | tf_op jit(solution)/shard_map/ppermute | solution.py:43
  109.7 2.8 %collective-permute-done.20.far_ref = bf16[40,1280]{1,0:T(8,128)(2,1)S(1)} collective-permute-done((bf16[40,1280]{1,0:T(8,128)(2,1)S(1)}, bf16[40,1280]{1,0:T(8,128)(2,1)S(1)}, u32[]{:S(2)}, u32[]{:S(2)}) %collective-permute-start.20) | collective-permute-done | bytes 102432 | tf_op jit(solution)/shard_map/ppermute | solution.py:43
  113.2 1.2 %shard_map.111 = (f32[1,40,640]{2,1,0:T(8,128)}, f32[20,1,1280]{2,1,0:T(1,128)}) custom-call(s32[7]{0:T(128)S(1)} %stack.31.at, f32[40,1280]{1,0:T(8,128)S(1)} %get-tuple-element.119.mine_ref, bf16[40,1280]{1,0:T(8,128)(2,1)S(1)} %collective-permute-done.21.beside_ref), custom_call_target="tpu_custom_call" | custom-call | bytes 512000 | tf_op jit(solution)/shard_map/pallas_call | solution.py:64
  114.6 1.5 %shard_map.112 = (f32[1,40,2560]{2,1,0:T(8,128)}, f32[1,80,1280]{2,1,0:T(8,128)}) custom-call(s32[7]{0:T(128)S(1)} %stack.31.at, f32[2,40,1280]{2,1,0:T(8,128)S(1)} %get-tuple-element.124.high_ref, bf16[2,40,1280]{2,1,0:T(8,128)(2,1)S(1)} %collective-permute-done.22.low_ref), custom_call_target="tpu_custom_call" | custom-call | bytes 1433600 | tf_op jit(solution)/shard_map/pallas_call | solution.py:64
  (51 shorter events, 14.6 us)
Async XLA Ops:
  0.7 23.3 %copy-start.3 = (s32[4,8]{1,0:T(4,128)S(1)}, s32[4,8]{1,0:T(4,128)}, u32[]{:S(2)}) copy-start(s32[4,8]{1,0:T(4,128)} %param.11) | copy-start | bytes 388
  12.2 20.0 %collective-permute-start.2 = (bf16[1792,1280]{1,0:T(8,128)(2,1)}, bf16[1792,1280]{1,0:T(8,128)(2,1)}, u32[]{:S(2)}, u32[]{:S(2)}) collective-permute-start(bf16[1792,1280]{1,0:T(8,128)(2,1)} %get-tuple-element.69.hand_hbm), channel_id=1, source_target_pairs={{0,32},{1,33},{2,34},{3,35},{4,36},{5,37},{6,38},{7,39},{8,40},{9,... | collective-permute-start | bytes 13762568 | tf_op jit(solution)/shard_map/ppermute | solution.py:43
  12.3 11.8 %collective-permute-start = (bf16[256,1280]{1,0:T(8,128)(2,1)S(1)}, bf16[256,1280]{1,0:T(8,128)(2,1)S(1)}, u32[]{:S(2)}, u32[]{:S(2)}) collective-permute-start(bf16[256,1280]{1,0:T(8,128)(2,1)S(1)} %get-tuple-element.67.own_ref), channel_id=1, source_target_pairs={{96,36},{97,37},{98,38},{99,39},{100,32},{101,33},{102,34},{103,35... | collective-permute-start | bytes 1966088 | tf_op jit(solution)/shard_map/ppermute | solution.py:43
  13.0 23.0 %all-to-all-start = ((bf16[32,8,1280]{2,1,0:T(8,128)(2,1)}), bf16[32,8,1280]{2,1,0:T(8,128)(2,1)S(1)}, u32[]{:S(2)}, u32[]{:S(2)}) async-start(bf16[32,8,1280]{2,1,0:T(8,128)(2,1)} %bitcast.9), calls=%async_computation | async-start | bytes 1310720 | tf_op jit(solution)/shard_map/all_to_all | solution.py:695
  22.3 20.6 %collective-permute-start.5 = (bf16[256,2560]{1,0:T(8,128)(2,1)}, bf16[256,2560]{1,0:T(8,128)(2,1)}, u32[]{:S(2)}, u32[]{:S(2)}) collective-permute-start(bf16[256,2560]{1,0:T(8,128)(2,1)} %get-tuple-element.81), channel_id=1, source_target_pairs={{96,36},{97,37},{98,38},{99,39},{100,32},{101,33},{102,34},{103,35... | collective-permute-start | bytes 3932168 | tf_op jit(solution)/shard_map/ppermute | solution.py:43
  24.6 3.1 %collective-permute-start.1 = (bf16[256,1280]{1,0:T(8,128)(2,1)S(1)}, bf16[256,1280]{1,0:T(8,128)(2,1)S(1)}, u32[]{:S(2)}, u32[]{:S(2)}) collective-permute-start(bf16[256,1280]{1,0:T(8,128)(2,1)S(1)} %shard_map.94.shared_ref), channel_id=1, source_target_pairs={{0,32},{1,33},{2,34},{3,35},{4,36},{5,37},{6,38},{7,39},{8,40},{9,... | collective-permute-start | bytes 1966088 | tf_op jit(solution)/shard_map/ppermute | solution.py:43
  31.5 0.7 copy-start
  35.9 4.2 %copy-start.1 = (bf16[256,640]{1,0:T(8,128)(2,1)S(1)}, bf16[256,640]{1,0:T(8,128)(2,1)}, u32[]{:S(2)}) copy-start(bf16[256,640]{1,0:T(8,128)(2,1)} %copy-done) | copy-start | bytes 983044
  39.9 2.3 %collective-permute-start.3 = (bf16[128,1280]{1,0:T(8,128)(2,1)S(1)}, bf16[128,1280]{1,0:T(8,128)(2,1)S(1)}, u32[]{:S(2)}, u32[]{:S(2)}) collective-permute-start(bf16[128,1280]{1,0:T(8,128)(2,1)S(1)} %get-tuple-element.72), channel_id=1, source_target_pairs={{0,32},{1,33},{2,34},{3,35},{4,36},{5,37},{6,38},{7,39},{8,40},{9,... | collective-permute-start | bytes 983048 | tf_op jit(solution)/shard_map/ppermute | solution.py:43
  42.9 4.5 %collective-permute-start.6 = (bf16[256,2560]{1,0:T(8,128)(2,1)}, bf16[256,2560]{1,0:T(8,128)(2,1)S(1)}, u32[]{:S(2)}, u32[]{:S(2)}) collective-permute-start(bf16[256,2560]{1,0:T(8,128)(2,1)} %collective-permute-done.5.crossed_hbm), channel_id=1, source_target_pairs={{0,32},{1,33},{2,34},{3,35},{4,36},{5,37},{6,38},{7,39},{8,40},{9,... | collective-permute-start | bytes 3932168 | tf_op jit(solution)/shard_map/ppermute | solution.py:43
  43.4 22.3 %collective-permute-start.9 = (bf16[2,8,40,1280]{3,2,1,0:T(8,128)(2,1)S(1)}, bf16[2,8,40,1280]{3,2,1,0:T(8,128)(2,1)S(1)}, u32[]{:S(2)}, u32[]{:S(2)}) collective-permute-start(bf16[2,8,40,1280]{3,2,1,0:T(8,128)(2,1)S(1)} %get-tuple-element.94), channel_id=1, source_target_pairs={{0,3},{1,2},{2,1},{3,0},{4,7},{5,6},{6,5},{7,4},{8,11},{9,10},{10,... | collective-permute-start | bytes 4915208 | tf_op jit(solution)/shard_map/ppermute | solution.py:43
  45.7 10.6 %collective-permute-start.4 = (bf16[128,1280]{1,0:T(8,128)(2,1)S(1)}, bf16[128,1280]{1,0:T(8,128)(2,1)S(1)}, u32[]{:S(2)}, u32[]{:S(2)}) collective-permute-start(bf16[128,1280]{1,0:T(8,128)(2,1)S(1)} %get-tuple-element.79), channel_id=1, source_target_pairs={{0,68},{1,69},{2,70},{3,71},{4,64},{5,65},{6,66},{7,67},{8,76},{9,... | collective-permute-start | bytes 983048 | tf_op jit(solution)/shard_map/ppermute | solution.py:43
  47.3 1.0 copy-start.2
  56.9 1.7 %collective-permute-start.7 = (bf16[128,1280]{1,0:T(8,128)(2,1)S(1)}, bf16[128,1280]{1,0:T(8,128)(2,1)S(1)}, u32[]{:S(2)}, u32[]{:S(2)}) collective-permute-start(bf16[128,1280]{1,0:T(8,128)(2,1)S(1)} %shard_map.100.mine_ref), channel_id=1, source_target_pairs={{0,32},{1,33},{2,34},{3,35},{4,36},{5,37},{6,38},{7,39},{8,40},{9,... | collective-permute-start | bytes 983048 | tf_op jit(solution)/shard_map/ppermute | solution.py:43
  60.6 12.4 %collective-permute-start.8 = (bf16[2,8,40,640]{3,2,1,0:T(8,128)(2,1)S(1)}, bf16[2,8,40,640]{3,2,1,0:T(8,128)(2,1)S(1)}, u32[]{:S(2)}, u32[]{:S(2)}) collective-permute-start(bf16[2,8,40,640]{3,2,1,0:T(8,128)(2,1)S(1)} %get-tuple-element.92), channel_id=1, source_target_pairs={{0,1},{1,0},{2,3},{3,2},{4,5},{5,4},{6,7},{7,6},{8,9},{9,8},{10,11... | collective-permute-start | bytes 2457608 | tf_op jit(solution)/shard_map/ppermute | solution.py:43
  62.2 13.6 %collective-permute-start.10 = (bf16[2,8,40,640]{3,2,1,0:T(8,128)(2,1)S(1)}, bf16[2,8,40,640]{3,2,1,0:T(8,128)(2,1)S(1)}, u32[]{:S(2)}, u32[]{:S(2)}) collective-permute-start(bf16[2,8,40,640]{3,2,1,0:T(8,128)(2,1)S(1)} %get-tuple-element.96), channel_id=1, source_target_pairs={{0,3},{1,2},{2,1},{3,0},{4,7},{5,6},{6,5},{7,4},{8,11},{9,10},{10,... | collective-permute-start | bytes 2457608 | tf_op jit(solution)/shard_map/ppermute | solution.py:43
  66.5 21.6 %collective-permute-start.13 = (bf16[8,40,1280]{2,1,0:T(8,128)(2,1)S(1)}, bf16[8,40,1280]{2,1,0:T(8,128)(2,1)S(1)}, u32[]{:S(2)}, u32[]{:S(2)}) collective-permute-start(bf16[8,40,1280]{2,1,0:T(8,128)(2,1)S(1)} %shard_map.104), channel_id=1, source_target_pairs={{0,1},{1,0},{2,3},{3,2},{4,5},{5,4},{6,7},{7,6},{8,9},{9,8},{10,11... | collective-permute-start | bytes 2457608 | tf_op jit(solution)/shard_map/ppermute | solution.py:43
  76.5 9.2 %collective-permute-start.11 = (bf16[8,40,640]{2,1,0:T(8,128)(2,1)S(1)}, bf16[8,40,640]{2,1,0:T(8,128)(2,1)S(1)}, u32[]{:S(2)}, u32[]{:S(2)}) collective-permute-start(bf16[8,40,640]{2,1,0:T(8,128)(2,1)S(1)} %get-tuple-element.97), channel_id=1, source_target_pairs={{0,3},{1,2},{2,1},{3,0},{4,7},{5,6},{6,5},{7,4},{8,11},{9,10},{10,... | collective-permute-start | bytes 1228808 | tf_op jit(solution)/shard_map/ppermute | solution.py:43
  77.6 8.7 %collective-permute-start.12 = (bf16[8,40,640]{2,1,0:T(8,128)(2,1)S(1)}, bf16[8,40,640]{2,1,0:T(8,128)(2,1)S(1)}, u32[]{:S(2)}, u32[]{:S(2)}) collective-permute-start(bf16[8,40,640]{2,1,0:T(8,128)(2,1)S(1)} %get-tuple-element.98), channel_id=1, source_target_pairs={{0,1},{1,0},{2,3},{3,2},{4,5},{5,4},{6,7},{7,6},{8,9},{9,8},{10,11... | collective-permute-start | bytes 1228808 | tf_op jit(solution)/shard_map/ppermute | solution.py:43
  87.3 8.0 %collective-permute-start.14 = (bf16[2,2,40,1280]{3,2,1,0:T(8,128)(2,1)S(1)}, bf16[2,2,40,1280]{3,2,1,0:T(8,128)(2,1)S(1)}, u32[]{:S(2)}, u32[]{:S(2)}) collective-permute-start(bf16[2,2,40,1280]{3,2,1,0:T(8,128)(2,1)S(1)} %get-tuple-element.103), channel_id=1, source_target_pairs={{0,8},{1,9},{2,10},{3,11},{4,12},{5,13},{6,14},{7,15},{8,0},{9,1},... | collective-permute-start | bytes 1228808 | tf_op jit(solution)/shard_map/ppermute | solution.py:43
  89.3 9.2 %collective-permute-start.16 = (bf16[2,2,40,1280]{3,2,1,0:T(8,128)(2,1)S(1)}, bf16[2,2,40,1280]{3,2,1,0:T(8,128)(2,1)S(1)}, u32[]{:S(2)}, u32[]{:S(2)}) collective-permute-start(bf16[2,2,40,1280]{3,2,1,0:T(8,128)(2,1)S(1)} %get-tuple-element.107), channel_id=1, source_target_pairs={{0,24},{1,25},{2,26},{3,27},{4,28},{5,29},{6,30},{7,31},{8,16},{9,... | collective-permute-start | bytes 1228808 | tf_op jit(solution)/shard_map/ppermute | solution.py:43
  95.9 7.0 %collective-permute-start.15 = (bf16[2,40,1280]{2,1,0:T(8,128)(2,1)S(1)}, bf16[2,40,1280]{2,1,0:T(8,128)(2,1)S(1)}, u32[]{:S(2)}, u32[]{:S(2)}) collective-permute-start(bf16[2,40,1280]{2,1,0:T(8,128)(2,1)S(1)} %shard_map.105), channel_id=1, source_target_pairs={{0,24},{1,25},{2,26},{3,27},{4,28},{5,29},{6,30},{7,31},{8,16},{9,... | collective-permute-start | bytes 614408 | tf_op jit(solution)/shard_map/ppermute | solution.py:43
  99.1 8.7 %collective-permute-start.17 = (bf16[2,40,1280]{2,1,0:T(8,128)(2,1)S(1)}, bf16[2,40,1280]{2,1,0:T(8,128)(2,1)S(1)}, u32[]{:S(2)}, u32[]{:S(2)}) collective-permute-start(bf16[2,40,1280]{2,1,0:T(8,128)(2,1)S(1)} %shard_map.108), channel_id=1, source_target_pairs={{0,8},{1,9},{2,10},{3,11},{4,12},{5,13},{6,14},{7,15},{8,0},{9,1},... | collective-permute-start | bytes 614408 | tf_op jit(solution)/shard_map/ppermute | solution.py:43
  103.6 5.5 %collective-permute-start.18 = (bf16[40,1280]{1,0:T(8,128)(2,1)S(1)}, bf16[40,1280]{1,0:T(8,128)(2,1)S(1)}, u32[]{:S(2)}, u32[]{:S(2)}) collective-permute-start(bf16[40,1280]{1,0:T(8,128)(2,1)S(1)} %get-tuple-element.110), channel_id=1, source_target_pairs={{0,4},{1,5},{2,6},{3,7},{4,0},{5,1},{6,2},{7,3},{8,12},{9,13},{10,... | collective-permute-start | bytes 307208 | tf_op jit(solution)/shard_map/ppermute | solution.py:43
  103.7 6.0 %collective-permute-start.19 = (bf16[40,1280]{1,0:T(8,128)(2,1)S(1)}, bf16[40,1280]{1,0:T(8,128)(2,1)S(1)}, u32[]{:S(2)}, u32[]{:S(2)}) collective-permute-start(bf16[40,1280]{1,0:T(8,128)(2,1)S(1)} %get-tuple-element.114), channel_id=1, source_target_pairs={{0,68},{1,69},{2,70},{3,71},{4,64},{5,65},{6,66},{7,67},{8,76},{9,... | collective-permute-start | bytes 307208 | tf_op jit(solution)/shard_map/ppermute | solution.py:43
  106.3 6.2 %collective-permute-start.20 = (bf16[40,1280]{1,0:T(8,128)(2,1)S(1)}, bf16[40,1280]{1,0:T(8,128)(2,1)S(1)}, u32[]{:S(2)}, u32[]{:S(2)}) collective-permute-start(bf16[40,1280]{1,0:T(8,128)(2,1)S(1)} %get-tuple-element.115), channel_id=1, source_target_pairs={{0,64},{1,65},{2,66},{3,67},{4,68},{5,69},{6,70},{7,71},{8,72},{9,... | collective-permute-start | bytes 307208 | tf_op jit(solution)/shard_map/ppermute | solution.py:43
  108.4 4.7 %collective-permute-start.21 = (bf16[40,1280]{1,0:T(8,128)(2,1)S(1)}, bf16[40,1280]{1,0:T(8,128)(2,1)S(1)}, u32[]{:S(2)}, u32[]{:S(2)}) collective-permute-start(bf16[40,1280]{1,0:T(8,128)(2,1)S(1)} %get-tuple-element.117), channel_id=1, source_target_pairs={{0,4},{1,5},{2,6},{3,7},{4,0},{5,1},{6,2},{7,3},{8,12},{9,13},{10,... | collective-permute-start | bytes 307208 | tf_op jit(solution)/shard_map/ppermute | solution.py:43
  113.2 1.5 %collective-permute-start.22 = (bf16[2,40,1280]{2,1,0:T(8,128)(2,1)S(1)}, bf16[2,40,1280]{2,1,0:T(8,128)(2,1)S(1)}, u32[]{:S(2)}, u32[]{:S(2)}) collective-permute-start(bf16[2,40,1280]{2,1,0:T(8,128)(2,1)S(1)} %get-tuple-element.118), channel_id=1, source_target_pairs={{0,32},{1,33},{2,34},{3,35},{4,36},{5,37},{6,38},{7,39},{8,40},{9,... | collective-permute-start | bytes 614408 | tf_op jit(solution)/shard_map/ppermute | solution.py:43

commit v6 on v4

--- a/solution.py
+++ b/solution.py
@@ -271,25 +271,16 @@
         out_shape=list(outputs),
         in_specs=[smem()] + vmem(len(inputs)) + [pl.BlockSpec(memory_space=pl.ANY)] * 2,
         out_specs=vmem(len(outputs)),
-        scratch_shapes=[
-            pltpu.VMEM(adapt_in.shape[1:], BF16),
-            pltpu.VMEM(adapt_out.shape[1:], BF16),
-            pltpu.SemaphoreType.DMA((2,)),
-        ],
+        scratch_shapes=[pltpu.SemaphoreType.DMA((2,))],
         compiler_params=pltpu.CompilerParams(vmem_limit_bytes=24 * MIB),
         cost_estimate=cost(1024, 1024),
     )(scalars, *inputs, *in_hbm(adapt_in, adapt_out))
 
 
 def adapt_backward_kernel(
-    scale, at, sorter_ref, arrived_ref, mixed_ref, first_hbm, second_hbm,
-    grad_pred_ref, grad_zeta_ref, kept_ref, given_ref, first_ref, second_ref, sems,
+    scale, at, sorter_ref, arrived_ref, mixed_ref, first_ref, second_ref,
+    grad_pred_ref, grad_zeta_ref, kept_ref, given_ref,
 ):
-    first_copy, second_copy = weight_copies(
-        at, first_hbm, second_hbm, first_ref, second_ref, sems
-    )
-    second_copy.start()
-    first_copy.start()
     target = jnp.dot(sorter_ref[...], arrived_ref[...], preferred_element_type=F32)
     pred = mixed_ref[:, :1280]
     inner = jnp.mean(pred * target, axis=-1, keepdims=True)
@@ -299,11 +290,9 @@
     grad_pred = scale * (2.0 * (pred - target) - turn * (target - (inner / first) * pred))
     grad_pred = grad_pred.astype(BF16)
     grad_pred_ref[...] = grad_pred
-    second_copy.wait()
     grad_gamma = contract_cols(grad_pred, second_ref[...])
     grad_zeta = (grad_gamma * mixed_ref[:, 1280:]).astype(BF16)
     grad_zeta_ref[...] = grad_zeta
-    first_copy.wait()
     grad = contract_cols(grad_zeta, first_ref[...])
     grad = jnp.where(at[GROUP_AT] < 3, grad, 0.0)
 
@@ -697,7 +686,7 @@
         pick_kernel, scalars, (output, crossed), [shaped((token_count, width), BF16)]
     )
     features = send(shared, swap_core)
-    student, gamma, mixed = adapt_call(
+    student, gamma, mixed, first, second = adapt_call(
         adapt_forward_kernel,
         scalars,
         (shared, features),
@@ -707,15 +696,15 @@
             shaped((token_count, width), BF16),
             shaped((token_count, 640), BF16),
             shaped((token_count, width + 640), F32),
+            shaped(adapt_in.shape[1:], BF16),
+            shaped(adapt_out.shape[1:], BF16),
         ],
     )
     mixed, handed = lax.optimization_barrier((mixed, handed))
-    grad_pred, grad_zeta, kept, given = adapt_call(
+    grad_pred, grad_zeta, kept, given = call(
         functools.partial(adapt_backward_kernel, loss_scale),
         scalars,
-        (sorter, arrived, mixed),
-        adapt_in,
-        adapt_out,
+        (sorter, arrived, mixed, first, second),
         [
             shaped((token_count, width), BF16),
             shaped((token_count, 640), BF16),

time: 117 us -> 120 us (1.026)
  local copies, waits for them, and re-layouts: 1.87 us -> 7.12 us
  waiting for transfers between devices: 46 us -> 42.3 us
  starting transfers between devices: 30.7 us -> 33.5 us
  Pallas kernels: 36 us -> 34.6 us
    unnamed x8 -> x16, local copies, waits for them, and re-layouts: 1.77 us -> 7.02 us
    pallas_call x2 -> x1, Pallas kernels: 7.69 us -> 3.75 us  [adapt_call(): pl.pallas_call(kernel, out_shape=list(outputs), in_specs=[smem()] + vmem(...]
    ppermute x23, starting transfers between devices: 21.4 us -> 24.2 us  [send(): return lax.ppermute(value, ALL, route(move))]
    pallas_call x16 -> x17, Pallas kernels: 15.3 us -> 17.9 us  [call(): pl.pallas_call(kernel, out_shape=list(outputs), in_specs=[smem()] + vmem(...]
    all_to_all x1, waiting for transfers between devices: 3.74 us -> 1.36 us  [body(): lax.all_to_all(outgoing, WIDE, split_axis=0, concat_axis=0, tiled=True)]
    ppermute x23, waiting for transfers between devices: 42.3 us -> 40.9 us  [send(): return lax.ppermute(value, ALL, route(move))]
  transfers between devices with their start and end apart: 24 -> 24, of which waited for: 17 -> 14; matrix products, arithmetic and copies ran while one was open for 0% -> 0% of each run, Pallas kernels for 20% -> 19%
where the time goes in v6:
time: 120 us; the launch traced here: 119 us
  waiting for transfers between devices  42.3 us (35%)
  Pallas kernels  34.6 us (29%)
  starting transfers between devices  33.5 us (28%)
  local copies, waits for them, and re-layouts  7.12 us (6%)
    ppermute x23, waiting for transfers between devices, send(): return lax.ppermute(value, ALL, route(move))  40.9 us
    ppermute x23, starting transfers between devices, send(): return lax.ppermute(value, ALL, route(move))  24.2 us
    pallas_call x17, Pallas kernels, call(): pl.pallas_call(kernel, out_shape=list(outputs), in_specs=[smem()] + vmem(...  17.9 us
    pallas_call x1, Pallas kernels, block_forward(): pl.pallas_call(forward_kernel, out_shape=[pltpu.HBM((tokens, hidden), BF1...  11.1 us
    all_to_all x1, starting transfers between devices, body(): lax.all_to_all(outgoing, WIDE, split_axis=0, concat_axis=0, tiled=True)  9.27 us
    unnamed x16, local copies, waits for them, and re-layouts  7.02 us
    pallas_call x1, Pallas kernels, adapt_call(): pl.pallas_call(kernel, out_shape=list(outputs), in_specs=[smem()] + vmem(...  3.75 us
  transfers between devices with their start and end apart: 24, of which 14 were waited for; matrix products, arithmetic and copies ran while one was open for 0% of the time, Pallas kernels for 19%

profile of v6, /device:TPU:0, one launch (start us, length us, event | category | flops | bytes accessed | tf_op | source)
XLA Modules:
  0.0 118.7 jit_solution(6973732357755935900)
XLA Ops:
  0.7 11.1 %shard_map.93 = (bf16[256,2560]{1,0:T(8,128)(2,1)}, bf16[1792,1280]{1,0:T(8,128)(2,1)}, bf16[256,1280]{1,0:T(8,128)(2,1)}, bf16[256,1280]{1,0:T(8,128)(2,1)S(1)}, bf16[256,1280]{1,0:T(8,128)(2,1)}) custom-call(s32[7]{0:T(128)S(1)} %stack.31.at, bf16[1,256,1280]{2,1,0:T(8,128)(2,1)} %acts_hbm.1, bf16[1,1280,2560]{2,1,0:T(8,128)(2,1)} %first_hbm.2, ...), custom_call_target="tpu_custom_call" | custom-call | flops 3355443200 | bytes 16777216 | tf_op jit(solution)/shard_map/pallas_call | solution.py:199
  12.6 9.3 %all-to-all-start = ((bf16[32,8,1280]{2,1,0:T(8,128)(2,1)}), bf16[32,8,1280]{2,1,0:T(8,128)(2,1)S(1)}, u32[]{:S(2)}, u32[]{:S(2)}) async-start(bf16[32,8,1280]{2,1,0:T(8,128)(2,1)} %bitcast.9), calls=%async_computation | async-start | bytes 1310720 | tf_op jit(solution)/shard_map/all_to_all | solution.py:684
  21.9 1.7 %collective-permute-start.5 = (bf16[256,2560]{1,0:T(8,128)(2,1)}, bf16[256,2560]{1,0:T(8,128)(2,1)}, u32[]{:S(2)}, u32[]{:S(2)}) collective-permute-start(bf16[256,2560]{1,0:T(8,128)(2,1)} %get-tuple-element.85), channel_id=1, source_target_pairs={{96,36},{97,37},{98,38},{99,39},{100,32},{101,33},{102,34},{103,35... | collective-permute-start | bytes 3932168 | tf_op jit(solution)/shard_map/ppermute | solution.py:43
  24.3 1.4 %collective-permute-start.1 = (bf16[256,1280]{1,0:T(8,128)(2,1)S(1)}, bf16[256,1280]{1,0:T(8,128)(2,1)S(1)}, u32[]{:S(2)}, u32[]{:S(2)}) collective-permute-start(bf16[256,1280]{1,0:T(8,128)(2,1)S(1)} %shard_map.94.shared_ref), channel_id=1, source_target_pairs={{0,32},{1,33},{2,34},{3,35},{4,36},{5,37},{6,38},{7,39},{8,40},{9,... | collective-permute-start | bytes 1966088 | tf_op jit(solution)/shard_map/ppermute | solution.py:43
  25.9 1.5 %collective-permute-done.1.handed_ref = bf16[256,1280]{1,0:T(8,128)(2,1)S(1)} collective-permute-done((bf16[256,1280]{1,0:T(8,128)(2,1)S(1)}, bf16[256,1280]{1,0:T(8,128)(2,1)S(1)}, u32[]{:S(2)}, u32[]{:S(2)}) %collective-permute-start.1) | collective-permute-done | bytes 655392 | tf_op jit(solution)/shard_map/ppermute | solution.py:43
  27.4 3.8 %shard_map.95 = (bf16[256,1280]{1,0:T(8,128)(2,1)S(1)}, bf16[256,640]{1,0:T(8,128)(2,1)S(1)}, f32[256,1920]{1,0:T(8,128)S(1)}, bf16[1280,640]{1,0:T(8,128)(2,1)S(1)}, bf16[640,1280]{1,0:T(8,128)(2,1)S(1)}) custom-call(s32[7]{0:T(128)S(1)} %stack.31.at, bf16[256,1280]{1,0:T(8,128)(2,1)S(1)} %shard_map.94.shared_ref, ...), custom_call_target="tpu_custom_call" | custom-call | flops 1024 | bytes 1024 | tf_op jit(solution)/shard_map/pallas_call | solution.py:269
  34.2 1.4 %all-to-all-done = bf16[32,8,1280]{2,1,0:T(8,128)(2,1)S(1)} async-done(((bf16[32,8,1280]{2,1,0:T(8,128)(2,1)}), bf16[32,8,1280]{2,1,0:T(8,128)(2,1)S(1)}, u32[]{:S(2)}, u32[]{:S(2)}) %all-to-all-start) | async-done | bytes 655392 | tf_op jit(solution)/shard_map/all_to_all | solution.py:684
  35.6 1.4 %copy-done.1 = bf16[1280,640]{1,0:T(8,128)(2,1)S(1)} copy-done((bf16[1280,640]{1,0:T(8,128)(2,1)S(1)}, bf16[1280,640]{1,0:T(8,128)(2,1)}, u32[]{:S(2)}) %copy-start.1) | copy-done | bytes 1638424
  37.0 1.4 %copy-done.3 = bf16[640,1280]{1,0:T(8,128)(2,1)S(1)} copy-done((bf16[640,1280]{1,0:T(8,128)(2,1)S(1)}, bf16[640,1280]{1,0:T(8,128)(2,1)}, u32[]{:S(2)}) %copy-start.3) | copy-done | bytes 1638424
  38.5 2.6 %shard_map.96 = (bf16[256,1280]{1,0:T(8,128)(2,1)S(1)}, bf16[256,640]{1,0:T(8,128)(2,1)S(1)}, f32[128,1280]{1,0:T(8,128)S(1)}, bf16[128,1280]{1,0:T(8,128)(2,1)S(1)}) custom-call(s32[7]{0:T(128)S(1)} %stack.31.at, bf16[256,256]{1,0:T(8,128)(2,1)S(1)} %and_convert_fusion.sorter_ref, bf16[256,1280]{1,0:T(8,128)(2,1)S(1)} %bitcast.14, ...), custom_call_target="tpu_custom_call" | custom-call | bytes 7995392 | tf_op jit(solution)/shard_map/pallas_call | solution.py:64
  41.1 2.0 %shard_map.97 = (bf16[2,8,40,1280]{3,2,1,0:T(8,128)(2,1)S(1)}, bf16[2,8,40,1280]{3,2,1,0:T(8,128)(2,1)S(1)}) custom-call(s32[7]{0:T(128)S(1)} %stack.31.at, bf16[256,1280]{1,0:T(8,128)(2,1)S(1)} %get-tuple-element.77.student_ref, bf16[256,640]{1,0:T(8,128)(2,1)S(1)} %get-tuple-element.78.grad_zeta_ref, bf16[256,640]{1,0:T(8,128)(2,1)S(1)} %copy-done.5, ...), custom_call_target="tpu_custom_call" | custom-call | flops 838860800 | bytes 5242880 | tf_op jit(solution)/shard_map/pallas_call | solution.py:64
  44.4 1.5 %collective-permute-start.9 = (bf16[2,8,40,1280]{3,2,1,0:T(8,128)(2,1)S(1)}, bf16[2,8,40,1280]{3,2,1,0:T(8,128)(2,1)S(1)}, u32[]{:S(2)}, u32[]{:S(2)}) collective-permute-start(bf16[2,8,40,1280]{3,2,1,0:T(8,128)(2,1)S(1)} %get-tuple-element.98), channel_id=1, source_target_pairs={{0,3},{1,2},{2,1},{3,0},{4,7},{5,6},{6,5},{7,4},{8,11},{9,10},{10,... | collective-permute-start | bytes 4915208 | tf_op jit(solution)/shard_map/ppermute | solution.py:43
  45.9 3.6 %collective-permute-start.4 = (bf16[128,1280]{1,0:T(8,128)(2,1)S(1)}, bf16[128,1280]{1,0:T(8,128)(2,1)S(1)}, u32[]{:S(2)}, u32[]{:S(2)}) collective-permute-start(bf16[128,1280]{1,0:T(8,128)(2,1)S(1)} %get-tuple-element.83), channel_id=1, source_target_pairs={{0,68},{1,69},{2,70},{3,71},{4,64},{5,65},{6,66},{7,67},{8,76},{9,... | collective-permute-start | bytes 983048 | tf_op jit(solution)/shard_map/ppermute | solution.py:43
  50.6 1.9 %shard_map.99 = (bf16[256,2560]{1,0:T(8,128)(2,1)S(1)}, bf16[256,1280]{1,0:T(8,128)(2,1)S(1)}, bf16[1280,1280]{1,0:T(8,128)(2,1)S(1)}) custom-call(s32[7]{0:T(128)S(1)} %stack.31.at, bf16[256,2560]{1,0:T(8,128)(2,1)} %collective-permute-done.5.crossed_hbm, bf16[256,2560]{1,0:T(8,128)(2,1)} %copy-done.6, bf16[1792,1280]{1,0:T(8,128)(2,1)} %get-tuple-element.71.hand_hbm, ...), custom_call_target="tpu_custom_call" | custom-call | bytes 8388608 | tf_op jit(solution)/shard_map/pallas_call | solution.py:387
  52.4 5.3 %collective-permute-done.4.across_ref = bf16[128,1280]{1,0:T(8,128)(2,1)S(1)} collective-permute-done((bf16[128,1280]{1,0:T(8,128)(2,1)S(1)}, bf16[128,1280]{1,0:T(8,128)(2,1)S(1)}, u32[]{:S(2)}, u32[]{:S(2)}) %collective-permute-start.4) | collective-permute-done | bytes 327712 | tf_op jit(solution)/shard_map/ppermute | solution.py:43
  58.9 1.3 %collective-permute-done.7.other_ref = bf16[128,1280]{1,0:T(8,128)(2,1)S(1)} collective-permute-done((bf16[128,1280]{1,0:T(8,128)(2,1)S(1)}, bf16[128,1280]{1,0:T(8,128)(2,1)S(1)}, u32[]{:S(2)}, u32[]{:S(2)}) %collective-permute-start.7) | collective-permute-done | bytes 327712 | tf_op jit(solution)/shard_map/ppermute | solution.py:43
  60.1 2.1 %shard_map.101 = (bf16[2,8,40,640]{3,2,1,0:T(8,128)(2,1)S(1)}, bf16[2,8,40,640]{3,2,1,0:T(8,128)(2,1)S(1)}, bf16[2,8,40,640]{3,2,1,0:T(8,128)(2,1)S(1)}, bf16[2,8,40,640]{3,2,1,0:T(8,128)(2,1)S(1)}) custom-call(s32[7]{0:T(128)S(1)} %stack.31.at, bf16[256,2560]{1,0:T(8,128)(2,1)S(1)} %get-tuple-element.90.left, ...), custom_call_target="tpu_custom_call" | custom-call | flops 1677721600 | bytes 9175040 | tf_op jit(solution)/shard_map/pallas_call | solution.py:64
  62.5 1.3 %collective-permute-start.10 = (bf16[2,8,40,640]{3,2,1,0:T(8,128)(2,1)S(1)}, bf16[2,8,40,640]{3,2,1,0:T(8,128)(2,1)S(1)}, u32[]{:S(2)}, u32[]{:S(2)}) collective-permute-start(bf16[2,8,40,640]{3,2,1,0:T(8,128)(2,1)S(1)} %get-tuple-element.100), channel_id=1, source_target_pairs={{0,3},{1,2},{2,1},{3,0},{4,7},{5,6},{6,5},{7,4},{8,11},{9,10},{10,... | collective-permute-start | bytes 2457608 | tf_op jit(solution)/shard_map/ppermute | solution.py:43
  63.8 2.9 %collective-permute-done.9.came_ref = bf16[2,8,40,1280]{3,2,1,0:T(8,128)(2,1)S(1)} collective-permute-done((bf16[2,8,40,1280]{3,2,1,0:T(8,128)(2,1)S(1)}, bf16[2,8,40,1280]{3,2,1,0:T(8,128)(2,1)S(1)}, u32[]{:S(2)}, u32[]{:S(2)}) %collective-permute-start.9) | collective-permute-done | bytes 1638432 | tf_op jit(solution)/shard_map/ppermute | solution.py:43
  67.6 7.0 %collective-permute-done.8.came_a = bf16[2,8,40,640]{3,2,1,0:T(8,128)(2,1)S(1)} collective-permute-done((bf16[2,8,40,640]{3,2,1,0:T(8,128)(2,1)S(1)}, bf16[2,8,40,640]{3,2,1,0:T(8,128)(2,1)S(1)}, u32[]{:S(2)}, u32[]{:S(2)}) %collective-permute-start.8) | collective-permute-done | bytes 819232 | tf_op jit(solution)/shard_map/ppermute | solution.py:43
  74.6 1.4 %collective-permute-done.10.came_b = bf16[2,8,40,640]{3,2,1,0:T(8,128)(2,1)S(1)} collective-permute-done((bf16[2,8,40,640]{3,2,1,0:T(8,128)(2,1)S(1)}, bf16[2,8,40,640]{3,2,1,0:T(8,128)(2,1)S(1)}, u32[]{:S(2)}, u32[]{:S(2)}) %collective-permute-start.10) | collective-permute-done | bytes 819232 | tf_op jit(solution)/shard_map/ppermute | solution.py:43
  76.8 1.4 %collective-permute-start.11 = (bf16[8,40,640]{2,1,0:T(8,128)(2,1)S(1)}, bf16[8,40,640]{2,1,0:T(8,128)(2,1)S(1)}, u32[]{:S(2)}, u32[]{:S(2)}) collective-permute-start(bf16[8,40,640]{2,1,0:T(8,128)(2,1)S(1)} %get-tuple-element.101), channel_id=1, source_target_pairs={{0,3},{1,2},{2,1},{3,0},{4,7},{5,6},{6,5},{7,4},{8,11},{9,10},{10,... | collective-permute-start | bytes 1228808 | tf_op jit(solution)/shard_map/ppermute | solution.py:43
  78.3 7.7 %collective-permute-done.11.last_a = bf16[8,40,640]{2,1,0:T(8,128)(2,1)S(1)} collective-permute-done((bf16[8,40,640]{2,1,0:T(8,128)(2,1)S(1)}, bf16[8,40,640]{2,1,0:T(8,128)(2,1)S(1)}, u32[]{:S(2)}, u32[]{:S(2)}) %collective-permute-start.11) | collective-permute-done | bytes 409632 | tf_op jit(solution)/shard_map/ppermute | solution.py:43
  86.0 1.8 %collective-permute-done.12.last_b = bf16[8,40,640]{2,1,0:T(8,128)(2,1)S(1)} collective-permute-done((bf16[8,40,640]{2,1,0:T(8,128)(2,1)S(1)}, bf16[8,40,640]{2,1,0:T(8,128)(2,1)S(1)}, u32[]{:S(2)}, u32[]{:S(2)}) %collective-permute-start.12) | collective-permute-done | bytes 409632 | tf_op jit(solution)/shard_map/ppermute | solution.py:43
  90.4 2.4 %collective-permute-start.16 = (bf16[2,2,40,1280]{3,2,1,0:T(8,128)(2,1)S(1)}, bf16[2,2,40,1280]{3,2,1,0:T(8,128)(2,1)S(1)}, u32[]{:S(2)}, u32[]{:S(2)}) collective-permute-start(bf16[2,2,40,1280]{3,2,1,0:T(8,128)(2,1)S(1)} %get-tuple-element.111), channel_id=1, source_target_pairs={{0,24},{1,25},{2,26},{3,27},{4,28},{5,29},{6,30},{7,31},{8,16},{9,... | collective-permute-start | bytes 1228808 | tf_op jit(solution)/shard_map/ppermute | solution.py:43
  92.8 4.0 %collective-permute-done.14.came_ref.came = bf16[2,2,40,1280]{3,2,1,0:T(8,128)(2,1)S(1)} collective-permute-done((bf16[2,2,40,1280]{3,2,1,0:T(8,128)(2,1)S(1)}, bf16[2,2,40,1280]{3,2,1,0:T(8,128)(2,1)S(1)}, u32[]{:S(2)}, u32[]{:S(2)}) %collective-permute-start.14) | collective-permute-done | bytes 409632 | tf_op jit(solution)/shard_map/ppermute | solution.py:43
  97.4 2.4 %collective-permute-start.15 = (bf16[2,40,1280]{2,1,0:T(8,128)(2,1)S(1)}, bf16[2,40,1280]{2,1,0:T(8,128)(2,1)S(1)}, u32[]{:S(2)}, u32[]{:S(2)}) collective-permute-start(bf16[2,40,1280]{2,1,0:T(8,128)(2,1)S(1)} %shard_map.105), channel_id=1, source_target_pairs={{0,24},{1,25},{2,26},{3,27},{4,28},{5,29},{6,30},{7,31},{8,16},{9,... | collective-permute-start | bytes 614408 | tf_op jit(solution)/shard_map/ppermute | solution.py:43
  100.8 3.7 %collective-permute-done.15.last = bf16[2,40,1280]{2,1,0:T(8,128)(2,1)S(1)} collective-permute-done((bf16[2,40,1280]{2,1,0:T(8,128)(2,1)S(1)}, bf16[2,40,1280]{2,1,0:T(8,128)(2,1)S(1)}, u32[]{:S(2)}, u32[]{:S(2)}) %collective-permute-start.15) | collective-permute-done | bytes 204832 | tf_op jit(solution)/shard_map/ppermute | solution.py:43
  105.2 3.6 %collective-permute-start.19 = (bf16[40,1280]{1,0:T(8,128)(2,1)S(1)}, bf16[40,1280]{1,0:T(8,128)(2,1)S(1)}, u32[]{:S(2)}, u32[]{:S(2)}) collective-permute-start(bf16[40,1280]{1,0:T(8,128)(2,1)S(1)} %get-tuple-element.118), channel_id=1, source_target_pairs={{0,68},{1,69},{2,70},{3,71},{4,64},{5,65},{6,66},{7,67},{8,76},{9,... | collective-permute-start | bytes 307208 | tf_op jit(solution)/shard_map/ppermute | solution.py:43
  108.9 1.4 %collective-permute-start.20 = (bf16[40,1280]{1,0:T(8,128)(2,1)S(1)}, bf16[40,1280]{1,0:T(8,128)(2,1)S(1)}, u32[]{:S(2)}, u32[]{:S(2)}) collective-permute-start(bf16[40,1280]{1,0:T(8,128)(2,1)S(1)} %get-tuple-element.119), channel_id=1, source_target_pairs={{0,64},{1,65},{2,66},{3,67},{4,68},{5,69},{6,70},{7,71},{8,72},{9,... | collective-permute-start | bytes 307208 | tf_op jit(solution)/shard_map/ppermute | solution.py:43
  112.2 2.9 %collective-permute-done.20.far_ref = bf16[40,1280]{1,0:T(8,128)(2,1)S(1)} collective-permute-done((bf16[40,1280]{1,0:T(8,128)(2,1)S(1)}, bf16[40,1280]{1,0:T(8,128)(2,1)S(1)}, u32[]{:S(2)}, u32[]{:S(2)}) %collective-permute-start.20) | collective-permute-done | bytes 102432 | tf_op jit(solution)/shard_map/ppermute | solution.py:43
  117.2 1.5 %shard_map.112 = (f32[1,40,2560]{2,1,0:T(8,128)}, f32[1,80,1280]{2,1,0:T(8,128)}) custom-call(s32[7]{0:T(128)S(1)} %stack.31.at, f32[2,40,1280]{2,1,0:T(8,128)S(1)} %get-tuple-element.128.high_ref, bf16[2,40,1280]{2,1,0:T(8,128)(2,1)S(1)} %collective-permute-done.22.low_ref), custom_call_target="tpu_custom_call" | custom-call | bytes 1433600 | tf_op jit(solution)/shard_map/pallas_call | solution.py:64
  (59 shorter events, 19.1 us)
Async XLA Ops:
  0.7 22.9 %copy-start.7 = (s32[4,8]{1,0:T(4,128)S(1)}, s32[4,8]{1,0:T(4,128)}, u32[]{:S(2)}) copy-start(s32[4,8]{1,0:T(4,128)} %param.11) | copy-start | bytes 388
  11.8 22.4 %collective-permute-start.2 = (bf16[1792,1280]{1,0:T(8,128)(2,1)}, bf16[1792,1280]{1,0:T(8,128)(2,1)}, u32[]{:S(2)}, u32[]{:S(2)}) collective-permute-start(bf16[1792,1280]{1,0:T(8,128)(2,1)} %get-tuple-element.71.hand_hbm), channel_id=1, source_target_pairs={{0,32},{1,33},{2,34},{3,35},{4,36},{5,37},{6,38},{7,39},{8,40},{9,... | collective-permute-start | bytes 13762568 | tf_op jit(solution)/shard_map/ppermute | solution.py:43
  11.9 11.7 %collective-permute-start = (bf16[256,1280]{1,0:T(8,128)(2,1)S(1)}, bf16[256,1280]{1,0:T(8,128)(2,1)S(1)}, u32[]{:S(2)}, u32[]{:S(2)}) collective-permute-start(bf16[256,1280]{1,0:T(8,128)(2,1)S(1)} %get-tuple-element.69.own_ref), channel_id=1, source_target_pairs={{96,36},{97,37},{98,38},{99,39},{100,32},{101,33},{102,34},{103,35... | collective-permute-start | bytes 1966088 | tf_op jit(solution)/shard_map/ppermute | solution.py:43
  12.6 23.0 %all-to-all-start = ((bf16[32,8,1280]{2,1,0:T(8,128)(2,1)}), bf16[32,8,1280]{2,1,0:T(8,128)(2,1)S(1)}, u32[]{:S(2)}, u32[]{:S(2)}) async-start(bf16[32,8,1280]{2,1,0:T(8,128)(2,1)} %bitcast.9), calls=%async_computation | async-start | bytes 1310720 | tf_op jit(solution)/shard_map/all_to_all | solution.py:684
  21.9 21.9 %collective-permute-start.5 = (bf16[256,2560]{1,0:T(8,128)(2,1)}, bf16[256,2560]{1,0:T(8,128)(2,1)}, u32[]{:S(2)}, u32[]{:S(2)}) collective-permute-start(bf16[256,2560]{1,0:T(8,128)(2,1)} %get-tuple-element.85), channel_id=1, source_target_pairs={{96,36},{97,37},{98,38},{99,39},{100,32},{101,33},{102,34},{103,35... | collective-permute-start | bytes 3932168 | tf_op jit(solution)/shard_map/ppermute | solution.py:43
  24.3 3.1 %collective-permute-start.1 = (bf16[256,1280]{1,0:T(8,128)(2,1)S(1)}, bf16[256,1280]{1,0:T(8,128)(2,1)S(1)}, u32[]{:S(2)}, u32[]{:S(2)}) collective-permute-start(bf16[256,1280]{1,0:T(8,128)(2,1)S(1)} %shard_map.94.shared_ref), channel_id=1, source_target_pairs={{0,32},{1,33},{2,34},{3,35},{4,36},{5,37},{6,38},{7,39},{8,40},{9,... | collective-permute-start | bytes 1966088 | tf_op jit(solution)/shard_map/ppermute | solution.py:43
  31.1 1.2 copy-start
  32.3 1.2 %copy-start.2 = (bf16[640,1280]{1,0:T(8,128)(2,1)}, bf16[640,1280]{1,0:T(8,128)(2,1)S(1)}, u32[]{:S(2)}) copy-start(bf16[640,1280]{1,0:T(8,128)(2,1)S(1)} %get-tuple-element.74.second_ref) | copy-start | bytes 4915204
  33.5 0.7 copy-start.4
  35.6 1.4 %copy-start.1 = (bf16[1280,640]{1,0:T(8,128)(2,1)S(1)}, bf16[1280,640]{1,0:T(8,128)(2,1)}, u32[]{:S(2)}) copy-start(bf16[1280,640]{1,0:T(8,128)(2,1)} %copy-done) | copy-start | bytes 4915204
  37.0 1.4 %copy-start.3 = (bf16[640,1280]{1,0:T(8,128)(2,1)S(1)}, bf16[640,1280]{1,0:T(8,128)(2,1)}, u32[]{:S(2)}) copy-start(bf16[640,1280]{1,0:T(8,128)(2,1)} %copy-done.2) | copy-start | bytes 4915204
  38.5 2.7 %copy-start.5 = (bf16[256,640]{1,0:T(8,128)(2,1)S(1)}, bf16[256,640]{1,0:T(8,128)(2,1)}, u32[]{:S(2)}) copy-start(bf16[256,640]{1,0:T(8,128)(2,1)} %copy-done.4) | copy-start | bytes 983044
  41.0 2.1 %collective-permute-start.3 = (bf16[128,1280]{1,0:T(8,128)(2,1)S(1)}, bf16[128,1280]{1,0:T(8,128)(2,1)S(1)}, u32[]{:S(2)}, u32[]{:S(2)}) collective-permute-start(bf16[128,1280]{1,0:T(8,128)(2,1)S(1)} %get-tuple-element.76), channel_id=1, source_target_pairs={{0,32},{1,33},{2,34},{3,35},{4,36},{5,37},{6,38},{7,39},{8,40},{9,... | collective-permute-start | bytes 983048 | tf_op jit(solution)/shard_map/ppermute | solution.py:43
  43.8 5.6 %collective-permute-start.6 = (bf16[256,2560]{1,0:T(8,128)(2,1)}, bf16[256,2560]{1,0:T(8,128)(2,1)S(1)}, u32[]{:S(2)}, u32[]{:S(2)}) collective-permute-start(bf16[256,2560]{1,0:T(8,128)(2,1)} %collective-permute-done.5.crossed_hbm), channel_id=1, source_target_pairs={{0,32},{1,33},{2,34},{3,35},{4,36},{5,37},{6,38},{7,39},{8,40},{9,... | collective-permute-start | bytes 3932168 | tf_op jit(solution)/shard_map/ppermute | solution.py:43
  44.4 22.3 %collective-permute-start.9 = (bf16[2,8,40,1280]{3,2,1,0:T(8,128)(2,1)S(1)}, bf16[2,8,40,1280]{3,2,1,0:T(8,128)(2,1)S(1)}, u32[]{:S(2)}, u32[]{:S(2)}) collective-permute-start(bf16[2,8,40,1280]{3,2,1,0:T(8,128)(2,1)S(1)} %get-tuple-element.98), channel_id=1, source_target_pairs={{0,3},{1,2},{2,1},{3,0},{4,7},{5,6},{6,5},{7,4},{8,11},{9,10},{10,... | collective-permute-start | bytes 4915208 | tf_op jit(solution)/shard_map/ppermute | solution.py:43
  45.9 11.8 %collective-permute-start.4 = (bf16[128,1280]{1,0:T(8,128)(2,1)S(1)}, bf16[128,1280]{1,0:T(8,128)(2,1)S(1)}, u32[]{:S(2)}, u32[]{:S(2)}) collective-permute-start(bf16[128,1280]{1,0:T(8,128)(2,1)S(1)} %get-tuple-element.83), channel_id=1, source_target_pairs={{0,68},{1,69},{2,70},{3,71},{4,64},{5,65},{6,66},{7,67},{8,76},{9,... | collective-permute-start | bytes 983048 | tf_op jit(solution)/shard_map/ppermute | solution.py:43
  49.5 1.1 copy-start.6
  58.3 1.8 %collective-permute-start.7 = (bf16[128,1280]{1,0:T(8,128)(2,1)S(1)}, bf16[128,1280]{1,0:T(8,128)(2,1)S(1)}, u32[]{:S(2)}, u32[]{:S(2)}) collective-permute-start(bf16[128,1280]{1,0:T(8,128)(2,1)S(1)} %shard_map.100.mine_ref), channel_id=1, source_target_pairs={{0,32},{1,33},{2,34},{3,35},{4,36},{5,37},{6,38},{7,39},{8,40},{9,... | collective-permute-start | bytes 983048 | tf_op jit(solution)/shard_map/ppermute | solution.py:43
  62.2 12.4 %collective-permute-start.8 = (bf16[2,8,40,640]{3,2,1,0:T(8,128)(2,1)S(1)}, bf16[2,8,40,640]{3,2,1,0:T(8,128)(2,1)S(1)}, u32[]{:S(2)}, u32[]{:S(2)}) collective-permute-start(bf16[2,8,40,640]{3,2,1,0:T(8,128)(2,1)S(1)} %get-tuple-element.96), channel_id=1, source_target_pairs={{0,1},{1,0},{2,3},{3,2},{4,5},{5,4},{6,7},{7,6},{8,9},{9,8},{10,11... | collective-permute-start | bytes 2457608 | tf_op jit(solution)/shard_map/ppermute | solution.py:43
  62.5 13.6 %collective-permute-start.10 = (bf16[2,8,40,640]{3,2,1,0:T(8,128)(2,1)S(1)}, bf16[2,8,40,640]{3,2,1,0:T(8,128)(2,1)S(1)}, u32[]{:S(2)}, u32[]{:S(2)}) collective-permute-start(bf16[2,8,40,640]{3,2,1,0:T(8,128)(2,1)S(1)} %get-tuple-element.100), channel_id=1, source_target_pairs={{0,3},{1,2},{2,1},{3,0},{4,7},{5,6},{6,5},{7,4},{8,11},{9,10},{10,... | collective-permute-start | bytes 2457608 | tf_op jit(solution)/shard_map/ppermute | solution.py:43
  67.5 21.8 %collective-permute-start.13 = (bf16[8,40,1280]{2,1,0:T(8,128)(2,1)S(1)}, bf16[8,40,1280]{2,1,0:T(8,128)(2,1)S(1)}, u32[]{:S(2)}, u32[]{:S(2)}) collective-permute-start(bf16[8,40,1280]{2,1,0:T(8,128)(2,1)S(1)} %shard_map.104), channel_id=1, source_target_pairs={{0,1},{1,0},{2,3},{3,2},{4,5},{5,4},{6,7},{7,6},{8,9},{9,8},{10,11... | collective-permute-start | bytes 2457608 | tf_op jit(solution)/shard_map/ppermute | solution.py:43
  76.8 9.2 %collective-permute-start.11 = (bf16[8,40,640]{2,1,0:T(8,128)(2,1)S(1)}, bf16[8,40,640]{2,1,0:T(8,128)(2,1)S(1)}, u32[]{:S(2)}, u32[]{:S(2)}) collective-permute-start(bf16[8,40,640]{2,1,0:T(8,128)(2,1)S(1)} %get-tuple-element.101), channel_id=1, source_target_pairs={{0,3},{1,2},{2,1},{3,0},{4,7},{5,6},{6,5},{7,4},{8,11},{9,10},{10,... | collective-permute-start | bytes 1228808 | tf_op jit(solution)/shard_map/ppermute | solution.py:43
  78.2 9.6 %collective-permute-start.12 = (bf16[8,40,640]{2,1,0:T(8,128)(2,1)S(1)}, bf16[8,40,640]{2,1,0:T(8,128)(2,1)S(1)}, u32[]{:S(2)}, u32[]{:S(2)}) collective-permute-start(bf16[8,40,640]{2,1,0:T(8,128)(2,1)S(1)} %get-tuple-element.102), channel_id=1, source_target_pairs={{0,1},{1,0},{2,3},{3,2},{4,5},{5,4},{6,7},{7,6},{8,9},{9,8},{10,11... | collective-permute-start | bytes 1228808 | tf_op jit(solution)/shard_map/ppermute | solution.py:43
  88.8 8.0 %collective-permute-start.14 = (bf16[2,2,40,1280]{3,2,1,0:T(8,128)(2,1)S(1)}, bf16[2,2,40,1280]{3,2,1,0:T(8,128)(2,1)S(1)}, u32[]{:S(2)}, u32[]{:S(2)}) collective-permute-start(bf16[2,2,40,1280]{3,2,1,0:T(8,128)(2,1)S(1)} %get-tuple-element.107), channel_id=1, source_target_pairs={{0,8},{1,9},{2,10},{3,11},{4,12},{5,13},{6,14},{7,15},{8,0},{9,1},... | collective-permute-start | bytes 1228808 | tf_op jit(solution)/shard_map/ppermute | solution.py:43
  90.4 9.4 %collective-permute-start.16 = (bf16[2,2,40,1280]{3,2,1,0:T(8,128)(2,1)S(1)}, bf16[2,2,40,1280]{3,2,1,0:T(8,128)(2,1)S(1)}, u32[]{:S(2)}, u32[]{:S(2)}) collective-permute-start(bf16[2,2,40,1280]{3,2,1,0:T(8,128)(2,1)S(1)} %get-tuple-element.111), channel_id=1, source_target_pairs={{0,24},{1,25},{2,26},{3,27},{4,28},{5,29},{6,30},{7,31},{8,16},{9,... | collective-permute-start | bytes 1228808 | tf_op jit(solution)/shard_map/ppermute | solution.py:43
  97.4 7.0 %collective-permute-start.15 = (bf16[2,40,1280]{2,1,0:T(8,128)(2,1)S(1)}, bf16[2,40,1280]{2,1,0:T(8,128)(2,1)S(1)}, u32[]{:S(2)}, u32[]{:S(2)}) collective-permute-start(bf16[2,40,1280]{2,1,0:T(8,128)(2,1)S(1)} %shard_map.105), channel_id=1, source_target_pairs={{0,24},{1,25},{2,26},{3,27},{4,28},{5,29},{6,30},{7,31},{8,16},{9,... | collective-permute-start | bytes 614408 | tf_op jit(solution)/shard_map/ppermute | solution.py:43
  100.4 9.8 %collective-permute-start.17 = (bf16[2,40,1280]{2,1,0:T(8,128)(2,1)S(1)}, bf16[2,40,1280]{2,1,0:T(8,128)(2,1)S(1)}, u32[]{:S(2)}, u32[]{:S(2)}) collective-permute-start(bf16[2,40,1280]{2,1,0:T(8,128)(2,1)S(1)} %shard_map.108), channel_id=1, source_target_pairs={{0,8},{1,9},{2,10},{3,11},{4,12},{5,13},{6,14},{7,15},{8,0},{9,1},... | collective-permute-start | bytes 614408 | tf_op jit(solution)/shard_map/ppermute | solution.py:43
  105.2 5.8 %collective-permute-start.18 = (bf16[40,1280]{1,0:T(8,128)(2,1)S(1)}, bf16[40,1280]{1,0:T(8,128)(2,1)S(1)}, u32[]{:S(2)}, u32[]{:S(2)}) collective-permute-start(bf16[40,1280]{1,0:T(8,128)(2,1)S(1)} %get-tuple-element.114), channel_id=1, source_target_pairs={{0,4},{1,5},{2,6},{3,7},{4,0},{5,1},{6,2},{7,3},{8,12},{9,13},{10,... | collective-permute-start | bytes 307208 | tf_op jit(solution)/shard_map/ppermute | solution.py:43
  105.2 6.9 %collective-permute-start.19 = (bf16[40,1280]{1,0:T(8,128)(2,1)S(1)}, bf16[40,1280]{1,0:T(8,128)(2,1)S(1)}, u32[]{:S(2)}, u32[]{:S(2)}) collective-permute-start(bf16[40,1280]{1,0:T(8,128)(2,1)S(1)} %get-tuple-element.118), channel_id=1, source_target_pairs={{0,68},{1,69},{2,70},{3,71},{4,64},{5,65},{6,66},{7,67},{8,76},{9,... | collective-permute-start | bytes 307208 | tf_op jit(solution)/shard_map/ppermute | solution.py:43
  108.9 6.2 %collective-permute-start.20 = (bf16[40,1280]{1,0:T(8,128)(2,1)S(1)}, bf16[40,1280]{1,0:T(8,128)(2,1)S(1)}, u32[]{:S(2)}, u32[]{:S(2)}) collective-permute-start(bf16[40,1280]{1,0:T(8,128)(2,1)S(1)} %get-tuple-element.119), channel_id=1, source_target_pairs={{0,64},{1,65},{2,66},{3,67},{4,68},{5,69},{6,70},{7,71},{8,72},{9,... | collective-permute-start | bytes 307208 | tf_op jit(solution)/shard_map/ppermute | solution.py:43
  110.9 4.8 %collective-permute-start.21 = (bf16[40,1280]{1,0:T(8,128)(2,1)S(1)}, bf16[40,1280]{1,0:T(8,128)(2,1)S(1)}, u32[]{:S(2)}, u32[]{:S(2)}) collective-permute-start(bf16[40,1280]{1,0:T(8,128)(2,1)S(1)} %get-tuple-element.121), channel_id=1, source_target_pairs={{0,4},{1,5},{2,6},{3,7},{4,0},{5,1},{6,2},{7,3},{8,12},{9,13},{10,... | collective-permute-start | bytes 307208 | tf_op jit(solution)/shard_map/ppermute | solution.py:43
  115.7 1.5 %collective-permute-start.22 = (bf16[2,40,1280]{2,1,0:T(8,128)(2,1)S(1)}, bf16[2,40,1280]{2,1,0:T(8,128)(2,1)S(1)}, u32[]{:S(2)}, u32[]{:S(2)}) collective-permute-start(bf16[2,40,1280]{2,1,0:T(8,128)(2,1)S(1)} %get-tuple-element.122), channel_id=1, source_target_pairs={{0,32},{1,33},{2,34},{3,35},{4,36},{5,37},{6,38},{7,39},{8,40},{9,... | collective-permute-start | bytes 614408 | tf_op jit(solution)/shard_map/ppermute | solution.py:43
